TPU v7x, 32 devices: a whole 2x2x4 slice. The times are simulated.
32 devices in a mesh: dp: 4 (over y, core), shard: 8 (over z, x).
Axes of the slice: x: 2, y: 2, z: 4, core: 2. Of those that a mesh axis runs over, the one named last changes fastest.
Arguments:
- tokens: bfloat16 [32768, 768], P(('dp', 'shard')), may hold values from -6 to 6
- segment_ids: int32 [32768], P(('dp', 'shard')), may hold values from 0 to 127, never falling along the last dimension, each value on 1 to 512 neighbouring positions
- routes: int32 [32768, 2], P(('dp', 'shard')), may hold values from 0 to 3, all different within a row; in each aligned block of 1024 rows (0 to 1023, 1024 to 2047, ...) at most 640 rows name the same one
- buckets: int32 [1024], replicated, may hold values from 0 to 31, never falling along the last dimension, each value on 1 to 128 neighbouring positions
- norm1_gain: bfloat16 [768], P('shard'), may hold values from 0.5 to 1.5
- w_qkv: bfloat16 [768, 2304], P('shard'), may hold values from -0.21875 to 0.21875
- w_attn_out: bfloat16 [768, 768], P('shard'), may hold values from -0.875 to 0.875
- bias_table: bfloat16 [32, 12], P('shard'), may hold values from -4 to 4
- norm2_gain: bfloat16 [768], P('shard'), may hold values from 0.5 to 1.5
- router: bfloat16 [768, 4], P('shard'), may hold values from -0.15625 to 0.15625
- w_in: bfloat16 [4, 768, 3072], P(None, 'shard'), may hold values from -0.21875 to 0.21875
- w_expert_out: bfloat16 [4, 3072, 768], P(None, 'shard'), may hold values from -0.15625 to 0.15625
- cotangent: bfloat16 [32768, 768], P(('dp', 'shard')), may hold values from -6 to 6
Outputs:
- mixed_out: bfloat16 [32768, 768], P(('dp', 'shard'))
- grad_tokens: bfloat16 [32768, 768], P(('dp', 'shard'))
- grad_norm1: float32 [768], P('shard')
- grad_qkv: float32 [768, 2304], P('shard')
- grad_attn_out: float32 [768, 768], P('shard')
- grad_bias_table: float32 [32, 12], P('shard')
- grad_norm2: float32 [768], P('shard')
- grad_router: float32 [768, 4], P('shard')
- grad_w_in: float32 [4, 768, 3072], P(None, 'shard')
- grad_w_expert_out: float32 [4, 3072, 768], P(None, 'shard')
Inputs may be any that keep to these rules, and one draw needn't show every extreme that they name: `routes`: each row names two different experts; among the rows of one device no expert is named more than 640 times, and in every draw some expert is named exactly 640 times by the rows of some device. `segment_ids`: never falling along the tokens; a document holds at most 1024 // 2 tokens. `buckets`: never falling with the distance.
All inputs are finite; a program needn't handle non-finite values.
Results may differ from a plain program's by a relative error of at most 0.023.
Values may be sent and summed in bfloat16 or wider, within the bound.
No kernel may reach another device: no remote copies, remote signals or barrier semaphores. Data moves between devices by JAX's collectives and lax.ppermute only.
A program may use at most 384 MiB of HBM per device.

v0:
```python
import jax
import jax.numpy as jnp
from jax import lax
from jax.sharding import PartitionSpec as P

D = 768
HEADS = 12
HEAD_DIM = 64
EXPERTS = 4
BUCKETS = 32
SEQ = 1024
CAP = 640


NORM_EPSILON = 1e-06
HIGHEST_PRECISION = lax.Precision.HIGHEST


def norm_forward(values, gain_vec):
    inv_rms = lax.rsqrt(jnp.mean(values * values, axis=-1, keepdims=True) + NORM_EPSILON)
    unit_rows = values * inv_rms
    return (unit_rows, inv_rms, unit_rows * gain_vec)


def norm_backward(grad_norm, unit_rows, inv_rms, gain_vec):
    grad_unit = grad_norm * gain_vec
    grad_gain = jnp.sum(grad_norm * unit_rows, axis=0)
    grad_input = inv_rms * (
        grad_unit - unit_rows * jnp.mean(grad_unit * unit_rows, axis=-1, keepdims=True)
    )
    return (grad_input, grad_gain)


def gelu_value(values):
    return jax.nn.gelu(values, approximate=True)


def slot_tables(route_rows):
    row_count = route_rows.shape[0]
    onehot = (route_rows[:, :, None] == jnp.arange(EXPERTS, dtype=jnp.int32)[None, None, :]).astype(
        jnp.int32
    )
    flat_hits = onehot.reshape(2 * row_count, EXPERTS)
    before = jnp.cumsum(flat_hits, axis=0, dtype=jnp.int32) - flat_hits
    slot_index = jnp.sum(before * flat_hits, axis=1, dtype=jnp.int32).reshape(row_count, 2)
    slot_place = route_rows * CAP + slot_index
    flat_place = slot_place.reshape(-1)
    token_ids = jnp.repeat(jnp.arange(row_count, dtype=jnp.int32), 2)
    token_of_slot = jnp.zeros((EXPERTS * CAP,), jnp.int32).at[flat_place].set(token_ids)
    assign_of_slot = (
        jnp.zeros((EXPERTS * CAP,), jnp.int32)
        .at[flat_place]
        .set(jnp.arange(2 * row_count, dtype=jnp.int32))
    )
    filled = jnp.zeros((EXPERTS * CAP,), jnp.float32).at[flat_place].set(1.0)
    return (slot_place, token_of_slot, assign_of_slot, filled)


def pair_layout(offset, block_rows, key_count, segments, bucket_ids):
    query_pos = offset + jnp.arange(block_rows, dtype=jnp.int32)
    distance = query_pos[:, None] - jnp.arange(key_count, dtype=jnp.int32)[None, :]
    row_segments = segments[offset : offset + block_rows]
    allowed = (distance >= 0) & (row_segments[:, None] == segments[None, :key_count])
    pair_buckets = jnp.take(bucket_ids, jnp.maximum(distance, 0), axis=0).reshape(-1)
    bucket_mask = (jnp.arange(BUCKETS, dtype=jnp.int32)[:, None] == pair_buckets[None, :]).astype(
        jnp.float32
    )
    return (allowed, bucket_mask)


def block_scores(query_rows, key_rows, allowed, bucket_mask, bias_heads):
    block_rows = query_rows.shape[0]
    key_count = key_rows.shape[0]
    inv_root = HEAD_DIM ** (-0.5)
    bias_rows = jnp.dot(bias_heads, bucket_mask, precision=HIGHEST_PRECISION).reshape(
        HEADS, block_rows, key_count
    )
    raw_scores = (
        jnp.einsum("qhd,khd->hqk", query_rows, key_rows, preferred_element_type=jnp.float32)
        * inv_root
        + bias_rows
    )
    return jnp.where(allowed[None], raw_scores, -1e30)


def attend_forward(split_rows, segments, bias_heads, bucket_ids):
    queries = split_rows[:, 0]
    key_rows = split_rows[:, 1]
    value_rows = split_rows[:, 2]
    block_rows = min(512, SEQ)
    mixed_parts = []
    total_parts = []
    for block in range(SEQ // block_rows):
        offset = block * block_rows
        key_count = offset + block_rows
        allowed, bucket_mask = pair_layout(offset, block_rows, key_count, segments, bucket_ids)
        scores = block_scores(
            queries[offset:key_count], key_rows[:key_count], allowed, bucket_mask, bias_heads
        )
        row_max = jnp.max(scores, axis=-1, keepdims=True)
        weights = jnp.exp(scores - row_max)
        denom_sum = jnp.sum(weights, axis=-1, keepdims=True)
        prob_rows = weights / denom_sum
        mixed_parts.append(
            jnp.einsum(
                "hqk,khd->qhd",
                prob_rows.astype(jnp.bfloat16),
                value_rows[:key_count],
                preferred_element_type=jnp.float32,
            )
        )
        total_parts.append((row_max + jnp.log(denom_sum))[..., 0])
    mixed_heads = jnp.concatenate(mixed_parts, axis=0)
    return (mixed_heads.reshape(SEQ, HEADS * HEAD_DIM), jnp.stack(total_parts, axis=0))


def attend_backward(split_rows, segments, bias_heads, bucket_ids, log_totals, grad_mixed):
    queries = split_rows[:, 0]
    key_rows = split_rows[:, 1]
    value_rows = split_rows[:, 2]
    inv_root = HEAD_DIM ** (-0.5)
    block_rows = min(512, SEQ)
    grad_keys = jnp.zeros((SEQ, HEADS, HEAD_DIM), jnp.float32)
    grad_values = jnp.zeros((SEQ, HEADS, HEAD_DIM), jnp.float32)
    grad_bias = jnp.zeros((HEADS, BUCKETS), jnp.float32)
    query_parts = []
    for block in range(SEQ // block_rows):
        offset = block * block_rows
        key_count = offset + block_rows
        query_rows = queries[offset:key_count]
        grad_rows = grad_mixed[offset:key_count]
        key_part = key_rows[:key_count]
        allowed, bucket_mask = pair_layout(offset, block_rows, key_count, segments, bucket_ids)
        scores = block_scores(query_rows, key_part, allowed, bucket_mask, bias_heads)
        prob_rows = jnp.exp(scores - log_totals[block][..., None])
        grad_probs = jnp.einsum(
            "qhd,khd->hqk", grad_rows, value_rows[:key_count], preferred_element_type=jnp.float32
        )
        inner_sum = jnp.sum(prob_rows * grad_probs, axis=-1, keepdims=True)
        grad_scores = (prob_rows * (grad_probs - inner_sum)).astype(jnp.bfloat16)
        query_parts.append(
            jnp.einsum("hqk,khd->qhd", grad_scores, key_part, preferred_element_type=jnp.float32)
            * inv_root
        )
        grad_keys = grad_keys.at[:key_count].add(
            jnp.einsum("hqk,qhd->khd", grad_scores, query_rows, preferred_element_type=jnp.float32)
            * inv_root
        )
        grad_values = grad_values.at[:key_count].add(
            jnp.einsum(
                "hqk,qhd->khd",
                prob_rows.astype(jnp.bfloat16),
                grad_rows,
                preferred_element_type=jnp.float32,
            )
        )
        grad_bias = grad_bias + jnp.einsum(
            "hp,bp->hb",
            grad_scores.reshape(HEADS, -1),
            bucket_mask.astype(jnp.bfloat16),
            preferred_element_type=jnp.float32,
        )
    grad_queries = jnp.concatenate(query_parts, axis=0)
    grad_split = jnp.stack([grad_queries, grad_keys, grad_values], axis=1).reshape(
        SEQ, 3 * HEADS * HEAD_DIM
    )
    return (grad_split, grad_bias)


def body(
    tokens,
    segment_ids,
    routes,
    buckets,
    norm1_gain,
    w_qkv,
    w_attn_out,
    bias_table,
    norm2_gain,
    router,
    w_in,
    w_expert_out,
    cotangent,
):
    gain_one, qkv_weight, attn_weight, bias_full, gain_two, router_weight = (
        lax.all_gather(norm1_gain, "shard", axis=0, tiled=True),
        lax.all_gather(w_qkv, "shard", axis=0, tiled=True),
        lax.all_gather(w_attn_out, "shard", axis=0, tiled=True),
        lax.all_gather(bias_table, "shard", axis=0, tiled=True),
        lax.all_gather(norm2_gain, "shard", axis=0, tiled=True),
        lax.all_gather(router, "shard", axis=0, tiled=True),
    )
    bias_heads = bias_full.astype(jnp.float32).T
    token_rows = tokens.astype(jnp.float32)
    unit_one, inv_one, normed_one = norm_forward(token_rows, gain_one.astype(jnp.float32))
    act_one = normed_one.astype(jnp.bfloat16)
    qkv_rows = jnp.dot(act_one, qkv_weight, preferred_element_type=jnp.float32).astype(jnp.bfloat16)
    seq_count = token_rows.shape[0] // SEQ
    splits = qkv_rows.reshape(seq_count, SEQ, 3, HEADS, HEAD_DIM)
    seq_segments = segment_ids.reshape(seq_count, SEQ)
    mixed_heads, log_totals = lax.map(
        lambda paired: attend_forward(paired[0], paired[1], bias_heads, buckets),
        (splits, seq_segments),
    )
    attended = mixed_heads.reshape(-1, D).astype(jnp.bfloat16)
    residual = token_rows + jnp.dot(attended, attn_weight, preferred_element_type=jnp.float32)
    unit_two, inv_two, normed_two = norm_forward(residual, gain_two.astype(jnp.float32))
    act_two = normed_two.astype(jnp.bfloat16)
    logits = jnp.dot(act_two, router_weight, preferred_element_type=jnp.float32)
    shifted = jnp.exp(logits - jnp.max(logits, axis=1, keepdims=True))
    prob_all = shifted / jnp.sum(shifted, axis=1, keepdims=True)
    route_hits = (routes[:, :, None] == jnp.arange(EXPERTS, dtype=jnp.int32)[None, None, :]).astype(
        jnp.float32
    )
    chosen = jnp.sum(route_hits * prob_all[:, None, :], axis=2)
    chosen_sum = jnp.sum(chosen, axis=1, keepdims=True)
    gate_vals = chosen / chosen_sum
    slot_place, token_of_slot, assign_of_slot, filled = slot_tables(routes)
    dispatched = act_two[token_of_slot].reshape(EXPERTS, CAP, D)
    expert_outputs = []
    kept_weights = []
    for expert in range(EXPERTS):
        w_in_full, w_out_full = (
            lax.all_gather(w_in[expert], "shard", axis=0, tiled=True),
            lax.all_gather(w_expert_out[expert], "shard", axis=0, tiled=True),
        )
        kept_weights.append((w_in_full, w_out_full))
        hidden = jnp.dot(dispatched[expert], w_in_full, preferred_element_type=jnp.float32)
        activated = gelu_value(hidden).astype(jnp.bfloat16)
        expert_outputs.append(jnp.dot(activated, w_out_full, preferred_element_type=jnp.float32))
    expert_rows = jnp.concatenate(expert_outputs, axis=0)
    picked = expert_rows[slot_place]
    moe_rows = jnp.sum(gate_vals[:, :, None] * picked, axis=1)
    mixed_out = (residual + moe_rows).astype(jnp.bfloat16)
    grad_rows = cotangent.astype(jnp.float32)
    grad_gates = jnp.sum(grad_rows[:, None, :] * picked, axis=2)
    slot_gate = gate_vals.reshape(-1)[assign_of_slot] * filled
    grad_expert = (
        (slot_gate[:, None] * grad_rows[token_of_slot])
        .astype(jnp.bfloat16)
        .reshape(EXPERTS, CAP, D)
    )
    gain_one, qkv_weight, attn_weight, gain_two, router_weight = (
        lax.all_gather(norm1_gain, "shard", axis=0, tiled=True),
        lax.all_gather(w_qkv, "shard", axis=0, tiled=True),
        lax.all_gather(w_attn_out, "shard", axis=0, tiled=True),
        lax.all_gather(norm2_gain, "shard", axis=0, tiled=True),
        lax.all_gather(router, "shard", axis=0, tiled=True),
    )
    grad_dispatch = []
    grad_in_parts = []
    grad_out_parts = []
    for expert in range(EXPERTS):
        w_in_full, w_out_full = (
            lax.all_gather(w_in[expert], "shard", axis=0, tiled=True),
            lax.all_gather(w_expert_out[expert], "shard", axis=0, tiled=True),
        )
        hidden = jnp.dot(dispatched[expert], w_in_full, preferred_element_type=jnp.float32)
        activated_full, gelu_pull = jax.vjp(gelu_value, hidden)
        activated = activated_full.astype(jnp.bfloat16)
        grad_w_out = jnp.einsum(
            "cf,cd->fd", activated, grad_expert[expert], preferred_element_type=jnp.float32
        )
        grad_act = jnp.einsum(
            "cd,fd->cf", grad_expert[expert], w_out_full, preferred_element_type=jnp.float32
        )
        grad_hidden = gelu_pull(grad_act)[0].astype(jnp.bfloat16)
        grad_w_in = jnp.einsum(
            "cd,cf->df", dispatched[expert], grad_hidden, preferred_element_type=jnp.float32
        )
        grad_dispatch.append(
            jnp.einsum("cf,df->cd", grad_hidden, w_in_full, preferred_element_type=jnp.float32)
        )
        shard_in, shard_out = (
            lax.psum_scatter(
                grad_w_in.astype(jnp.bfloat16), "shard", scatter_dimension=0, tiled=True
            ).astype(jnp.float32),
            lax.psum_scatter(
                grad_w_out.astype(jnp.bfloat16), "shard", scatter_dimension=0, tiled=True
            ).astype(jnp.float32),
        )
        grad_in_parts.append(shard_in)
        grad_out_parts.append(shard_out)
    grad_dispatch_rows = jnp.concatenate(grad_dispatch, axis=0)
    grad_act_two = jnp.sum(grad_dispatch_rows[slot_place], axis=1)
    weighted = jnp.sum(grad_gates * gate_vals, axis=1, keepdims=True)
    grad_chosen = (grad_gates - weighted) / chosen_sum
    grad_prob = jnp.sum(grad_chosen[:, :, None] * route_hits, axis=1)
    grad_logits = (
        prob_all * (grad_prob - jnp.sum(prob_all * grad_prob, axis=1, keepdims=True))
    ).astype(jnp.bfloat16)
    grad_router = jnp.einsum("nd,ne->de", act_two, grad_logits, preferred_element_type=jnp.float32)
    grad_act_two = grad_act_two + jnp.einsum(
        "ne,de->nd", grad_logits, router_weight, preferred_element_type=jnp.float32
    )
    grad_norm_two, grad_gain_two = norm_backward(
        grad_act_two, unit_two, inv_two, gain_two.astype(jnp.float32)
    )
    grad_residual = grad_rows + grad_norm_two
    grad_branch = grad_residual.astype(jnp.bfloat16)
    grad_attn_weight = jnp.einsum(
        "nd,ne->de", attended, grad_branch, preferred_element_type=jnp.float32
    )
    grad_attended = jnp.einsum(
        "ne,de->nd", grad_branch, attn_weight, preferred_element_type=jnp.float32
    ).astype(jnp.bfloat16)
    grad_heads = grad_attended.reshape(seq_count, SEQ, HEADS, HEAD_DIM)
    grad_splits, grad_bias = lax.map(
        lambda paired: attend_backward(
            paired[0], paired[1], bias_heads, buckets, paired[2], paired[3]
        ),
        (splits, seq_segments, log_totals, grad_heads),
    )
    grad_qkv_rows = grad_splits.reshape(-1, 3 * D).astype(jnp.bfloat16)
    grad_qkv_weight = jnp.einsum(
        "nd,nf->df", act_one, grad_qkv_rows, preferred_element_type=jnp.float32
    )
    grad_act_one = jnp.einsum(
        "nf,df->nd", grad_qkv_rows, qkv_weight, preferred_element_type=jnp.float32
    )
    grad_norm_one, grad_gain_one = norm_backward(
        grad_act_one, unit_one, inv_one, gain_one.astype(jnp.float32)
    )
    grad_tokens = (grad_residual + grad_norm_one).astype(jnp.bfloat16)
    grad_table = jnp.sum(grad_bias, axis=0).T
    sum_one, sum_qkv, sum_attn, sum_table, sum_two, sum_router = (
        lax.psum_scatter(
            grad_gain_one.astype(jnp.bfloat16), "shard", scatter_dimension=0, tiled=True
        ).astype(jnp.float32),
        lax.psum_scatter(
            grad_qkv_weight.astype(jnp.bfloat16), "shard", scatter_dimension=0, tiled=True
        ).astype(jnp.float32),
        lax.psum_scatter(
            grad_attn_weight.astype(jnp.bfloat16), "shard", scatter_dimension=0, tiled=True
        ).astype(jnp.float32),
        lax.psum_scatter(
            grad_table.astype(jnp.bfloat16), "shard", scatter_dimension=0, tiled=True
        ).astype(jnp.float32),
        lax.psum_scatter(
            grad_gain_two.astype(jnp.bfloat16), "shard", scatter_dimension=0, tiled=True
        ).astype(jnp.float32),
        lax.psum_scatter(
            grad_router.astype(jnp.bfloat16), "shard", scatter_dimension=0, tiled=True
        ).astype(jnp.float32),
    )
    grad_w_in_all = jnp.stack(grad_in_parts, axis=0)
    grad_w_out_all = jnp.stack(grad_out_parts, axis=0)
    sum_one, sum_qkv, sum_attn, sum_table, sum_two, sum_router, grad_w_in_all, grad_w_out_all = (
        lax.psum(
            (
                sum_one,
                sum_qkv,
                sum_attn,
                sum_table,
                sum_two,
                sum_router,
                grad_w_in_all,
                grad_w_out_all,
            ),
            "dp",
        )
    )
    return (
        mixed_out,
        grad_tokens,
        sum_one,
        sum_qkv,
        sum_attn,
        sum_table,
        sum_two,
        sum_router,
        grad_w_in_all,
        grad_w_out_all,
    )


def solution(mesh):
    return jax.shard_map(
        body,
        mesh=mesh,
        in_specs=(
            P(("dp", "shard"), None),
            P(("dp", "shard")),
            P(("dp", "shard"), None),
            P(),
            P("shard"),
            P("shard", None),
            P("shard", None),
            P("shard", None),
            P("shard"),
            P("shard", None),
            P(None, "shard", None),
            P(None, "shard", None),
            P(("dp", "shard"), None),
        ),
        out_specs=(
            P(("dp", "shard"), None),
            P(("dp", "shard"), None),
            P("shard"),
            P("shard", None),
            P("shard", None),
            P("shard", None),
            P("shard"),
            P("shard", None),
            P(None, "shard", None),
            P(None, "shard", None),
        ),
        check_vma=False,
    )
```

profile of v0, /device:TPU:9, one launch (start us, length us, event | category | flops | bytes accessed | tf_op | source)
XLA Modules:
  0.0 6853.6 jit_solution(3197307358673483647)
XLA Ops:
  20.0 15.7 all-reduce.10
  36.9 13.8 all-gather.8
  50.7 15.4 all-gather.9
  92.7 1041.4 %gather_fusion.5 = s32[262144]{0:T(1024)S(1)} fusion(s32[1024]{0:T(1024)S(1)} %copy-done, s32[262144]{0:T(1024)S(1)} %broadcast_clamp_fusion.1), kind=kCustom, calls=%fused_computation.clone | custom fusion | bytes 3145728 | tf_op jit(solution)/shard_map/while/body/eval_jaxpr/jit(_take)/gather | solution.py:64
  1144.0 4249.8 %gather_fusion.6 = s32[524288]{0:T(1024)} fusion(s32[1024]{0:T(1024)S(1)} %copy-done, s32[524288]{0:T(1024)} %broadcast_clamp_fusion), kind=kCustom, calls=%fused_computation.1.clone | custom fusion | bytes 6291456 | tf_op jit(solution)/shard_map/while/body/eval_jaxpr/jit(_take)/gather | solution.py:64
  5409.6 17.8 copy.193
  5427.4 10.7 slice.335
  5438.1 12.7 copy.156
  5450.8 17.3 fusion
  5468.1 31.8 copy.196
  5548.9 16.7 fusion.169
  5565.6 10.9 fusion.6
  5576.5 11.2 fusion.122
  5607.2 13.6 gather_fusion.2
  5712.8 10.6 fusion.30
  5772.4 10.8 fusion.44
  5794.0 14.0 gather_fusion.4
  5861.7 13.9 gather_fusion.1
  5884.1 17.5 multiply_reduce_fusion.2
  5957.1 18.5 multiply_reduce_fusion
  5975.6 18.3 multiply_convert_fusion
  6016.1 11.5 fusion.111
  6048.5 94.4 %reduce-scatter.22.cloned.1.call-done = bf16[96,3072]{1,0:T(8,128)(2,1)} async-done(((bf16[768,3072]{1,0:T(8,128)(2,1)}), bf16[96,3072]{1,0:T(8,128)(2,1)}) %reduce-scatter.22.cloned.1.call-update) | async-done | bytes 589840 | tf_op jit(solution)/shard_map/reduce_scatter | solution.py:275
  6142.9 98.5 %reduce-scatter.20.cloned.1.call-done = bf16[96,3072]{1,0:T(8,128)(2,1)} async-done(((bf16[768,3072]{1,0:T(8,128)(2,1)}), bf16[96,3072]{1,0:T(8,128)(2,1)}) %reduce-scatter.20.cloned.1.call-update) | async-done | bytes 589840 | tf_op jit(solution)/shard_map/reduce_scatter | solution.py:275
  6241.5 98.5 %reduce-scatter.18.cloned.1.call-done = bf16[96,3072]{1,0:T(8,128)(2,1)} async-done(((bf16[768,3072]{1,0:T(8,128)(2,1)}), bf16[96,3072]{1,0:T(8,128)(2,1)}) %reduce-scatter.18.cloned.1.call-update) | async-done | bytes 589840 | tf_op jit(solution)/shard_map/reduce_scatter | solution.py:275
  6340.0 98.7 %reduce-scatter.24.cloned.1.call-done = bf16[96,3072]{1,0:T(8,128)(2,1)} async-done(((bf16[768,3072]{1,0:T(8,128)(2,1)}), bf16[96,3072]{1,0:T(8,128)(2,1)}) %reduce-scatter.24.cloned.1.call-update) | async-done | bytes 589840 | tf_op jit(solution)/shard_map/reduce_scatter | solution.py:275
  6461.7 11.4 copy.198
  6488.8 29.2 copy.199
  6532.4 26.2 all-reduce.9
  6567.7 83.8 %reduce-scatter.14.cloned.1.call-done = bf16[96,2304]{1,0:T(8,128)(2,1)} async-done(((bf16[768,2304]{1,0:T(8,128)(2,1)}), bf16[96,2304]{1,0:T(8,128)(2,1)}) %reduce-scatter.14.cloned.1.call-update) | async-done | bytes 442384 | tf_op jit(solution)/shard_map/reduce_scatter | solution.py:330
  6651.6 44.6 all-reduce.15
  6696.2 142.7 %all-reduce.14.cloned.1.call-done = (f32[4,96,3072]{2,1,0:T(8,128)}, f32[4,384,768]{2,1,0:T(8,128)}) async-done(((f32[4,96,3072]{2,1,0:T(8,128)}, f32[4,384,768]{2,1,0:T(8,128)}), (f32[4,96,3072]{2,1,0:T(8,128)}, f32[4,384,768]{2,1,0:T(8,128)})) %all-reduce.14.cloned.1.call-update) | async-done | bytes 9437200 | tf_op jit(solution)/shard_map/psum | solution.py:349
  (432 shorter events, 513.0 us)
Async XLA Ops:
  7.2 85.5 %copy-start = (s32[1024]{0:T(1024)S(1)}, s32[1024]{0:T(1024)}, u32[]{:S(2)}) copy-start(s32[1024]{0:T(1024)} %param.32) | copy-start | bytes 12292
  7.2 5509.6 %all-gather.21.cloned.1.call-start = ((), (), s32[]{:S(2)}) async-start(), calls=%async_computation.11 | async-start | bytes 3981312 | tf_op jit(solution)/shard_map/all_gather | solution.py:187
  7.9 5580.0 %all-gather.23.cloned.1.call-start = ((), (), s32[]{:S(2)}) async-start(), calls=%async_computation.12 | async-start | bytes 1327104 | tf_op jit(solution)/shard_map/all_gather | solution.py:188
  8.7 5617.8 %all-gather.33.cloned.1.call-start = ((), (), s32[]{:S(2)}) async-start(), calls=%async_computation.27 | async-start | bytes 5308416 | tf_op jit(solution)/shard_map/all_gather | solution.py:224
  11.8 5631.6 %all-gather.29.cloned.1.call-start = ((), (), s32[]{:S(2)}) async-start(), calls=%async_computation.25 | async-start | bytes 5308416 | tf_op jit(solution)/shard_map/all_gather | solution.py:224
  12.4 5647.5 %all-gather.25.cloned.1.call-start = ((), (), s32[]{:S(2)}) async-start(), calls=%async_computation.23 | async-start | bytes 5308416 | tf_op jit(solution)/shard_map/all_gather | solution.py:224
  12.9 5663.7 %all-gather.37.cloned.1.call-start = ((), (), s32[]{:S(2)}) async-start(), calls=%async_computation.29 | async-start | bytes 5308416 | tf_op jit(solution)/shard_map/all_gather | solution.py:224
  13.6 23.3 copy-start.67
  13.6 37.1 copy-start.72
  13.6 5679.9 %all-gather.35.cloned.1.call-start = ((), (), s32[]{:S(2)}) async-start(), calls=%async_computation.28 | async-start | bytes 5308416 | tf_op jit(solution)/shard_map/all_gather | solution.py:225
  15.1 5697.6 %all-gather.31.cloned.1.call-start = ((), (), s32[]{:S(2)}) async-start(), calls=%async_computation.26 | async-start | bytes 5308416 | tf_op jit(solution)/shard_map/all_gather | solution.py:225
  15.9 5718.6 %all-gather.27.cloned.1.call-start = ((), (), s32[]{:S(2)}) async-start(), calls=%async_computation.24 | async-start | bytes 5308416 | tf_op jit(solution)/shard_map/all_gather | solution.py:225
  16.6 5755.8 %all-gather.39.cloned.1.call-start = ((), (), s32[]{:S(2)}) async-start(), calls=%async_computation.30 | async-start | bytes 5308416 | tf_op jit(solution)/shard_map/all_gather | solution.py:225
  17.2 6018.9 %reduce-scatter.30.cloned.1.call-start = ((), (), s32[]{:S(2)}) async-start(), calls=%async_computation.21 | async-start | bytes 5308416 | tf_op jit(solution)/shard_map/reduce_scatter | solution.py:278
  17.3 66.3 copy-start.60
  1144.0 4251.6 %copy-start.61 = (s32[512]{0:T(512)S(1)}, s32[512]{0:T(512)}, u32[]{:S(2)}) copy-start(s32[512]{0:T(512)} %copy-done.60) | copy-start | bytes 6148
  5399.5 108.6 %copy-start.2 = (f32[1024,768]{1,0:T(8,128)}, f32[1024,768]{1,0:T(8,128)S(1)}, u32[]{:S(2)}) copy-start(f32[1024,768]{1,0:T(8,128)S(1)} %copy.169) | copy-start | bytes 9437188
  5468.1 40.0 copy-start.43
  5643.3 392.8 %reduce-scatter.28.cloned.1.call-start = ((), (), s32[]{:S(2)}) async-start(), calls=%async_computation.20 | async-start | bytes 5308416 | tf_op jit(solution)/shard_map/reduce_scatter | solution.py:278
  5659.8 376.4 %reduce-scatter.26.cloned.1.call-start = ((), (), s32[]{:S(2)}) async-start(), calls=%async_computation.19 | async-start | bytes 5308416 | tf_op jit(solution)/shard_map/reduce_scatter | solution.py:278
  5676.6 367.8 %reduce-scatter.32.cloned.1.call-start = ((), (), s32[]{:S(2)}) async-start(), calls=%async_computation.22 | async-start | bytes 5308416 | tf_op jit(solution)/shard_map/reduce_scatter | solution.py:278
  5693.4 449.5 %reduce-scatter.22.cloned.1.call-start = ((), (), s32[]{:S(2)}) async-start(), calls=%async_computation.17 | async-start | bytes 5308416 | tf_op jit(solution)/shard_map/reduce_scatter | solution.py:275
  5712.7 528.7 %reduce-scatter.20.cloned.1.call-start = ((), (), s32[]{:S(2)}) async-start(), calls=%async_computation.16 | async-start | bytes 5308416 | tf_op jit(solution)/shard_map/reduce_scatter | solution.py:275
  5732.0 608.0 %reduce-scatter.18.cloned.1.call-start = ((), (), s32[]{:S(2)}) async-start(), calls=%async_computation.15 | async-start | bytes 5308416 | tf_op jit(solution)/shard_map/reduce_scatter | solution.py:275
  5753.6 685.1 %reduce-scatter.24.cloned.1.call-start = ((), (), s32[]{:S(2)}) async-start(), calls=%async_computation.18 | async-start | bytes 5308416 | tf_op jit(solution)/shard_map/reduce_scatter | solution.py:275
  5922.0 636.7 %reduce-scatter.34.cloned.1.call-start = ((), (), s32[]{:S(2)}) async-start(), calls=%async_computation.31 | async-start | bytes 221184
  5957.1 41.4 slice-start.5
  6010.9 556.9 %reduce-scatter.16.cloned.1.call-start = ((), (), s32[]{:S(2)}) async-start(), calls=%async_computation.14 | async-start | bytes 1327104 | tf_op jit(solution)/shard_map/reduce_scatter | solution.py:333
  6015.9 635.7 %reduce-scatter.14.cloned.1.call-start = ((), (), s32[]{:S(2)}) async-start(), calls=%async_computation.13 | async-start | bytes 3981312 | tf_op jit(solution)/shard_map/reduce_scatter | solution.py:330
  6036.0 802.9 %all-reduce.14.cloned.1.call-start = ((), (), s32[]{:S(2)}) async-start(), calls=%async_computation.32 | async-start | bytes 18874368 | tf_op jit(solution)/shard_map/psum | solution.py:349
  6488.7 29.2 copy-start.16
  6488.7 38.5 slice-start.7
  (94 other events, 700.8 us)
Sparse Core Ops, SparseCore 0:
  10.2 65.3 all-gather.20
  77.7 39.6 all-gather.22
  119.7 78.0 all-gather.32
  199.8 78.0 all-gather.28
  279.9 78.0 all-gather.24
  360.0 78.0 all-gather.36
  440.3 77.9 all-gather.34
  520.5 78.0 all-gather.30
  600.8 78.0 all-gather.26
  680.9 78.0 all-gather.38
  5643.4 104.9 reduce-scatter.29
  5752.0 94.9 reduce-scatter.27
  5850.6 95.1 reduce-scatter.25
  5949.3 94.9 reduce-scatter.31
  6047.9 95.0 reduce-scatter.21
  6146.4 94.9 reduce-scatter.19
  6245.0 94.9 reduce-scatter.17
  6343.5 95.1 reduce-scatter.23
  6442.5 58.9 reduce-scatter.33
  6504.8 62.9 reduce-scatter.15
  6571.4 80.1 reduce-scatter.13
  6654.7 184.1 all-reduce.13
where the time goes:
time: 6860 us; the launch traced here: 6850 us
  local copies, waits for them, and re-layouts  5620 us (82%)
  waiting for transfers between devices  638 us (9%)
  matrix products  356 us (5%)
  blocking collectives  116 us (2%)
  other arithmetic  108 us (2%)
    gather x4, local copies, waits for them, and re-layouts, pair_layout(): jnp.take(bucket_ids, jnp.maximum(distance, 0), axis=0).reshape(-1)  5290 us
    reduce_scatter x4, waiting for transfers between devices, body(): lax.psum_scatter(grad_w_in.astype(jnp.bfloat16), 'shard', scatter_dimensi...  390 us
    unnamed x233, local copies, waits for them, and re-layouts  163 us
    psum x1, waiting for transfers between devices, body(): lax.psum((sum_one, sum_qkv, sum_attn, sum_table, sum_two, sum_router, gra...  143 us
  transfers between devices with their start and end apart: 22, of which 8 were waited for; matrix products, arithmetic and copies ran while one was open for 88% of the time, Pallas kernels for 0%

commit v1 on v0

v1 whole, which is shorter than its diff:
```python
import functools

import jax
import jax.numpy as jnp
from jax import lax
from jax.experimental import pallas as pl
from jax.experimental.pallas import tpu as pltpu
from jax.sharding import PartitionSpec as P

D = 768
HEADS = 12
HEAD_DIM = 64
FF = 3072
EXPERTS = 4
BUCKETS = 32
SEQ = 1024
CAP = 640
BLOCK = 256
REACH = 768
NORM_EPSILON = 1e-06
HIGHEST = lax.Precision.HIGHEST
NEG = -1e30
F32 = jnp.float32
BF16 = jnp.bfloat16
MIB = 1024 * 1024
GELU_ROOT = 0.7978845608028654
GELU_CUBE = 0.044715


def norm_forward(values, gain_vec):
    inv_rms = lax.rsqrt(jnp.mean(values * values, axis=-1, keepdims=True) + NORM_EPSILON)
    unit_rows = values * inv_rms
    return unit_rows, inv_rms, unit_rows * gain_vec


def norm_backward(grad_norm, unit_rows, inv_rms, gain_vec):
    grad_unit = grad_norm * gain_vec
    grad_gain = jnp.sum(grad_norm * unit_rows, axis=0)
    grad_input = inv_rms * (
        grad_unit - unit_rows * jnp.mean(grad_unit * unit_rows, axis=-1, keepdims=True)
    )
    return grad_input, grad_gain


def key_span(block):
    low = max(0, (block + 1) * BLOCK - REACH)
    return low, (block + 1) * BLOCK - low


def fill_mask(seg_col_ref, seg_row_ref, mask_ref):
    for block in range(SEQ // BLOCK):
        low, width = key_span(block)
        same = (
            seg_col_ref[low : low + width, :]
            == seg_row_ref[:, block * BLOCK : (block + 1) * BLOCK]
        )
        mask_ref[block, REACH - width :, :] = jnp.where(same, 0.0, NEG)


def fill_bias(line_ref, bias_ref):
    for head in range(2):
        for part in range(3):
            rows = line_ref[0, 3 * head + part : 3 * head + part + 1, :]
            count = 1
            while count < BLOCK:
                rows = jnp.concatenate([rows, pltpu.roll(rows, count, 1)], axis=0)
                count *= 2
            bias_ref[head, part * BLOCK : (part + 1) * BLOCK, :] = rows[:, :BLOCK]


def diagonal_sums(square):
    rows = jnp.concatenate([square, jnp.zeros_like(square)], axis=1)
    count = BLOCK
    while count > 1:
        count //= 2
        rows = rows[:count] + pltpu.roll(rows[count:], 2 * BLOCK - count, 1)
    return rows


def head_lanes(head, rows):
    lane = lax.broadcasted_iota(jnp.int32, rows.shape, 1)
    return jnp.where(lane // HEAD_DIM == head, rows, jnp.zeros_like(rows))


def dot_nt(left, right):
    return lax.dot_general(left, right, (((1,), (1,)), ((), ())), preferred_element_type=F32)


def dot_nn(left, right):
    return jnp.dot(left, right, preferred_element_type=F32)


def attention_kernel(
    q_ref, k_ref, v_ref, seg_col_ref, seg_row_ref, line_ref, out_ref, total_ref, mask_ref, bias_ref
):
    @pl.when(pl.program_id(0) == 0)
    def _():
        fill_mask(seg_col_ref, seg_row_ref, mask_ref)

    fill_bias(line_ref, bias_ref)
    values_t = v_ref[...].T
    for block in range(SEQ // BLOCK):
        low, width = key_span(block)
        here = slice(block * BLOCK, (block + 1) * BLOCK)
        queries = q_ref[here, :] * jnp.asarray(HEAD_DIM**-0.5, BF16)
        parts = []
        for head in range(2):
            scores = dot_nt(k_ref[low : low + width, :], head_lanes(head, queries))
            scores = scores + bias_ref[head, REACH - width :, :] + mask_ref[block, REACH - width :, :]
            top = jnp.max(scores, axis=0, keepdims=True)
            weights = jnp.exp(scores - top)
            denom = jnp.sum(weights, axis=0, keepdims=True)
            mixed = dot_nn(values_t[:, low : low + width], weights.astype(BF16))
            parts.append(mixed[head * HEAD_DIM : (head + 1) * HEAD_DIM, :] / denom)
            total_ref[0, head : head + 1, here] = top + jnp.log(denom)
        out_ref[here, :] = jnp.concatenate(parts, axis=0).T.astype(BF16)


def attention_back_kernel(
    q_ref, k_ref, v_ref, out_ref, grad_ref, total_ref, seg_col_ref, seg_row_ref, line_ref,
    dqkv_ref, dline_ref, mask_ref, bias_ref, dbias_ref, dk_ref, dv_ref,
):
    @pl.when(pl.program_id(0) == 0)
    def _():
        fill_mask(seg_col_ref, seg_row_ref, mask_ref)

    fill_bias(line_ref, bias_ref)
    keys_t = k_ref[...].T
    dk_ref[...] = jnp.zeros_like(dk_ref)
    dv_ref[...] = jnp.zeros_like(dv_ref)
    dbias_ref[...] = jnp.zeros_like(dbias_ref)
    scale = HEAD_DIM**-0.5
    for block in range(SEQ // BLOCK):
        low, width = key_span(block)
        here = slice(block * BLOCK, (block + 1) * BLOCK)
        span = slice(low, low + width)
        queries = q_ref[here, :] * jnp.asarray(scale, BF16)
        grads = grad_ref[here, :]
        inner = (grads.astype(F32) * out_ref[here, :].astype(F32)).T
        parts = []
        for head in range(2):
            rows = slice(head * HEAD_DIM, (head + 1) * HEAD_DIM)
            query_head = head_lanes(head, queries)
            grad_head = head_lanes(head, grads)
            scores = dot_nt(k_ref[span, :], query_head)
            scores = scores + bias_ref[head, REACH - width :, :] + mask_ref[block, REACH - width :, :]
            probs = jnp.exp(scores - total_ref[0, head : head + 1, here])
            grad_probs = dot_nt(v_ref[span, :], grad_head)
            delta = jnp.sum(inner[rows, :], axis=0, keepdims=True)
            grad_scores = probs * (grad_probs - delta)
            dbias_ref[head, REACH - width :, :] += grad_scores
            low_scores = grad_scores.astype(BF16)
            dv_ref[span, :] += dot_nn(probs.astype(BF16), grad_head)
            dk_ref[span, :] += dot_nn(low_scores, query_head)
            parts.append(dot_nn(keys_t[:, span], low_scores)[rows, :])
        dqkv_ref[0, here, :] = (jnp.concatenate(parts, axis=0).T * scale).astype(BF16)
    dqkv_ref[1, :, :] = dk_ref[...].astype(BF16)
    dqkv_ref[2, :, :] = dv_ref[...].astype(BF16)
    for head in range(2):
        for part in range(3):
            sums = diagonal_sums(dbias_ref[head, part * BLOCK : (part + 1) * BLOCK, :])
            dline_ref[0, 3 * head + part : 3 * head + part + 1, :] = sums
    dline_ref[0, 6:8, :] = jnp.zeros((2, 2 * BLOCK), F32)


def pair_spec(offset):
    return pl.BlockSpec((SEQ, 2 * HEAD_DIM), lambda pair: (0, pair + offset))


PAIRS = HEADS // 2
SEG_SPECS = [
    pl.BlockSpec((SEQ, 1), lambda pair: (0, 0)),
    pl.BlockSpec((1, SEQ), lambda pair: (0, 0)),
    pl.BlockSpec((1, 8, 2 * BLOCK), lambda pair: (pair, 0, 0)),
]
TOTAL_SPEC = pl.BlockSpec((1, 8, SEQ), lambda pair: (pair, 0, 0))
PAIR_SCRATCH = [
    pltpu.VMEM((SEQ // BLOCK, REACH, BLOCK), F32),
    pltpu.VMEM((2, REACH, BLOCK), F32),
]


def attend_forward(qkv_rows, seg_col, seg_row, lines):
    return pl.pallas_call(
        attention_kernel,
        grid=(PAIRS,),
        in_specs=[pair_spec(0), pair_spec(PAIRS), pair_spec(2 * PAIRS)] + SEG_SPECS,
        out_specs=[pair_spec(0), TOTAL_SPEC],
        out_shape=[
            jax.ShapeDtypeStruct((SEQ, D), BF16),
            jax.ShapeDtypeStruct((PAIRS, 8, SEQ), F32),
        ],
        scratch_shapes=PAIR_SCRATCH,
        compiler_params=pltpu.CompilerParams(vmem_limit_bytes=48 * MIB),
        cost_estimate=pl.CostEstimate(
            flops=4 * SEQ * SEQ * D, bytes_accessed=8 * SEQ * D, transcendentals=0
        ),
        name="attend_forward",
    )(qkv_rows, qkv_rows, qkv_rows, seg_col, seg_row, lines)


def attend_backward(qkv_rows, attended, grad_attended, totals, seg_col, seg_row, lines):
    return pl.pallas_call(
        attention_back_kernel,
        grid=(PAIRS,),
        in_specs=[
            pair_spec(0), pair_spec(PAIRS), pair_spec(2 * PAIRS), pair_spec(0), pair_spec(0), TOTAL_SPEC,
        ] + SEG_SPECS,
        out_specs=[
            pl.BlockSpec((3, SEQ, 2 * HEAD_DIM), lambda pair: (0, 0, pair)),
            pl.BlockSpec((1, 8, 2 * BLOCK), lambda pair: (pair, 0, 0)),
        ],
        out_shape=[
            jax.ShapeDtypeStruct((3, SEQ, D), BF16),
            jax.ShapeDtypeStruct((PAIRS, 8, 2 * BLOCK), F32),
        ],
        scratch_shapes=PAIR_SCRATCH + [
            pltpu.VMEM((2, REACH, BLOCK), F32),
            pltpu.VMEM((SEQ, 2 * HEAD_DIM), F32),
            pltpu.VMEM((SEQ, 2 * HEAD_DIM), F32),
        ],
        compiler_params=pltpu.CompilerParams(vmem_limit_bytes=48 * MIB),
        cost_estimate=pl.CostEstimate(
            flops=10 * SEQ * SEQ * D, bytes_accessed=16 * SEQ * D, transcendentals=0
        ),
        name="attend_backward",
    )(qkv_rows, qkv_rows, qkv_rows, attended, grad_attended, totals, seg_col, seg_row, lines)


def bias_lines(bias_vec):
    reach = jnp.concatenate([jnp.full((HEADS, BLOCK), NEG, F32), bias_vec], axis=1)
    parts = []
    for part in range(3):
        middle = REACH - part * BLOCK
        parts.append(
            jnp.concatenate([reach[:, middle : middle + BLOCK], reach[:, middle - BLOCK : middle]], axis=1)
        )
    lines = jnp.stack(parts, axis=1).reshape(PAIRS, 6, 2 * BLOCK)
    return jnp.concatenate([lines, jnp.zeros((PAIRS, 2, 2 * BLOCK), F32)], axis=1)


def bias_line_grads(grad_lines):
    parts = grad_lines[:, :6].reshape(HEADS, 3, 2 * BLOCK)
    total = jnp.zeros((HEADS, SEQ + BLOCK), F32)
    for part in range(3):
        middle = REACH - part * BLOCK
        line = jnp.concatenate([parts[:, part, BLOCK:], parts[:, part, :BLOCK]], axis=1)
        total = total + jnp.pad(line, ((0, 0), (middle - BLOCK, SEQ - middle)))
    return total[:, BLOCK:]


FF_BLOCK = 512


def expert_kernel(
    rows_ref, grad_ref, gate_ref, w_in_ref, w_out_ref,
    act_ref, dhid_ref, dout_ref, out_ref, drow_ref, dgate_ref, out_acc, drow_acc,
):
    gates = gate_ref[...]
    dout_ref[...] = (gates * grad_ref[...].astype(F32)).astype(BF16)
    out_acc[...] = jnp.zeros_like(out_acc)
    drow_acc[...] = jnp.zeros_like(drow_acc)

    def step(index, carry):
        cols = pl.ds(pl.multiple_of(index * FF_BLOCK, FF_BLOCK), FF_BLOCK)
        w_in = w_in_ref[:, cols]
        w_out = w_out_ref[cols, :]
        hidden = dot_nn(rows_ref[...], w_in)
        grad_act = dot_nt(dout_ref[...], w_out)
        square = hidden * hidden
        bend = jnp.tanh(hidden * (GELU_ROOT + (GELU_ROOT * GELU_CUBE) * square))
        half = 0.5 + 0.5 * bend
        act = (hidden * half).astype(BF16)
        slope = half + 0.5 * hidden * (1.0 - bend * bend) * (
            GELU_ROOT + (3.0 * GELU_ROOT * GELU_CUBE) * square
        )
        dhid = (grad_act * slope).astype(BF16)
        act_ref[:, cols] = act
        dhid_ref[:, cols] = dhid
        out_acc[...] += dot_nn(act, w_out)
        drow_acc[...] += dot_nt(dhid, w_in)
        return carry

    lax.fori_loop(0, FF // FF_BLOCK, step, 0)
    outs = out_acc[...]
    out_ref[...] = (gates * outs).astype(BF16)
    drow_ref[...] = drow_acc[...].astype(BF16)
    dgate_ref[...] = jnp.sum(grad_ref[...].astype(F32) * outs, axis=1, keepdims=True)


def run_expert(rows, grads, gates, w_in, w_out):
    count = rows.shape[0] // CAP
    row_spec = pl.BlockSpec((CAP, D), lambda part: (part, 0))
    wide_spec = pl.BlockSpec((CAP, FF), lambda part: (part, 0))
    gate_spec = pl.BlockSpec((CAP, 1), lambda part: (part, 0))
    once = pl.Buffered(1)
    narrow = jax.ShapeDtypeStruct((count * CAP, D), BF16)
    wide = jax.ShapeDtypeStruct((count * CAP, FF), BF16)
    return pl.pallas_call(
        expert_kernel,
        grid=(count,),
        in_specs=[
            row_spec,
            row_spec,
            gate_spec,
            pl.BlockSpec((D, FF), lambda part: (0, 0), pipeline_mode=once),
            pl.BlockSpec((FF, D), lambda part: (0, 0), pipeline_mode=once),
        ],
        out_specs=[wide_spec, wide_spec, row_spec, row_spec, row_spec, gate_spec],
        out_shape=[wide, wide, narrow, narrow, narrow, jax.ShapeDtypeStruct((count * CAP, 1), F32)],
        scratch_shapes=[pltpu.VMEM((CAP, D), F32), pltpu.VMEM((CAP, D), F32)],
        compiler_params=pltpu.CompilerParams(vmem_limit_bytes=56 * MIB),
        cost_estimate=pl.CostEstimate(
            flops=8 * count * CAP * D * FF, bytes_accessed=4 * D * FF + 4 * count * CAP * FF, transcendentals=0
        ),
        name="run_expert",
    )(rows, grads, gates, w_in, w_out)


def split_three(values):
    first = values.astype(BF16)
    rest = values - first.astype(F32)
    second = rest.astype(BF16)
    third = (rest - second.astype(F32)).astype(BF16)
    return jnp.stack([first, second, third], axis=-1)


def body(
    dp_size, tokens, segment_ids, routes, buckets, norm1_gain, w_qkv, w_attn_out, bias_table,
    norm2_gain, router, w_in, w_expert_out, cotangent,
):
    shard_rows = w_qkv.shape[0]
    table_rows = bias_table.shape[0]
    me = lax.axis_index("dp") % EXPERTS

    def swap(value, relation):
        if relation == 0:
            return value
        return lax.ppermute(value, "dp", [(i, i ^ relation) for i in range(dp_size)])

    def spread(value):
        across = swap(value, 2)
        return [value, swap(value, 1), across, swap(across, 1)]

    table_col = jnp.pad(bias_table.reshape(-1), (0, shard_rows - table_rows * HEADS))
    small = jnp.concatenate(
        [norm1_gain[:, None], norm2_gain[:, None], router, table_col[:, None]], axis=1
    )
    packed = jnp.concatenate([w_qkv, w_attn_out, jnp.pad(small, ((0, 0), (0, 121)))], axis=1)
    packed = lax.all_gather(packed, "shard", axis=0, tiled=True)
    qkv_weight = packed[:, : 3 * D]
    attn_weight = packed[:, 3 * D : 4 * D]
    gain_one = packed[:, 4 * D].astype(F32)
    gain_two = packed[:, 4 * D + 1].astype(F32)
    router_weight = packed[:, 4 * D + 2 : 4 * D + 6]
    bias_full = packed[:, 4 * D + 6].reshape(-1, shard_rows)[:, : table_rows * HEADS].reshape(BUCKETS, HEADS)

    my_in = lax.dynamic_index_in_dim(w_in, me, 0, keepdims=False)
    my_out = lax.dynamic_index_in_dim(w_expert_out, me, 0, keepdims=False)
    full_in = lax.all_gather(my_in, "shard", axis=0, tiled=True)
    full_out = lax.all_gather(my_out, "shard", axis=0, tiled=True)

    cot_parts = spread(cotangent)

    expert_ids = jnp.arange(EXPERTS, dtype=jnp.int32)
    hits = (
        (routes[:, 0][None, :] == expert_ids[:, None]) | (routes[:, 1][None, :] == expert_ids[:, None])
    ).astype(F32)
    token_ids = jnp.arange(SEQ, dtype=jnp.int32)
    before = (token_ids[:, None] < token_ids[None, :]).astype(BF16)
    places = jnp.dot(hits.astype(BF16), before, preferred_element_type=F32)
    keys = jnp.where(hits > 0, places, -1.0)
    relation_ids = me ^ expert_ids

    def related(rows):
        return [lax.dynamic_index_in_dim(rows, relation_ids[x], 0, keepdims=False) for x in range(EXPERTS)]

    slot_ids = jnp.arange(CAP, dtype=F32)

    def pick_matrix(key_row):
        return (key_row[None, :] == slot_ids[:, None]).astype(BF16)

    my_keys = related(keys)
    their_picks = [pick_matrix(swap(my_keys[x], x)) for x in range(EXPERTS)]
    my_picks = jnp.concatenate([pick_matrix(my_keys[x]) for x in range(EXPERTS)], axis=0)
    grad_slots = [
        jnp.dot(their_picks[x], cot_parts[x], preferred_element_type=F32).astype(BF16) for x in range(EXPERTS)
    ]

    bucket_hits = (jnp.arange(BUCKETS, dtype=jnp.int32)[:, None] == buckets[None, :]).astype(BF16)
    bias_vec = lax.dot_general(bias_full, bucket_hits, (((0,), (0,)), ((), ())), preferred_element_type=F32)
    lines = bias_lines(bias_vec)
    seg_col, seg_row = segment_ids[:, None], segment_ids[None, :]

    token_rows = tokens.astype(F32)
    unit_one, inv_one, normed_one = norm_forward(token_rows, gain_one)
    act_one = normed_one.astype(BF16)
    qkv_rows = jnp.dot(act_one, qkv_weight, preferred_element_type=F32).astype(BF16)
    attended, totals = attend_forward(qkv_rows, seg_col, seg_row, lines)
    residual = token_rows + jnp.dot(attended, attn_weight, preferred_element_type=F32)
    unit_two, inv_two, normed_two = norm_forward(residual, gain_two)
    act_two = normed_two.astype(BF16)
    act_parts = spread(act_two)

    logits = lax.dot_general(router_weight, act_two, (((0,), (1,)), ((), ())), preferred_element_type=F32)
    shifted = jnp.exp(logits - jnp.max(logits, axis=0, keepdims=True))
    prob_all = shifted / jnp.sum(shifted, axis=0, keepdims=True)
    chosen_sum = jnp.sum(hits * prob_all, axis=0, keepdims=True)
    gates = hits * prob_all / chosen_sum
    my_gates = related(gates)
    their_gates = [swap(my_gates[x], x) for x in range(EXPERTS)]

    def dispatch(relations):
        rows = jnp.concatenate(
            [jnp.dot(their_picks[x], act_parts[x], preferred_element_type=F32).astype(BF16) for x in relations], axis=0
        )
        gate_col = jnp.concatenate(
            [
                jnp.sum(
                    jnp.dot(their_picks[x], split_three(their_gates[x]), preferred_element_type=F32),
                    axis=1,
                    keepdims=True,
                )
                for x in relations
            ],
            axis=0,
        )
        return rows, gate_col

    halves = []
    for relations in ((0, 1), (2, 3)):
        rows, gate_col = dispatch(relations)
        grads = jnp.concatenate([grad_slots[x] for x in relations], axis=0)
        halves.append((rows,) + tuple(run_expert(rows, grads, gate_col, full_in, full_out)))

    def back_to_tokens(picks, dgate_rows):
        parts = split_three(dgate_rows[:, 0])
        return jnp.sum(
            lax.dot_general(parts, picks, (((0,), (0,)), ((), ())), preferred_element_type=F32), axis=0
        )

    out_parts, drow_parts, dgate_parts = [], [], []
    for half, relations in zip(halves, ((0, 1), (2, 3))):
        _, _, _, _, outs, drows, dgates = half
        for index, x in enumerate(relations):
            part = slice(index * CAP, (index + 1) * CAP)
            drow_parts.append(swap(drows[part], x))
            out_parts.append(swap(outs[part], x))
            dgate_parts.append(swap(back_to_tokens(their_picks[x], dgates[part]), x))

    def weight_grad(left, right):
        total = lax.dot_general(left[0], right[0], (((0,), (0,)), ((), ())), preferred_element_type=F32)
        total += lax.dot_general(left[1], right[1], (((0,), (0,)), ((), ())), preferred_element_type=F32)
        return total.astype(BF16)

    grad_in = weight_grad([h[0] for h in halves], [h[2] for h in halves])
    grad_out = weight_grad([h[1] for h in halves], [h[3] for h in halves])
    grad_in = lax.psum_scatter(grad_in, "shard", scatter_dimension=0, tiled=True)
    grad_out = lax.psum_scatter(grad_out, "shard", scatter_dimension=0, tiled=True)

    def over_groups(value):
        total = value.astype(F32)
        for group in range(1, dp_size // EXPERTS):
            moved = lax.ppermute(value, "dp", [(i, (i + EXPERTS * group) % dp_size) for i in range(dp_size)])
            total = total + moved.astype(F32)
        return total.astype(BF16)

    def place(value):
        parts = spread(over_groups(value))
        out = jnp.zeros((EXPERTS,) + value.shape, F32)
        for x in range(EXPERTS):
            out = lax.dynamic_update_index_in_dim(out, parts[x].astype(F32), relation_ids[x], 0)
        return out

    grad_w_in = place(grad_in)
    grad_w_out = place(grad_out)

    def collect(parts):
        stacked = jnp.concatenate(parts, axis=0)
        return lax.dot_general(my_picks, stacked, (((0,), (0,)), ((), ())), preferred_element_type=F32)

    mixed_out = (residual + collect(out_parts)).astype(BF16)
    grad_act_two = collect(drow_parts)
    grad_gates = jnp.stack(related(jnp.stack(dgate_parts, axis=0)), axis=0)
    weighted = jnp.sum(grad_gates * gates, axis=0, keepdims=True)
    grad_prob = hits * (grad_gates - weighted) / chosen_sum
    grad_logits = (prob_all * (grad_prob - jnp.sum(prob_all * grad_prob, axis=0, keepdims=True))).astype(BF16)
    grad_router = lax.dot_general(act_two, grad_logits, (((0,), (1,)), ((), ())), preferred_element_type=F32)
    grad_act_two = grad_act_two + lax.dot_general(
        grad_logits, router_weight, (((0,), (1,)), ((), ())), preferred_element_type=F32
    )
    grad_norm_two, grad_gain_two = norm_backward(grad_act_two, unit_two, inv_two, gain_two)
    grad_residual = cotangent.astype(F32) + grad_norm_two
    grad_branch = grad_residual.astype(BF16)
    grad_attn_weight = lax.dot_general(
        attended, grad_branch, (((0,), (0,)), ((), ())), preferred_element_type=F32
    )
    grad_attended = dot_nt(grad_branch, attn_weight).astype(BF16)
    grad_split, grad_lines = attend_backward(
        qkv_rows, attended, grad_attended, totals, seg_col, seg_row, lines
    )
    grad_act_one = sum(dot_nt(grad_split[i], qkv_weight[:, i * D : (i + 1) * D]) for i in range(3))
    grad_qkv_weight = [
        lax.dot_general(act_one, grad_split[i], (((0,), (0,)), ((), ())), preferred_element_type=F32)
        for i in range(3)
    ]
    grad_norm_one, grad_gain_one = norm_backward(grad_act_one, unit_one, inv_one, gain_one)
    grad_tokens = (grad_residual + grad_norm_one).astype(BF16)
    grad_table = lax.dot_general(
        bucket_hits.astype(F32), bias_line_grads(grad_lines), (((1,), (1,)), ((), ())), precision=HIGHEST
    )
    shards = D // shard_rows
    table_sums = jnp.pad(
        grad_table.reshape(shards, table_rows * HEADS), ((0, 0), (0, shard_rows - table_rows * HEADS))
    ).reshape(D, 1)
    small = jnp.concatenate([grad_gain_one[:, None], grad_gain_two[:, None], grad_router, table_sums], axis=1)
    packed = jnp.concatenate(
        [g.astype(BF16) for g in grad_qkv_weight]
        + [grad_attn_weight.astype(BF16), jnp.pad(small, ((0, 0), (0, 121))).astype(BF16)],
        axis=1,
    )
    packed = lax.psum_scatter(packed, "shard", scatter_dimension=0, tiled=True).astype(F32)
    packed = lax.psum(packed, "dp")
    return (
        mixed_out,
        grad_tokens,
        packed[:, 4 * D],
        packed[:, : 3 * D],
        packed[:, 3 * D : 4 * D],
        packed[:, 4 * D + 6][: table_rows * HEADS].reshape(table_rows, HEADS),
        packed[:, 4 * D + 1],
        packed[:, 4 * D + 2 : 4 * D + 6],
        grad_w_in,
        grad_w_out,
    )


def solution(mesh):
    return jax.shard_map(
        functools.partial(body, mesh.shape["dp"]),
        mesh=mesh,
        in_specs=(
            P(("dp", "shard"), None),
            P(("dp", "shard")),
            P(("dp", "shard"), None),
            P(),
            P("shard"),
            P("shard", None),
            P("shard", None),
            P("shard", None),
            P("shard"),
            P("shard", None),
            P(None, "shard", None),
            P(None, "shard", None),
            P(("dp", "shard"), None),
        ),
        out_specs=(
            P(("dp", "shard"), None),
            P(("dp", "shard"), None),
            P("shard"),
            P("shard", None),
            P("shard", None),
            P("shard", None),
            P("shard"),
            P("shard", None),
            P(None, "shard", None),
            P(None, "shard", None),
        ),
        check_vma=False,
    )
```

time: 6860 us -> 715 us (0.10)
  local copies, waits for them, and re-layouts: 5620 us -> 66.2 us
  waiting for transfers between devices: 638 us -> 247 us
  matrix products: 356 us -> 135 us
  Pallas kernels: 0 us -> 138 us
  blocking collectives: 116 us -> 34.8 us
  other arithmetic: 108 us -> 35.8 us
    gather x11 -> x0, local copies, waits for them, and re-layouts: 5370 us -> none  [the longest x4 5290 us: pair_layout(): jnp.take(bucket_ids, jnp.maximum(distance, 0), axis=0).reshape(-1)]
    reduce_scatter x10 -> x2, waiting for transfers between devices: 491 us -> 0.01 us  [the longest x1 0.01 us: body(): lax.psum_scatter(grad_out, 'shard', scatter_dimension=0, tiled=True)]
    dot_general x49 -> x38, matrix products: 356 us -> 135 us  [the longest x2 24.1 us: weight_grad(): lax.dot_general(left[1], right[1], (((0,), (0,)), ((), ())), preferred_el...]
    psum x1 -> x0, waiting for transfers between devices: 143 us -> none  [body(): lax.psum((sum_one, sum_qkv, sum_attn, sum_table, sum_two, sum_router, gra...]
    ppermute x0 -> x27, waiting for transfers between devices: none -> 142 us  [swap(): lax.ppermute(value, 'dp', [(i, i ^ relation) for i in range(dp_size)])]
    pallas_call x0 -> x4, Pallas kernels: none -> 138 us  [the longest x2 77.6 us: run_expert(): pl.pallas_call(expert_kernel, grid=(count,), in_specs=[row_spec, row_spec...]
    unnamed x233 -> x111, local copies, waits for them, and re-layouts: 163 us -> 26.8 us
    all_gather x10 -> x3, waiting for transfers between devices: 0.12 us -> 91.1 us  [the longest x1 47.8 us: body(): full_out = lax.all_gather(my_out, 'shard', axis=0, tiled=True)]
  transfers between devices with their start and end apart: 22 -> 33, of which waited for: 8 -> 15; matrix products, arithmetic and copies ran while one was open for 88% -> 29% of each run, Pallas kernels for 0% -> 14%
where the time goes in v1:
time: 715 us; the launch traced here: 707 us
  waiting for transfers between devices  247 us (35%)
  Pallas kernels  138 us (19%)
  matrix products  135 us (19%)
  local copies, waits for them, and re-layouts  66.2 us (9%)
  other arithmetic  35.8 us (5%)
  blocking collectives  34.8 us (5%)
  starting transfers between devices  27.6 us (4%)
  between operations  23.2 us (3%)
    ppermute x27, waiting for transfers between devices, swap(): lax.ppermute(value, 'dp', [(i, i ^ relation) for i in range(dp_size)])  142 us
    pallas_call x2, Pallas kernels, run_expert(): pl.pallas_call(expert_kernel, grid=(count,), in_specs=[row_spec, row_spec...  77.6 us
    all_gather x1, waiting for transfers between devices, body(): full_out = lax.all_gather(my_out, 'shard', axis=0, tiled=True)  47.8 us
    all_gather x1, waiting for transfers between devices, body(): packed = lax.all_gather(packed, 'shard', axis=0, tiled=True)  43.4 us
    psum x1, blocking collectives, body(): packed = lax.psum(packed, 'dp')  34.8 us
    pallas_call x1, Pallas kernels, attend_backward(): pl.pallas_call(attention_back_kernel, grid=(PAIRS,), in_specs=[pair_spec(...  31.6 us
    pallas_call x1, Pallas kernels, attend_forward(): pl.pallas_call(attention_kernel, grid=(PAIRS,), in_specs=[pair_spec(0), p...  28.5 us
    ppermute x27, starting transfers between devices, swap(): lax.ppermute(value, 'dp', [(i, i ^ relation) for i in range(dp_size)])  26.9 us
  transfers between devices with their start and end apart: 33, of which 15 were waited for; matrix products, arithmetic and copies ran while one was open for 29% of the time, Pallas kernels for 14%

profile of v1, /device:TPU:9, one launch (start us, length us, event | category | flops | bytes accessed | tf_op | source)
XLA Modules:
  0.0 706.8 jit_solution(17087559752181629367)
XLA Ops:
  27.1 20.6 %collective-permute-done.9 = bf16[1024,768]{1,0:T(8,128)(2,1)} collective-permute-done((bf16[1024,768]{1,0:T(8,128)(2,1)}, bf16[1024,768]{1,0:T(8,128)(2,1)}, u32[]{:S(2)}, u32[]{:S(2)}) %collective-permute-start.9) | collective-permute-done | bytes 1572896 | tf_op jit(solution)/shard_map/ppermute | solution.py:339
  49.2 43.4 %all-gather.6.cloned.1.call-done = bf16[768,3200]{1,0:T(8,128)(2,1)} async-done(((bf16[96,3200]{1,0:T(8,128)(2,1)}), bf16[768,3200]{1,0:T(8,128)(2,1)}) %all-gather.6.cloned.1.call-update) | async-done | bytes 4915216 | tf_op jit(solution)/shard_map/all_gather | solution.py:350
  95.6 7.8 %convolution_convert_fusion.q_ref.k_ref.v_ref = bf16[1024,2304]{1,0:T(8,128)(2,1)} fusion(bf16[768,3200]{1,0:T(8,128)(2,1)} %all-gather.6.cloned.1.call-done, bf16[1024,768]{0,1:T(8,128)(2,1)S(1)} %copy.108, f32[768]{0:T(1024)S(1)} %get-tuple-element.85, f32[1024]{0:T(1024)S(1)} %add_rsqrt_fusion.1), kind=kOutput, calls=%fused_computation.3 | convolution fusion | flops 3629383680 | bytes 9837568 | tf_op jit(solution)/shard_map/dot_general | solution.py:398
  103.4 28.5 %attend_forward.1 = (bf16[1024,768]{1,0:T(8,128)(2,1)S(1)}, f32[6,8,1024]{2,1,0:T(8,128)S(1)}) custom-call(bf16[1024,2304]{1,0:T(8,128)(2,1)} %convolution_convert_fusion.q_ref.k_ref.v_ref, bf16[1024,2304]{1,0:T(8,128)(2,1)} %convolution_convert_fusion.q_ref.k_ref.v_ref, bf16[1024,2304]{1,0:T(8,128)(2,1)} %convolution_convert_fusion.q_ref.k_ref.v_ref, ...), custom_call_target="tpu_custom_call" | custom-call | flops 3221225472 | bytes 6291456 | tf_op jit(solution)/shard_map/attend_forward/pallas_call | solution.py:184
  131.9 3.0 multiply_reduce_fusion.2
  148.3 26.4 %collective-permute-done.11 = f32[1024]{0:T(1024)S(1)} collective-permute-done((f32[1024]{0:T(1024)S(1)}, f32[1024]{0:T(1024)S(1)}, u32[]{:S(2)}, u32[]{:S(2)}) %collective-permute-start.11) | collective-permute-done | bytes 4128 | tf_op jit(solution)/shard_map/ppermute | solution.py:339
  195.7 3.1 fusion.88
  205.4 47.8 %all-gather.10.cloned.1.call-done = bf16[1,3072,768]{2,1,0:T(8,128)(2,1)} async-done(((bf16[1,384,768]{2,1,0:T(8,128)(2,1)}), bf16[1,3072,768]{2,1,0:T(8,128)(2,1)}) %all-gather.10.cloned.1.call-update) | async-done | bytes 4718608 | tf_op jit(solution)/shard_map/all_gather | solution.py:361
  253.1 38.7 %run_expert.2 = (bf16[1280,3072]{1,0:T(8,128)(2,1)}, bf16[1280,3072]{1,0:T(8,128)(2,1)}, bf16[1280,768]{1,0:T(8,128)(2,1)}, bf16[1280,768]{1,0:T(8,128)(2,1)}, b...) custom-call(bf16[1280,768]{1,0:T(8,128)(2,1)} %pad_maximum_fusion.rows_ref, bf16[1280,768]{1,0:T(8,128)(2,1)} %pad_maximum_fusion.1.grad_ref, ...), custom_call_target="tpu_custom_call" | custom-call | flops 24159191040 | bytes 25165824 | tf_op jit(solution)/shard_map/run_expert/pallas_call | solution.py:299
  296.5 10.9 %fusion.261 = f32[3072,768]{1,0:T(8,128)} fusion(bf16[1280,3072]{1,0:T(8,128)(2,1)} %get-tuple-element.38, bf16[1280,768]{1,0:T(8,128)(2,1)S(1)} %copy-done.45), kind=kOutput, calls=%fused_computation.351 | convolution fusion | flops 6039797760 | bytes 19267584 | tf_op jit(solution)/shard_map/dot_general | solution.py:452
  311.1 38.8 %run_expert.3 = (bf16[1280,3072]{1,0:T(8,128)(2,1)}, bf16[1280,3072]{1,0:T(8,128)(2,1)}, bf16[1280,768]{1,0:T(8,128)(2,1)}, bf16[1280,768]{1,0:T(8,128)(2,1)}, b...) custom-call(bf16[1280,768]{1,0:T(8,128)(2,1)} %pad_maximum_fusion.2.rows_ref, bf16[1280,768]{1,0:T(8,128)(2,1)} %pad_maximum_fusion.3.grad_ref, ...), custom_call_target="tpu_custom_call" | custom-call | flops 24159191040 | bytes 25165824 | tf_op jit(solution)/shard_map/run_expert/pallas_call | solution.py:299
  350.0 12.1 %add_convert_fusion = bf16[3072,768]{1,0:T(8,128)(2,1)} fusion(f32[3072,768]{1,0:T(8,128)} %fusion.261, bf16[1280,3072]{1,0:T(8,128)(2,1)} %get-tuple-element.40, bf16[1280,768]{1,0:T(8,128)(2,1)} %get-tuple-element.41), kind=kOutput, calls=%fused_computation.1 | convolution fusion | flops 6044516352 | bytes 23986176 | tf_op jit(solution)/shard_map/dot_general | solution.py:453
  379.7 3.0 fusion.243
  383.8 12.3 %fusion.236 = f32[768,3072]{1,0:T(8,128)} fusion(bf16[1280,3072]{1,0:T(8,128)(2,1)} %get-tuple-element.36, bf16[640,768]{1,0:T(8,128)(2,1)S(1)} %copy-done.27, bf16[640,768]{1,0:T(8,128)(2,1)S(1)} %copy-done.24), kind=kOutput, calls=%fused_computation.332 | convolution fusion | flops 6043729920 | bytes 19267584 | tf_op jit(solution)/shard_map/dot_general | solution.py:452
  403.0 11.9 %add_convert_fusion.1 = bf16[768,3072]{1,0:T(8,128)(2,1)} fusion(f32[768,3072]{1,0:T(8,128)} %fusion.236, bf16[1280,3072]{1,0:T(8,128)(2,1)} %get-tuple-element.37, bf16[640,768]{1,0:T(8,128)(2,1)} %copy-done.18, bf16[640,768]{1,0:T(8,128)(2,1)S(1)} %fusion.85), kind=kOutput, calls=%fused_computation.2 | convolution fusion | flops 6048448512 | bytes 23986176 | tf_op jit(solution)/shard_map/dot_general | solution.py:453
  424.3 3.2 fusion.137
  427.6 15.9 %collective-permute-done.16 = bf16[640,768]{1,0:T(8,128)(2,1)S(1)} collective-permute-done((bf16[640,768]{1,0:T(8,128)(2,1)S(1)}, bf16[640,768]{1,0:T(8,128)(2,1)S(1)}, u32[]{:S(2)}, u32[]{:S(2)}) %collective-permute-start.16) | collective-permute-done | bytes 983072 | tf_op jit(solution)/shard_map/ppermute | solution.py:339
  443.5 21.4 %collective-permute-done.17 = bf16[640,768]{1,0:T(8,128)(2,1)S(1)} collective-permute-done((bf16[640,768]{1,0:T(8,128)(2,1)S(1)}, bf16[640,768]{1,0:T(8,128)(2,1)S(1)}, u32[]{:S(2)}, u32[]{:S(2)}) %collective-permute-start.17) | collective-permute-done | bytes 983072 | tf_op jit(solution)/shard_map/ppermute | solution.py:339
  465.9 10.3 %multiply_reduce_fusion = (bf16[768]{0:T(1024)(128)(2,1)S(1)}, f32[1024]{0:T(1024)S(1)}, f32[1024,768]{0,1:T(8,128)}) fusion(f32[1024,768]{0,1:T(8,128)S(1)} %copy-done.14, f32[1024]{0:T(1024)S(1)} %add_rsqrt_fusion, f32[768]{0:T(1024)S(1)} %get-tuple-element.84, f32[1024,768]{0,1:T(8,128)} %fusion.137, bf16[640,768]{1,0:T(8,128)(2,1)} %copy-done.42, ...), kind=kOutput, calls=%fused_computation.38 | convolution fusion | flops 4055628032 | bytes 16003584 | tf_op jit(solution)/shard_map/dot_general | solution.py:480
  479.0 3.7 convolution_convert_fusion.1.grad_ref
  482.8 31.6 %attend_backward.1 = (bf16[3,1024,768]{2,1,0:T(8,128)(2,1)}, f32[6,8,512]{2,1,0:T(8,128)S(1)}) custom-call(bf16[1024,2304]{1,0:T(8,128)(2,1)} %convolution_convert_fusion.q_ref.k_ref.v_ref, bf16[1024,2304]{1,0:T(8,128)(2,1)} %convolution_convert_fusion.q_ref.k_ref.v_ref, bf16[1024,2304]{1,0:T(8,128)(2,1)} %convolution_convert_fusion.q_ref.k_ref.v_ref, ...), custom_call_target="tpu_custom_call" | custom-call | flops 8053063680 | bytes 12582912 | tf_op jit(solution)/shard_map/attend_backward/pallas_call | solution.py:203
  515.0 3.4 fusion.56
  521.3 4.7 fusion.28
  537.2 7.5 %copy.154 = bf16[768,3200]{1,0:T(8,128)(2,1)} copy(bf16[768,3200]{0,1:T(8,128)(2,1)} %fusion.136) | data formatting | bytes 9830400
  547.6 3.8 fusion.246
  558.4 16.1 %collective-permute-done.13 = bf16[640,768]{1,0:T(8,128)(2,1)} collective-permute-done((bf16[640,768]{1,0:T(8,128)(2,1)}, bf16[640,768]{1,0:T(8,128)(2,1)}, u32[]{:S(2)}, u32[]{:S(2)}) %collective-permute-start.13) | collective-permute-done | bytes 983072 | tf_op jit(solution)/shard_map/ppermute | solution.py:339
  574.5 21.8 %collective-permute-done.14 = bf16[640,768]{1,0:T(8,128)(2,1)} collective-permute-done((bf16[640,768]{1,0:T(8,128)(2,1)}, bf16[640,768]{1,0:T(8,128)(2,1)}, u32[]{:S(2)}, u32[]{:S(2)}) %collective-permute-start.14) | collective-permute-done | bytes 983072 | tf_op jit(solution)/shard_map/ppermute | solution.py:339
  596.4 8.4 %add_convert_fusion.2 = bf16[1024,768]{0,1:T(8,128)(2,1)} fusion(f32[1024,768]{0,1:T(8,128)S(1)} %copy-done.15, bf16[640,768]{1,0:T(8,128)(2,1)} %collective-permute-done.14, bf16[640,768]{1,0:T(8,128)(2,1)} %collective-permute-done.13, bf16[640,768]{1,0:T(8,128)(2,1)} %collective-permute-done.4, bf16[640,768]{1,0:T(8,128)(2,1)} %get-tuple-element.97, ...), kind=kOutput, calls=%fused_computation.42 | convolution fusion | flops 4051697664 | bytes 11272192 | tf_op jit(solution)/shard_map/dot_general | solution.py:480
  617.2 5.0 collective-permute-done.25
  624.3 10.5 %collective-permute-done.22 = bf16[96,3072]{1,0:T(8,128)(2,1)S(1)} collective-permute-done((bf16[96,3072]{1,0:T(8,128)(2,1)}, bf16[96,3072]{1,0:T(8,128)(2,1)S(1)}, u32[]{:S(2)}, u32[]{:S(2)}) %collective-permute-start.22) | collective-permute-done | bytes 589856 | tf_op jit(solution)/shard_map/ppermute | solution.py:339
  642.6 14.0 %reduce-scatter.10.cloned.1.call-done = bf16[96,3200]{1,0:T(8,128)(2,1)} async-done(((bf16[768,3200]{1,0:T(8,128)(2,1)}), bf16[96,3200]{1,0:T(8,128)(2,1)}) %reduce-scatter.10.cloned.1.call-update) | async-done | bytes 614416
  658.1 34.8 %all-reduce.9 = f32[96,3200]{0,1:T(8,128)} all-reduce(bf16[96,3200]{0,1:T(8,128)(2,1)S(1)} %copy.155), channel_id=1, replica_groups=mesh['dp'=4,'shard'=8] {'dp'}, use_global_device_ids=true, to_apply=%region_20.21 | all-reduce | flops 307200 | bytes 1843200 | tf_op jit(solution)/shard_map/psum | solution.py:523
  (313 shorter events, 159.3 us)
Async XLA Ops:
  7.2 85.4 %all-gather.6.cloned.1.call-start = ((), (), s32[]{:S(2)}) async-start(), calls=%async_computation.3 | async-start | bytes 5529600 | tf_op jit(solution)/shard_map/all_gather | solution.py:350
  11.0 194.4 %all-gather.8.cloned.1.call-start = ((), (), s32[]{:S(2)}) async-start(), calls=%async_computation.6 | async-start | bytes 5308416 | tf_op jit(solution)/shard_map/all_gather | solution.py:360
  12.0 241.2 %all-gather.10.cloned.1.call-start = ((), (), s32[]{:S(2)}) async-start(), calls=%async_computation.7 | async-start | bytes 5308416 | tf_op jit(solution)/shard_map/all_gather | solution.py:361
  12.0 35.6 %collective-permute-start.9 = (bf16[1024,768]{1,0:T(8,128)(2,1)}, bf16[1024,768]{1,0:T(8,128)(2,1)}, u32[]{:S(2)}, u32[]{:S(2)}) collective-permute-start(bf16[1024,768]{1,0:T(8,128)(2,1)} %param.25), channel_id=1, source_target_pairs={{0,16},{8,24},{16,0},{24,8},{1,17},{9,25},{17,1},{25,9},{2,18},{10... | collective-permute-start | bytes 4718600 | tf_op jit(solution)/shard_map/ppermute | solution.py:339
  13.3 175.5 %collective-permute-start.2 = (bf16[1024,768]{1,0:T(8,128)(2,1)}, bf16[1024,768]{1,0:T(8,128)(2,1)}, u32[]{:S(2)}, u32[]{:S(2)}) collective-permute-start(bf16[1024,768]{1,0:T(8,128)(2,1)} %param.25), channel_id=1, source_target_pairs={{0,8},{8,0},{16,24},{24,16},{1,9},{9,1},{17,25},{25,17},{2,10},{10... | collective-permute-start | bytes 4718600 | tf_op jit(solution)/shard_map/ppermute | solution.py:339
  16.2 591.1 %reduce-scatter.8.cloned.1.call-start = ((), (), s32[]{:S(2)}) async-start(), calls=%async_computation.5 | async-start | bytes 5308416 | tf_op jit(solution)/shard_map/reduce_scatter | solution.py:459
  47.7 148.0 %collective-permute-start.10 = (bf16[1024,768]{1,0:T(8,128)(2,1)}, bf16[1024,768]{1,0:T(8,128)(2,1)}, u32[]{:S(2)}, u32[]{:S(2)}) collective-permute-start(bf16[1024,768]{1,0:T(8,128)(2,1)} %collective-permute-done.9), channel_id=1, source_target_pairs={{0,8},{8,0},{16,24},{24,16},{1,9},{9,1},{17,25},{25,17},{2,10},{10... | collective-permute-start | bytes 4718600 | tf_op jit(solution)/shard_map/ppermute | solution.py:339
  136.7 63.5 %collective-permute-start.1 = (bf16[1024,768]{0,1:T(8,128)(2,1)}, bf16[1024,768]{0,1:T(8,128)(2,1)}, u32[]{:S(2)}, u32[]{:S(2)}) collective-permute-start(bf16[1024,768]{0,1:T(8,128)(2,1)} %multiply_convert_fusion), channel_id=1, source_target_pairs={{0,8},{8,0},{16,24},{24,16},{1,9},{9,1},{17,25},{25,17},{2,10},{10... | collective-permute-start | bytes 4718600 | tf_op jit(solution)/shard_map/ppermute | solution.py:339
  138.3 153.6 %collective-permute-start.6 = (bf16[1024,768]{0,1:T(8,128)(2,1)}, bf16[1024,768]{0,1:T(8,128)(2,1)}, u32[]{:S(2)}, u32[]{:S(2)}) collective-permute-start(bf16[1024,768]{0,1:T(8,128)(2,1)} %multiply_convert_fusion), channel_id=1, source_target_pairs={{0,16},{8,24},{16,0},{24,8},{1,17},{9,25},{17,1},{25,9},{2,18},{10... | collective-permute-start | bytes 4718600 | tf_op jit(solution)/shard_map/ppermute | solution.py:339
  141.6 6.4 collective-permute-start.3
  148.0 26.7 %collective-permute-start.11 = (f32[1024]{0:T(1024)S(1)}, f32[1024]{0:T(1024)S(1)}, u32[]{:S(2)}, u32[]{:S(2)}) collective-permute-start(f32[1024]{0:T(1024)S(1)} %bitcast.169), channel_id=1, source_target_pairs={{0,16},{8,24},{16,0},{24,8},{1,17},{9,25},{17,1},{25,9},{2,18},{10... | collective-permute-start | bytes 12296 | tf_op jit(solution)/shard_map/ppermute | solution.py:339
  174.7 3.4 collective-permute-start.12
  179.3 2.5 collective-permute-start.5
  181.8 4.2 collective-permute-start.7
  294.7 12.7 %collective-permute-start.8 = (bf16[1024,768]{0,1:T(8,128)(2,1)}, bf16[1024,768]{0,1:T(8,128)(2,1)S(1)}, u32[]{:S(2)}, u32[]{:S(2)}) collective-permute-start(bf16[1024,768]{0,1:T(8,128)(2,1)} %collective-permute-done.6), channel_id=1, source_target_pairs={{0,8},{8,0},{16,24},{24,16},{1,9},{9,1},{17,25},{25,17},{2,10},{10... | collective-permute-start | bytes 4718600 | tf_op jit(solution)/shard_map/ppermute | solution.py:339
  362.1 246.7 %reduce-scatter.6.cloned.1.call-start = ((), (), s32[]{:S(2)}) async-start(), calls=%async_computation.4 | async-start | bytes 5308416 | tf_op jit(solution)/shard_map/reduce_scatter | solution.py:458
  379.6 41.9 %collective-permute-start.18 = (f32[1024]{0:T(1024)S(1)}, f32[1024]{0:T(1024)S(1)}, u32[]{:S(2)}, u32[]{:S(2)}) collective-permute-start(f32[1024]{0:T(1024)S(1)} %fusion.117), channel_id=1, source_target_pairs={{0,8},{8,0},{16,24},{24,16},{1,9},{9,1},{17,25},{25,17},{2,10},{10... | collective-permute-start | bytes 12296 | tf_op jit(solution)/shard_map/ppermute | solution.py:339
  382.7 44.9 %collective-permute-start.15 = (bf16[640,768]{1,0:T(8,128)(2,1)}, bf16[640,768]{1,0:T(8,128)(2,1)}, u32[]{:S(2)}, u32[]{:S(2)}) collective-permute-start(bf16[640,768]{1,0:T(8,128)(2,1)} %get-tuple-element.94), channel_id=1, source_target_pairs={{0,8},{8,0},{16,24},{24,16},{1,9},{9,1},{17,25},{25,17},{2,10},{10... | collective-permute-start | bytes 2949128 | tf_op jit(solution)/shard_map/ppermute | solution.py:339
  415.0 241.6 %reduce-scatter.10.cloned.1.call-start = ((), (), s32[]{:S(2)}) async-start(), calls=%async_computation.8 | async-start | bytes 5529600
  416.0 6.2 collective-permute-start.19
  418.1 4.2 collective-permute-start.20
  420.3 23.2 %collective-permute-start.16 = (bf16[640,768]{1,0:T(8,128)(2,1)S(1)}, bf16[640,768]{1,0:T(8,128)(2,1)S(1)}, u32[]{:S(2)}, u32[]{:S(2)}) collective-permute-start(bf16[640,768]{1,0:T(8,128)(2,1)S(1)} %get-tuple-element.95), channel_id=1, source_target_pairs={{0,16},{8,24},{16,0},{24,8},{1,17},{9,25},{17,1},{25,9},{2,18},{10... | collective-permute-start | bytes 2949128 | tf_op jit(solution)/shard_map/ppermute | solution.py:339
  421.6 43.3 %collective-permute-start.17 = (bf16[640,768]{1,0:T(8,128)(2,1)S(1)}, bf16[640,768]{1,0:T(8,128)(2,1)S(1)}, u32[]{:S(2)}, u32[]{:S(2)}) collective-permute-start(bf16[640,768]{1,0:T(8,128)(2,1)S(1)} %get-tuple-element.96), channel_id=1, source_target_pairs={{0,24},{8,16},{16,8},{24,0},{1,25},{9,17},{17,9},{25,1},{2,26},{10... | collective-permute-start | bytes 2949128 | tf_op jit(solution)/shard_map/ppermute | solution.py:339
  547.6 10.8 %collective-permute-start.4 = (bf16[640,768]{1,0:T(8,128)(2,1)}, bf16[640,768]{1,0:T(8,128)(2,1)}, u32[]{:S(2)}, u32[]{:S(2)}) collective-permute-start(bf16[640,768]{1,0:T(8,128)(2,1)} %get-tuple-element.98), channel_id=1, source_target_pairs={{0,8},{8,0},{16,24},{24,16},{1,9},{9,1},{17,25},{25,17},{2,10},{10... | collective-permute-start | bytes 2949128 | tf_op jit(solution)/shard_map/ppermute | solution.py:339
  551.4 23.1 %collective-permute-start.13 = (bf16[640,768]{1,0:T(8,128)(2,1)}, bf16[640,768]{1,0:T(8,128)(2,1)}, u32[]{:S(2)}, u32[]{:S(2)}) collective-permute-start(bf16[640,768]{1,0:T(8,128)(2,1)} %get-tuple-element.99), channel_id=1, source_target_pairs={{0,16},{8,24},{16,0},{24,8},{1,17},{9,25},{17,1},{25,9},{2,18},{10... | collective-permute-start | bytes 2949128 | tf_op jit(solution)/shard_map/ppermute | solution.py:339
  552.6 43.8 %collective-permute-start.14 = (bf16[640,768]{1,0:T(8,128)(2,1)}, bf16[640,768]{1,0:T(8,128)(2,1)}, u32[]{:S(2)}, u32[]{:S(2)}) collective-permute-start(bf16[640,768]{1,0:T(8,128)(2,1)} %get-tuple-element.100), channel_id=1, source_target_pairs={{0,24},{8,16},{16,8},{24,0},{1,25},{9,17},{17,9},{25,1},{2,26},{10... | collective-permute-start | bytes 2949128 | tf_op jit(solution)/shard_map/ppermute | solution.py:339
  607.4 30.9 %collective-permute-start.24 = (bf16[384,768]{1,0:T(8,128)(2,1)}, bf16[384,768]{1,0:T(8,128)(2,1)S(1)}, u32[]{:S(2)}, u32[]{:S(2)}) collective-permute-start(bf16[384,768]{1,0:T(8,128)(2,1)} %reduce-scatter.8.cloned.1.call-done), channel_id=1, source_target_pairs={{0,8},{8,0},{16,24},{24,16},{1,9},{9,1},{17,25},{25,17},{2,10},{10... | collective-permute-start | bytes 1769480 | tf_op jit(solution)/shard_map/ppermute | solution.py:339
  607.4 14.8 %collective-permute-start.25 = (bf16[384,768]{1,0:T(8,128)(2,1)}, bf16[384,768]{1,0:T(8,128)(2,1)S(1)}, u32[]{:S(2)}, u32[]{:S(2)}) collective-permute-start(bf16[384,768]{1,0:T(8,128)(2,1)} %reduce-scatter.8.cloned.1.call-done), channel_id=1, source_target_pairs={{0,16},{8,24},{16,0},{24,8},{1,17},{9,25},{17,1},{25,9},{2,18},{10... | collective-permute-start | bytes 1769480 | tf_op jit(solution)/shard_map/ppermute | solution.py:339
  608.8 27.2 %collective-permute-start.21 = (bf16[96,3072]{1,0:T(8,128)(2,1)}, bf16[96,3072]{1,0:T(8,128)(2,1)S(1)}, u32[]{:S(2)}, u32[]{:S(2)}) collective-permute-start(bf16[96,3072]{1,0:T(8,128)(2,1)} %reduce-scatter.6.cloned.1.call-done), channel_id=1, source_target_pairs={{0,8},{8,0},{16,24},{24,16},{1,9},{9,1},{17,25},{25,17},{2,10},{10... | collective-permute-start | bytes 1769480 | tf_op jit(solution)/shard_map/ppermute | solution.py:339
  609.5 25.2 %collective-permute-start.22 = (bf16[96,3072]{1,0:T(8,128)(2,1)}, bf16[96,3072]{1,0:T(8,128)(2,1)S(1)}, u32[]{:S(2)}, u32[]{:S(2)}) collective-permute-start(bf16[96,3072]{1,0:T(8,128)(2,1)} %reduce-scatter.6.cloned.1.call-done), channel_id=1, source_target_pairs={{0,16},{8,24},{16,0},{24,8},{1,17},{9,25},{17,1},{25,9},{2,18},{10... | collective-permute-start | bytes 1769480 | tf_op jit(solution)/shard_map/ppermute | solution.py:339
  622.2 18.2 %collective-permute-start.26 = (bf16[384,768]{1,0:T(8,128)(2,1)S(1)}, bf16[384,768]{1,0:T(8,128)(2,1)S(1)}, u32[]{:S(2)}, u32[]{:S(2)}) collective-permute-start(bf16[384,768]{1,0:T(8,128)(2,1)S(1)} %collective-permute-done.25), channel_id=1, source_target_pairs={{0,8},{8,0},{16,24},{24,16},{1,9},{9,1},{17,25},{25,17},{2,10},{10... | collective-permute-start | bytes 1769480 | tf_op jit(solution)/shard_map/ppermute | solution.py:339
  634.7 6.8 collective-permute-start.23
  (50 other events, 914.8 us)
Sparse Core Ops, SparseCore 0:
  11.1 81.4 all-gather.5
  94.8 78.0 all-gather.7
  175.1 78.0 all-gather.9
  362.2 93.9 reduce-scatter.7
  459.7 94.9 reduce-scatter.5
  558.2 98.3 reduce-scatter.9

commit v2 on v1

--- a/solution.py
+++ b/solution.py
@@ -15,11 +15,13 @@
 BUCKETS = 32
 SEQ = 1024
 CAP = 640
+DEEP = 4
 BLOCK = 256
 REACH = 768
 NORM_EPSILON = 1e-06
 HIGHEST = lax.Precision.HIGHEST
 NEG = -1e30
+COST_CUT = 256
 F32 = jnp.float32
 BF16 = jnp.bfloat16
 MIB = 1024 * 1024
@@ -33,13 +35,8 @@
     return unit_rows, inv_rms, unit_rows * gain_vec
 
 
-def norm_backward(grad_norm, unit_rows, inv_rms, gain_vec):
-    grad_unit = grad_norm * gain_vec
-    grad_gain = jnp.sum(grad_norm * unit_rows, axis=0)
-    grad_input = inv_rms * (
-        grad_unit - unit_rows * jnp.mean(grad_unit * unit_rows, axis=-1, keepdims=True)
-    )
-    return grad_input, grad_gain
+def cost(flops, moved):
+    return pl.CostEstimate(flops=flops // COST_CUT, bytes_accessed=moved // COST_CUT, transcendentals=0)
 
 
 def key_span(block):
@@ -192,9 +189,7 @@
         ],
         scratch_shapes=PAIR_SCRATCH,
         compiler_params=pltpu.CompilerParams(vmem_limit_bytes=48 * MIB),
-        cost_estimate=pl.CostEstimate(
-            flops=4 * SEQ * SEQ * D, bytes_accessed=8 * SEQ * D, transcendentals=0
-        ),
+        cost_estimate=cost(4 * SEQ * SEQ * D, 8 * SEQ * D),
         name="attend_forward",
     )(qkv_rows, qkv_rows, qkv_rows, seg_col, seg_row, lines)
 
@@ -220,9 +215,7 @@
             pltpu.VMEM((SEQ, 2 * HEAD_DIM), F32),
         ],
         compiler_params=pltpu.CompilerParams(vmem_limit_bytes=48 * MIB),
-        cost_estimate=pl.CostEstimate(
-            flops=10 * SEQ * SEQ * D, bytes_accessed=16 * SEQ * D, transcendentals=0
-        ),
+        cost_estimate=cost(10 * SEQ * SEQ * D, 16 * SEQ * D),
         name="attend_backward",
     )(qkv_rows, qkv_rows, qkv_rows, attended, grad_attended, totals, seg_col, seg_row, lines)
 
@@ -249,18 +242,12 @@
     return total[:, BLOCK:]
 
 
+FF_HALF = FF // 2
 FF_BLOCK = 512
-
-
-def expert_kernel(
-    rows_ref, grad_ref, gate_ref, w_in_ref, w_out_ref,
-    act_ref, dhid_ref, dout_ref, out_ref, drow_ref, dgate_ref, out_acc, drow_acc,
-):
-    gates = gate_ref[...]
-    dout_ref[...] = (gates * grad_ref[...].astype(F32)).astype(BF16)
-    out_acc[...] = jnp.zeros_like(out_acc)
-    drow_acc[...] = jnp.zeros_like(drow_acc)
-
+SLOTS = EXPERTS * CAP
+
+
+def hidden_half(rows_ref, dout_ref, w_in_ref, w_out_ref, act_ref, dhid_ref, out_acc, drow_acc):
     def step(index, carry):
         cols = pl.ds(pl.multiple_of(index * FF_BLOCK, FF_BLOCK), FF_BLOCK)
         w_in = w_in_ref[:, cols]
@@ -281,48 +268,286 @@
         drow_acc[...] += dot_nt(dhid, w_in)
         return carry
 
-    lax.fori_loop(0, FF // FF_BLOCK, step, 0)
+    lax.fori_loop(0, FF_HALF // FF_BLOCK, step, 0)
+
+
+def route_gates(logits, hits):
+    shifted = jnp.exp(logits - jnp.max(logits, axis=0, keepdims=True))
+    prob_all = shifted / jnp.sum(shifted, axis=0, keepdims=True)
+    chosen_sum = jnp.sum(hits * prob_all, axis=0, keepdims=True)
+    return prob_all, chosen_sum, hits * prob_all / chosen_sum
+
+
+def pick_slots(key_row):
+    slot = lax.broadcasted_iota(jnp.int32, (CAP, SEQ), 0).astype(F32)
+    return key_row == slot
+
+
+def first_half_kernel(
+    act_one_ref, act_two_ref, cot_one_ref, cot_two_ref, key_ref, router_ref, mine_ref, w_in_ref, w_out_ref, *rest
+):
+    rows_ref, graw_ref, dout_ref, gcol_ref, act_ref, dhid_ref, out_acc, drow_acc = rest[-8:]
+
+    def dispatch(index, act_part, cot_part):
+        keys = key_ref[index * EXPERTS : (index + 1) * EXPERTS, :]
+        logits = dot_nt(router_ref[...], act_part[...])[:EXPERTS, :]
+        _, _, gate_rows = route_gates(logits, jnp.where(keys >= 0.0, 1.0, 0.0))
+        mine = mine_ref[...] > 0.0
+        picks = pick_slots(jnp.sum(jnp.where(mine, keys, 0.0), axis=0, keepdims=True))
+        gate_row = jnp.sum(jnp.where(mine, gate_rows, 0.0), axis=0, keepdims=True)
+        gates = jnp.sum(jnp.where(picks, gate_row, 0.0), axis=1, keepdims=True)
+        chosen = jnp.where(picks, 1.0, 0.0).astype(BF16)
+        rows_ref[...] = dot_nn(chosen, act_part[...]).astype(BF16)
+        grads = dot_nn(chosen, cot_part[...])
+        graw_ref[...] = grads.astype(BF16)
+        dout_ref[...] = (gates * grads).astype(BF16)
+        gcol_ref[...] = gates
+
+    @pl.when(pl.program_id(0) == 0)
+    def _():
+        dispatch(0, act_one_ref, cot_one_ref)
+
+    @pl.when(pl.program_id(0) == 1)
+    def _():
+        dispatch(1, act_two_ref, cot_two_ref)
+
+    out_acc[...] = jnp.zeros_like(out_acc)
+    drow_acc[...] = jnp.zeros_like(drow_acc)
+    hidden_half(rows_ref, dout_ref, w_in_ref, w_out_ref, act_ref, dhid_ref, out_acc, drow_acc)
+
+
+def second_half_kernel(
+    rows_ref, graw_ref, dout_ref, gcol_ref, out_in, drow_in, key_ref, w_in_ref, w_out_ref, *rest
+):
+    act_ref, dhid_ref, out_ref, drow_ref, dgate_ref, out_acc, drow_acc = rest[-7:]
+    out_acc[...] = out_in[...]
+    drow_acc[...] = drow_in[...]
+    hidden_half(rows_ref, dout_ref, w_in_ref, w_out_ref, act_ref, dhid_ref, out_acc, drow_acc)
     outs = out_acc[...]
-    out_ref[...] = (gates * outs).astype(BF16)
+    out_ref[...] = (gcol_ref[...] * outs).astype(BF16)
     drow_ref[...] = drow_acc[...].astype(BF16)
-    dgate_ref[...] = jnp.sum(grad_ref[...].astype(F32) * outs, axis=1, keepdims=True)
-
-
-def run_expert(rows, grads, gates, w_in, w_out):
-    count = rows.shape[0] // CAP
-    row_spec = pl.BlockSpec((CAP, D), lambda part: (part, 0))
-    wide_spec = pl.BlockSpec((CAP, FF), lambda part: (part, 0))
-    gate_spec = pl.BlockSpec((CAP, 1), lambda part: (part, 0))
-    once = pl.Buffered(1)
-    narrow = jax.ShapeDtypeStruct((count * CAP, D), BF16)
-    wide = jax.ShapeDtypeStruct((count * CAP, FF), BF16)
+    dgates = jnp.sum(graw_ref[...].astype(F32) * outs, axis=1, keepdims=True)
+    for index in range(2):
+
+        @pl.when(pl.program_id(0) == index)
+        def _():
+            picks = pick_slots(key_ref[index : index + 1, :])
+            dgate_ref[index : index + 1, :] = jnp.sum(jnp.where(picks, dgates, 0.0), axis=0, keepdims=True)
+
+
+ANY_SPEC = pl.BlockSpec(memory_space=pl.ANY)
+
+
+def place_kernel(order_ref, *refs):
+    out_ref = refs[-1]
+    for index, block in enumerate(refs[:-1]):
+        out_ref[order_ref[index]] = block[...]
+
+
+def place_blocks(order, blocks):
+    shape = blocks[0].shape
+    vmem = pl.BlockSpec(memory_space=pltpu.VMEM)
     return pl.pallas_call(
-        expert_kernel,
-        grid=(count,),
+        place_kernel,
+        in_specs=[pl.BlockSpec(memory_space=pltpu.SMEM)] + [vmem] * len(blocks),
+        out_specs=vmem,
+        out_shape=jax.ShapeDtypeStruct((len(blocks),) + shape, blocks[0].dtype),
+        compiler_params=pltpu.CompilerParams(vmem_limit_bytes=32 * MIB),
+        cost_estimate=cost(0, 4 * len(blocks) * shape[0] * shape[1]),
+        name="place_blocks",
+    )(order, *blocks)
+
+
+ROW_BLOCK = 256
+
+
+def picked_sum(key_ref, parts):
+    slot = lax.broadcasted_iota(jnp.int32, (ROW_BLOCK, CAP), 1).astype(F32)
+    total = None
+    for index, part in enumerate(parts):
+        picks = jnp.where(key_ref[:, index : index + 1] == slot, 1.0, 0.0).astype(BF16)
+        rows = dot_nn(picks, part[...])
+        total = rows if total is None else total + rows
+    return total
+
+
+def mix_kernel(key_ref, base_ref, one_ref, two_ref, three_ref, four_ref, out_ref):
+    total = picked_sum(key_ref, (one_ref, two_ref, three_ref, four_ref))
+    out_ref[...] = (base_ref[...] + total).astype(BF16)
+
+
+def row_spec(width):
+    return pl.BlockSpec((ROW_BLOCK, width), lambda step: (step, 0))
+
+
+def mix_rows(keys, base, parts):
+    return pl.pallas_call(
+        mix_kernel,
+        grid=(SEQ // ROW_BLOCK,),
+        in_specs=[row_spec(EXPERTS), row_spec(D)] + [fixed_spec((CAP, D))] * EXPERTS,
+        out_specs=row_spec(D),
+        out_shape=jax.ShapeDtypeStruct((SEQ, D), BF16),
+        compiler_params=pltpu.CompilerParams(vmem_limit_bytes=32 * MIB),
+        cost_estimate=cost(2 * SEQ * SLOTS * D, 2 * SLOTS * D + 6 * SEQ * D),
+        name="mix_rows",
+    )(keys, base, *parts)
+
+
+def norm_back(values, grad_norm, gain):
+    inv_rms = lax.rsqrt(jnp.mean(values * values, axis=-1, keepdims=True) + NORM_EPSILON)
+    unit_rows = values * inv_rms
+    grad_gain = jnp.sum(grad_norm * unit_rows, axis=0, keepdims=True)
+    grad_unit = grad_norm * gain
+    middle = jnp.mean(grad_unit * unit_rows, axis=-1, keepdims=True)
+    return inv_rms * (grad_unit - unit_rows * middle), grad_gain
+
+
+def token_back_kernel(
+    key_ref, extra_ref, residual_ref, cot_ref, attended_ref, gain_ref, weight_ref,
+    one_ref, two_ref, three_ref, four_ref,
+    grad_ref, dattended_ref, dweight_ref, dgain_ref, dweight_acc,
+):
+    step = pl.program_id(0)
+
+    @pl.when(step == 0)
+    def _():
+        dweight_acc[...] = jnp.zeros_like(dweight_acc)
+        dgain_ref[...] = jnp.zeros_like(dgain_ref)
+
+    grad_act = extra_ref[...] + picked_sum(key_ref, (one_ref, two_ref, three_ref, four_ref))
+    grad_norm, grad_gain = norm_back(residual_ref[...], grad_act, gain_ref[...])
+    grad_rows = cot_ref[...].astype(F32) + grad_norm
+    grad_ref[...] = grad_rows
+    dgain_ref[...] += grad_gain
+    branch = grad_rows.astype(BF16)
+    dattended_ref[...] = dot_nt(branch, weight_ref[...]).astype(BF16)
+    dweight_acc[...] += lax.dot_general(
+        attended_ref[...], branch, (((0,), (0,)), ((), ())), preferred_element_type=F32
+    )
+
+    @pl.when(step == SEQ // ROW_BLOCK - 1)
+    def _():
+        dweight_ref[...] = dweight_acc[...].astype(BF16)
+
+
+def token_back(keys, extra, residual, cotangent, attended, gain, packed, parts):
+    return pl.pallas_call(
+        token_back_kernel,
+        grid=(SEQ // ROW_BLOCK,),
+        in_specs=[row_spec(EXPERTS), row_spec(D), row_spec(D), row_spec(D), row_spec(D)]
+        + [fixed_spec((1, D)), pl.BlockSpec((D, D), lambda step: (0, 3), pipeline_mode=pl.Buffered(1))]
+        + [fixed_spec((CAP, D))] * EXPERTS,
+        out_specs=[row_spec(D), row_spec(D), fixed_spec((D, D)), fixed_spec((1, D))],
+        out_shape=[
+            jax.ShapeDtypeStruct((SEQ, D), F32),
+            jax.ShapeDtypeStruct((SEQ, D), BF16),
+            jax.ShapeDtypeStruct((D, D), BF16),
+            jax.ShapeDtypeStruct((1, D), F32),
+        ],
+        scratch_shapes=[pltpu.VMEM((D, D), F32)],
+        compiler_params=pltpu.CompilerParams(vmem_limit_bytes=40 * MIB),
+        cost_estimate=cost(2 * SEQ * (SLOTS + 2 * D) * D, 2 * SLOTS * D + 18 * SEQ * D),
+        name="token_back",
+    )(keys, extra, residual, cotangent, attended, gain, packed, *parts)
+
+
+def qkv_back_kernel(
+    act_ref, split_ref, weight_ref, token_ref, gain_ref, grad_ref,
+    dweight_ref, dtoken_ref, dgain_ref, act_t, total,
+):
+    step = pl.program_id(0)
+
+    @pl.when(step == 0)
+    def _():
+        act_t[...] = act_ref[...].T
+        total[...] = jnp.zeros_like(total)
+
+    split = split_ref[0]
+    dweight_ref[...] = dot_nn(act_t[...], split).astype(BF16)
+    total[...] += dot_nt(split, weight_ref[...])
+
+    @pl.when(step == 2)
+    def _():
+        grad_norm, grad_gain = norm_back(token_ref[...].astype(F32), total[...], gain_ref[...])
+        dtoken_ref[...] = (grad_ref[...] + grad_norm).astype(BF16)
+        dgain_ref[...] = grad_gain
+
+
+def qkv_back(act_one, grad_split, packed, tokens, gain, grad_residual):
+    return pl.pallas_call(
+        qkv_back_kernel,
+        grid=(3,),
         in_specs=[
-            row_spec,
-            row_spec,
-            gate_spec,
-            pl.BlockSpec((D, FF), lambda part: (0, 0), pipeline_mode=once),
-            pl.BlockSpec((FF, D), lambda part: (0, 0), pipeline_mode=once),
+            fixed_spec((SEQ, D)),
+            pl.BlockSpec((1, SEQ, D), lambda step: (step, 0, 0)),
+            pl.BlockSpec((D, D), lambda step: (0, step)),
+            fixed_spec((SEQ, D)),
+            fixed_spec((1, D)),
+            fixed_spec((SEQ, D)),
         ],
-        out_specs=[wide_spec, wide_spec, row_spec, row_spec, row_spec, gate_spec],
-        out_shape=[wide, wide, narrow, narrow, narrow, jax.ShapeDtypeStruct((count * CAP, 1), F32)],
+        out_specs=[pl.BlockSpec((D, D), lambda step: (0, step)), fixed_spec((SEQ, D)), fixed_spec((1, D))],
+        out_shape=[
+            jax.ShapeDtypeStruct((D, 3 * D), BF16),
+            jax.ShapeDtypeStruct((SEQ, D), BF16),
+            jax.ShapeDtypeStruct((1, D), F32),
+        ],
+        scratch_shapes=[pltpu.VMEM((D, SEQ), BF16), pltpu.VMEM((SEQ, D), F32)],
+        compiler_params=pltpu.CompilerParams(vmem_limit_bytes=48 * MIB),
+        cost_estimate=cost(12 * SEQ * D * D, 16 * SEQ * D + 12 * D * D),
+        name="qkv_back",
+    )(act_one, grad_split, packed, tokens, gain, grad_residual)
+
+
+def slot_spec(pair, width):
+    return pl.BlockSpec((CAP, width), lambda step: (2 * pair + step, 0))
+
+
+def fixed_spec(shape, row=0):
+    return pl.BlockSpec(shape, lambda step: (row, 0), pipeline_mode=pl.Buffered(1))
+
+
+def expert_cost():
+    return cost(16 * CAP * D * FF_HALF, 4 * D * FF_HALF + 20 * CAP * D)
+
+
+def expert_first(pair, acts, cots, keys, router_rows, mine, w_in, w_out, earlier):
+    widths = [(D, BF16), (D, BF16), (D, BF16), (1, F32), (FF_HALF, BF16), (FF_HALF, BF16), (D, F32), (D, F32)]
+    inputs = [acts[0], acts[1], cots[0], cots[1], keys, router_rows, mine, w_in, w_out]
+    return pl.pallas_call(
+        first_half_kernel,
+        grid=(2,),
+        in_specs=[fixed_spec((SEQ, D))] * 4
+        + [fixed_spec((2 * EXPERTS, SEQ)), fixed_spec((2 * EXPERTS, D)), fixed_spec((EXPERTS, 1))]
+        + [fixed_spec((D, FF_HALF)), fixed_spec((FF_HALF, D))]
+        + [ANY_SPEC] * len(earlier),
+        out_specs=[slot_spec(pair, width) for width, _ in widths],
+        out_shape=[jax.ShapeDtypeStruct((SLOTS, width), kind) for width, kind in widths],
+        input_output_aliases={len(inputs) + i: i for i in range(len(earlier))},
+        compiler_params=pltpu.CompilerParams(vmem_limit_bytes=56 * MIB),
+        cost_estimate=expert_cost(),
+        name="expert_first",
+    )(*inputs, *earlier)
+
+
+def expert_second(pair, first, keys, w_in, w_out, earlier):
+    rows, graw, dout, gcol, _, _, outs, drows = first
+    wide = jax.ShapeDtypeStruct((SLOTS, FF_HALF), BF16)
+    narrow = jax.ShapeDtypeStruct((2 * CAP, D), BF16)
+    inputs = [rows, graw, dout, gcol, outs, drows, keys, w_in, w_out]
+    return pl.pallas_call(
+        second_half_kernel,
+        grid=(2,),
+        in_specs=[slot_spec(pair, width) for width in (D, D, D, 1, D, D)]
+        + [fixed_spec((2, SEQ)), fixed_spec((D, FF_HALF)), fixed_spec((FF_HALF, D), 1)]
+        + [ANY_SPEC] * len(earlier),
+        out_specs=[slot_spec(pair, FF_HALF)] * 2 + [slot_spec(0, D)] * 2 + [fixed_spec((8, SEQ))],
+        out_shape=[wide, wide, narrow, narrow, jax.ShapeDtypeStruct((8, SEQ), F32)],
+        input_output_aliases={len(inputs) + i: i for i in range(len(earlier))},
         scratch_shapes=[pltpu.VMEM((CAP, D), F32), pltpu.VMEM((CAP, D), F32)],
         compiler_params=pltpu.CompilerParams(vmem_limit_bytes=56 * MIB),
-        cost_estimate=pl.CostEstimate(
-            flops=8 * count * CAP * D * FF, bytes_accessed=4 * D * FF + 4 * count * CAP * FF, transcendentals=0
-        ),
-        name="run_expert",
-    )(rows, grads, gates, w_in, w_out)
-
-
-def split_three(values):
-    first = values.astype(BF16)
-    rest = values - first.astype(F32)
-    second = rest.astype(BF16)
-    third = (rest - second.astype(F32)).astype(BF16)
-    return jnp.stack([first, second, third], axis=-1)
+        cost_estimate=expert_cost(),
+        name="expert_second",
+    )(*inputs, *earlier)
 
 
 def body(
@@ -338,6 +563,52 @@
             return value
         return lax.ppermute(value, "dp", [(i, i ^ relation) for i in range(dp_size)])
 
+    across_x = (D // shard_rows) // DEEP
+    shard_id = lax.axis_index("shard")
+    my_z, my_x = shard_id // across_x, shard_id % across_x
+
+    def step_z(value, step):
+        pairs = [
+            (z * across_x + x, (z + step) % DEEP * across_x + x) for z in range(DEEP) for x in range(across_x)
+        ]
+        return lax.ppermute(value, "shard", pairs)
+
+    def step_x(value, step):
+        pairs = [
+            (z * across_x + x, z * across_x + (x + step) % across_x) for z in range(DEEP) for x in range(across_x)
+        ]
+        return lax.ppermute(value, "shard", pairs)
+
+    def gather_rows(value):
+        pieces = {}
+        for back in range(DEEP):
+            pieces[back, 0] = value if back == 0 else step_z(value, back)
+            for side in range(1, across_x):
+                pieces[back, side] = step_x(pieces[back, 0], side)
+        order, blocks = [], []
+        for (back, side), block in pieces.items():
+            order.append((my_z - back) % DEEP * across_x + (my_x - side) % across_x)
+            blocks.append(block)
+        return place_blocks(jnp.stack(order).astype(jnp.int32), blocks)
+
+    def sum_over_x(value):
+        value = value.reshape(DEEP, across_x, -1, value.shape[-1])
+        total = lax.dynamic_index_in_dim(value, my_x, 1, keepdims=False).astype(F32)
+        for step in range(1, across_x):
+            sent = lax.dynamic_index_in_dim(value, (my_x + step) % across_x, 1, keepdims=False)
+            total = total + step_x(sent, step).astype(F32)
+        return total.astype(BF16)
+
+    def sum_over_z(value):
+        total = lax.dynamic_index_in_dim(value, my_z, 0, keepdims=False).astype(F32)
+        for step in range(1, DEEP):
+            sent = lax.dynamic_index_in_dim(value, (my_z + step) % DEEP, 0, keepdims=False)
+            total = total + step_z(sent, step).astype(F32)
+        return total
+
+    def after(values, earlier):
+        return lax.optimization_barrier((values, earlier))[0]
+
     def spread(value):
         across = swap(value, 2)
         return [value, swap(value, 1), across, swap(across, 1)]
@@ -347,7 +618,14 @@
         [norm1_gain[:, None], norm2_gain[:, None], router, table_col[:, None]], axis=1
     )
     packed = jnp.concatenate([w_qkv, w_attn_out, jnp.pad(small, ((0, 0), (0, 121)))], axis=1)
-    packed = lax.all_gather(packed, "shard", axis=0, tiled=True)
+    core = lax.axis_index("dp") % 2
+    core_rows = shard_rows // 2
+    mine = lax.dynamic_slice_in_dim(packed, core * core_rows, core_rows, 0)
+    mine = gather_rows(mine)
+    other = swap(mine, 1)
+    first_rows = jnp.where(core == 0, mine, other)[:, None]
+    last_rows = jnp.where(core == 0, other, mine)[:, None]
+    packed = jnp.concatenate([first_rows, last_rows], axis=1).reshape(D, mine.shape[2])
     qkv_weight = packed[:, : 3 * D]
     attn_weight = packed[:, 3 * D : 4 * D]
     gain_one = packed[:, 4 * D].astype(F32)
@@ -357,8 +635,9 @@
 
     my_in = lax.dynamic_index_in_dim(w_in, me, 0, keepdims=False)
     my_out = lax.dynamic_index_in_dim(w_expert_out, me, 0, keepdims=False)
-    full_in = lax.all_gather(my_in, "shard", axis=0, tiled=True)
+    half_in = [lax.all_gather(my_in[:, :FF_HALF], "shard", axis=0, tiled=True)]
     full_out = lax.all_gather(my_out, "shard", axis=0, tiled=True)
+    half_in.append(lax.all_gather(my_in[:, FF_HALF:], "shard", axis=0, tiled=True))
 
     cot_parts = spread(cotangent)
 
@@ -375,17 +654,11 @@
     def related(rows):
         return [lax.dynamic_index_in_dim(rows, relation_ids[x], 0, keepdims=False) for x in range(EXPERTS)]
 
-    slot_ids = jnp.arange(CAP, dtype=F32)
-
-    def pick_matrix(key_row):
-        return (key_row[None, :] == slot_ids[:, None]).astype(BF16)
-
     my_keys = related(keys)
-    their_picks = [pick_matrix(swap(my_keys[x], x)) for x in range(EXPERTS)]
-    my_picks = jnp.concatenate([pick_matrix(my_keys[x]) for x in range(EXPERTS)], axis=0)
-    grad_slots = [
-        jnp.dot(their_picks[x], cot_parts[x], preferred_element_type=F32).astype(BF16) for x in range(EXPERTS)
-    ]
+    all_keys = spread(keys)
+    their_keys = [lax.dynamic_index_in_dim(rows, me, 0, keepdims=False) for rows in all_keys]
+    mine_col = (expert_ids == me).astype(F32)[:, None]
+    key_cols = jnp.stack(my_keys, axis=1)
 
     bucket_hits = (jnp.arange(BUCKETS, dtype=jnp.int32)[:, None] == buckets[None, :]).astype(BF16)
     bias_vec = lax.dot_general(bias_full, bucket_hits, (((0,), (0,)), ((), ())), preferred_element_type=F32)
@@ -403,109 +676,75 @@
     act_parts = spread(act_two)
 
     logits = lax.dot_general(router_weight, act_two, (((0,), (1,)), ((), ())), preferred_element_type=F32)
-    shifted = jnp.exp(logits - jnp.max(logits, axis=0, keepdims=True))
-    prob_all = shifted / jnp.sum(shifted, axis=0, keepdims=True)
-    chosen_sum = jnp.sum(hits * prob_all, axis=0, keepdims=True)
-    gates = hits * prob_all / chosen_sum
-    my_gates = related(gates)
-    their_gates = [swap(my_gates[x], x) for x in range(EXPERTS)]
-
-    def dispatch(relations):
-        rows = jnp.concatenate(
-            [jnp.dot(their_picks[x], act_parts[x], preferred_element_type=F32).astype(BF16) for x in relations], axis=0
+    prob_all, chosen_sum, gates = route_gates(logits, hits)
+
+    key_pairs = [jnp.stack(their_keys[:2]), jnp.stack(their_keys[2:])]
+    all_pairs = [jnp.concatenate(all_keys[:2], axis=0), jnp.concatenate(all_keys[2:], axis=0)]
+    router_rows = jnp.pad(router_weight.T, ((0, EXPERTS), (0, 0)))
+    first = []
+    for pair in range(2):
+        here = slice(2 * pair, 2 * pair + 2)
+        first = expert_first(
+            pair, act_parts[here], cot_parts[here], all_pairs[pair], router_rows, mine_col, half_in[0], full_out, first
         )
-        gate_col = jnp.concatenate(
-            [
-                jnp.sum(
-                    jnp.dot(their_picks[x], split_three(their_gates[x]), preferred_element_type=F32),
-                    axis=1,
-                    keepdims=True,
-                )
-                for x in relations
-            ],
-            axis=0,
-        )
-        return rows, gate_col
-
-    halves = []
-    for relations in ((0, 1), (2, 3)):
-        rows, gate_col = dispatch(relations)
-        grads = jnp.concatenate([grad_slots[x] for x in relations], axis=0)
-        halves.append((rows,) + tuple(run_expert(rows, grads, gate_col, full_in, full_out)))
-
-    def back_to_tokens(picks, dgate_rows):
-        parts = split_three(dgate_rows[:, 0])
-        return jnp.sum(
-            lax.dot_general(parts, picks, (((0,), (0,)), ((), ())), preferred_element_type=F32), axis=0
-        )
-
-    out_parts, drow_parts, dgate_parts = [], [], []
-    for half, relations in zip(halves, ((0, 1), (2, 3))):
-        _, _, _, _, outs, drows, dgates = half
-        for index, x in enumerate(relations):
-            part = slice(index * CAP, (index + 1) * CAP)
-            drow_parts.append(swap(drows[part], x))
-            out_parts.append(swap(outs[part], x))
-            dgate_parts.append(swap(back_to_tokens(their_picks[x], dgates[part]), x))
+    rows, _, dout, _, act_first, dhid_first, _, _ = first
 
     def weight_grad(left, right):
-        total = lax.dot_general(left[0], right[0], (((0,), (0,)), ((), ())), preferred_element_type=F32)
-        total += lax.dot_general(left[1], right[1], (((0,), (0,)), ((), ())), preferred_element_type=F32)
-        return total.astype(BF16)
-
-    grad_in = weight_grad([h[0] for h in halves], [h[2] for h in halves])
-    grad_out = weight_grad([h[1] for h in halves], [h[3] for h in halves])
-    grad_in = lax.psum_scatter(grad_in, "shard", scatter_dimension=0, tiled=True)
-    grad_out = lax.psum_scatter(grad_out, "shard", scatter_dimension=0, tiled=True)
-
-    def over_groups(value):
-        total = value.astype(F32)
-        for group in range(1, dp_size // EXPERTS):
-            moved = lax.ppermute(value, "dp", [(i, (i + EXPERTS * group) % dp_size) for i in range(dp_size)])
-            total = total + moved.astype(F32)
-        return total.astype(BF16)
-
-    def place(value):
-        parts = spread(over_groups(value))
-        out = jnp.zeros((EXPERTS,) + value.shape, F32)
+        return lax.dot_general(left, right, (((0,), (0,)), ((), ())), preferred_element_type=F32).astype(BF16)
+
+    grad_in_first = weight_grad(rows, dhid_first)
+    sum_in_first = lax.psum_scatter(grad_in_first, "shard", scatter_dimension=0, tiled=True)
+    far = expert_second(1, first, after(key_pairs[1], grad_in_first), half_in[1], full_out, [])
+    near = expert_second(0, first, key_pairs[0], half_in[1], full_out, far[:2])
+    act_second, dhid_second = near[:2]
+    dgate_parts = [swap(row, x) for x, row in enumerate([near[4][0], near[4][1], far[4][0], far[4][1]])]
+    across_one = swap(far[3][:CAP], 2)
+    across_two = swap(far[3][CAP:], 2)
+
+    act_first, act_second = after((act_first, act_second), across_one)
+    grad_out = jnp.concatenate([weight_grad(act_first, dout), weight_grad(act_second, dout)], axis=0)
+    sum_out = lax.psum_scatter(grad_out, "shard", scatter_dimension=0, tiled=True)
+    grad_in_second = weight_grad(rows, after(dhid_second, (grad_out, across_two, sum_in_first)))
+    sum_in_second = lax.psum_scatter(grad_in_second, "shard", scatter_dimension=0, tiled=True)
+
+    def send_back(near_rows, across_one, across_two):
+        return [near_rows[:CAP], swap(near_rows[CAP:], 1), across_one, swap(across_two, 1)]
+
+    drow_parts = send_back(near[3], across_one, across_two)
+    out_far = swap(after(far[2], across_two), 2)
+
+    def place(values):
+        if dp_size > EXPERTS:
+            every = [
+                jnp.sum(lax.all_gather(v, "dp", axis=0).astype(F32).reshape((-1, EXPERTS) + v.shape), axis=0)
+                for v in values
+            ]
+            return jnp.concatenate(every, axis=2)
+        parts = [jnp.concatenate(list(pieces), axis=1).astype(F32) for pieces in zip(*[spread(v) for v in values])]
+        out = jnp.zeros((EXPERTS,) + parts[0].shape, F32)
         for x in range(EXPERTS):
-            out = lax.dynamic_update_index_in_dim(out, parts[x].astype(F32), relation_ids[x], 0)
+            out = lax.dynamic_update_index_in_dim(out, parts[x], relation_ids[x], 0)
         return out
 
-    grad_w_in = place(grad_in)
-    grad_w_out = place(grad_out)
-
-    def collect(parts):
-        stacked = jnp.concatenate(parts, axis=0)
-        return lax.dot_general(my_picks, stacked, (((0,), (0,)), ((), ())), preferred_element_type=F32)
-
-    mixed_out = (residual + collect(out_parts)).astype(BF16)
-    grad_act_two = collect(drow_parts)
     grad_gates = jnp.stack(related(jnp.stack(dgate_parts, axis=0)), axis=0)
     weighted = jnp.sum(grad_gates * gates, axis=0, keepdims=True)
     grad_prob = hits * (grad_gates - weighted) / chosen_sum
     grad_logits = (prob_all * (grad_prob - jnp.sum(prob_all * grad_prob, axis=0, keepdims=True))).astype(BF16)
     grad_router = lax.dot_general(act_two, grad_logits, (((0,), (1,)), ((), ())), preferred_element_type=F32)
-    grad_act_two = grad_act_two + lax.dot_general(
-        grad_logits, router_weight, (((0,), (1,)), ((), ())), preferred_element_type=F32
-    )
-    grad_norm_two, grad_gain_two = norm_backward(grad_act_two, unit_two, inv_two, gain_two)
-    grad_residual = cotangent.astype(F32) + grad_norm_two
-    grad_branch = grad_residual.astype(BF16)
-    grad_attn_weight = lax.dot_general(
-        attended, grad_branch, (((0,), (0,)), ((), ())), preferred_element_type=F32
-    )
-    grad_attended = dot_nt(grad_branch, attn_weight).astype(BF16)
+    extra = lax.dot_general(grad_logits, router_weight, (((0,), (1,)), ((), ())), preferred_element_type=F32)
+    grad_residual, grad_attended, grad_attn_weight, grad_gain_two = token_back(
+        key_cols, extra, residual, cotangent, attended, gain_two[None], packed, drow_parts
+    )
+    grad_attended = after(grad_attended, grad_in_second)
     grad_split, grad_lines = attend_backward(
         qkv_rows, attended, grad_attended, totals, seg_col, seg_row, lines
     )
-    grad_act_one = sum(dot_nt(grad_split[i], qkv_weight[:, i * D : (i + 1) * D]) for i in range(3))
-    grad_qkv_weight = [
-        lax.dot_general(act_one, grad_split[i], (((0,), (0,)), ((), ())), preferred_element_type=F32)
-        for i in range(3)
-    ]
-    grad_norm_one, grad_gain_one = norm_backward(grad_act_one, unit_one, inv_one, gain_one)
-    grad_tokens = (grad_residual + grad_norm_one).astype(BF16)
+    grad_split, out_far, sum_out = lax.optimization_barrier((grad_split, out_far, sum_out))
+    grad_qkv_weight, grad_tokens, grad_gain_one = qkv_back(
+        act_one, grad_split, packed, tokens, gain_one[None], grad_residual
+    )
+    mixed_out = mix_rows(key_cols, residual, send_back(near[2], out_far[:CAP], out_far[CAP:]))
+    grad_w_out = place([sum_out])
     grad_table = lax.dot_general(
         bucket_hits.astype(F32), bias_line_grads(grad_lines), (((1,), (1,)), ((), ())), precision=HIGHEST
     )
@@ -513,14 +752,28 @@
     table_sums = jnp.pad(
         grad_table.reshape(shards, table_rows * HEADS), ((0, 0), (0, shard_rows - table_rows * HEADS))
     ).reshape(D, 1)
-    small = jnp.concatenate([grad_gain_one[:, None], grad_gain_two[:, None], grad_router, table_sums], axis=1)
+    small = jnp.concatenate([grad_gain_one.T, grad_gain_two.T, grad_router, table_sums], axis=1)
     packed = jnp.concatenate(
-        [g.astype(BF16) for g in grad_qkv_weight]
-        + [grad_attn_weight.astype(BF16), jnp.pad(small, ((0, 0), (0, 121))).astype(BF16)],
+        [grad_qkv_weight, grad_attn_weight, jnp.pad(small, ((0, 0), (0, 121))).astype(BF16)],
         axis=1,
     )
-    packed = lax.psum_scatter(packed, "shard", scatter_dimension=0, tiled=True).astype(F32)
-    packed = lax.psum(packed, "dp")
+    packed = packed.reshape(shards, 2, core_rows, packed.shape[1])
+    kept = lax.dynamic_index_in_dim(packed, core, 1, keepdims=False)
+    sent = lax.dynamic_index_in_dim(packed, 1 - core, 1, keepdims=False)
+    kept = (kept.astype(F32) + swap(sent, 1).astype(F32)).astype(BF16)
+    kept, mixed_out, grad_tokens, grad_w_out = lax.optimization_barrier(
+        (sum_over_x(kept), mixed_out, grad_tokens, grad_w_out)
+    )
+    kept, sum_in_second = lax.optimization_barrier((sum_over_z(kept), sum_in_second))
+    grad_w_in = place([sum_in_first, sum_in_second])
+    if dp_size > EXPERTS:
+        total = lax.all_gather(kept, "dp", axis=0).reshape((-1, 2) + kept.shape)
+        total = jnp.sum(lax.dynamic_index_in_dim(total, core, 1, keepdims=False), axis=0)
+    else:
+        kept = kept.astype(BF16)
+        total = kept.astype(F32) + swap(kept, 2).astype(F32)
+    other = swap(total, 1)
+    packed = jnp.concatenate([jnp.where(core == 0, total, other), jnp.where(core == 0, other, total)], axis=0)
     return (
         mixed_out,
         grad_tokens,

time: 715 us -> 612 us (0.86)
  matrix products: 135 us -> 58 us
  Pallas kernels: 138 us -> 206 us
  waiting for transfers between devices: 247 us -> 195 us
  blocking collectives: 34.8 us -> 0 us
  local copies, waits for them, and re-layouts: 66.2 us -> 39.7 us
  starting transfers between devices: 27.6 us -> 45.9 us
    ppermute x0 -> x11, waiting for transfers between devices: none -> 90.9 us  [the longest x6 58.5 us: step_z(): return lax.ppermute(value, 'shard', pairs)]
    dot_general x30 -> x4, matrix products: 116 us -> 38 us  [weight_grad(): lax.dot_general(left, right, (((0,), (0,)), ((), ())), preferred_element_...]
    pallas_call x2 -> x8, Pallas kernels: 77.6 us -> 146 us  [the longest x2 58 us: expert_first(): pl.pallas_call(first_half_kernel, grid=(2,), in_specs=[fixed_spec((SEQ, D...]
    ppermute x27 -> x32, waiting for transfers between devices: 142 us -> 73.1 us  [swap(): lax.ppermute(value, 'dp', [(i, i ^ relation) for i in range(dp_size)])]
    all_gather x1, waiting for transfers between devices: 47.8 us -> 0.02 us  [body(): full_out = lax.all_gather(my_out, 'shard', axis=0, tiled=True)]
    all_gather x2, waiting for transfers between devices: 43.4 us -> 0.01 us  [the longest x1 0.01 us: body(): half_in = [lax.all_gather(my_in[:, :FF_HALF], 'shard', axis=0, tiled=True)]]
    psum x1 -> x0, blocking collectives: 34.8 us -> none  [body(): packed = lax.psum(packed, 'dp')]
    reduce_scatter x1, waiting for transfers between devices: 0.01 us -> 30.5 us  [body(): lax.psum_scatter(grad_out, 'shard', scatter_dimension=0, tiled=True)]
  transfers between devices with their start and end apart: 33 -> 49, of which waited for: 15 -> 19; matrix products, arithmetic and copies ran while one was open for 29% -> 17% of each run, Pallas kernels for 14% -> 28%
where the time goes in v2:
time: 612 us; the launch traced here: 601 us
  Pallas kernels  206 us (34%)
  waiting for transfers between devices  195 us (32%)
  matrix products  58 us (9%)
  starting transfers between devices  45.9 us (8%)
  local copies, waits for them, and re-layouts  39.7 us (6%)
  other arithmetic  33.5 us (5%)
  between operations  23.4 us (4%)
    ppermute x32, waiting for transfers between devices, swap(): lax.ppermute(value, 'dp', [(i, i ^ relation) for i in range(dp_size)])  73.1 us
    ppermute x6, waiting for transfers between devices, step_z(): return lax.ppermute(value, 'shard', pairs)  58.5 us
    pallas_call x2, Pallas kernels, expert_first(): pl.pallas_call(first_half_kernel, grid=(2,), in_specs=[fixed_spec((SEQ, D...  58 us
    pallas_call x2, Pallas kernels, expert_second(): pl.pallas_call(second_half_kernel, grid=(2,), in_specs=[slot_spec(pair, w...  47.9 us
    dot_general x4, matrix products, weight_grad(): lax.dot_general(left, right, (((0,), (0,)), ((), ())), preferred_element_...  38 us
    ppermute x32, starting transfers between devices, swap(): lax.ppermute(value, 'dp', [(i, i ^ relation) for i in range(dp_size)])  32.8 us
    ppermute x5, waiting for transfers between devices, step_x(): return lax.ppermute(value, 'shard', pairs)  32.4 us
    pallas_call x1, Pallas kernels, attend_backward(): pl.pallas_call(attention_back_kernel, grid=(PAIRS,), in_specs=[pair_spec(...  31.4 us
  transfers between devices with their start and end apart: 49, of which 19 were waited for; matrix products, arithmetic and copies ran while one was open for 17% of the time, Pallas kernels for 28%

profile of v2, /device:TPU:9, one launch (start us, length us, event | category | flops | bytes accessed | tf_op | source)
XLA Modules:
  0.0 601.3 jit_solution(1451290205099278941)
XLA Ops:
  17.5 3.1 collective-permute-done.1.refs_2_
  21.9 27.1 %collective-permute-done.3.refs_4_ = bf16[48,3200]{1,0:T(8,128)(2,1)S(1)} collective-permute-done((bf16[48,3200]{1,0:T(8,128)(2,1)S(1)}, bf16[48,3200]{1,0:T(8,128)(2,1)S(1)}, u32[]{:S(2)}, u32[]{:S(2)}) %collective-permute-start.3) | collective-permute-done | bytes 307232 | tf_op jit(solution)/shard_map/ppermute | solution.py:574
  56.3 11.6 %collective-permute-done.6.refs_7_ = bf16[48,3200]{1,0:T(8,128)(2,1)} collective-permute-done((bf16[48,3200]{1,0:T(8,128)(2,1)S(1)}, bf16[48,3200]{1,0:T(8,128)(2,1)}, u32[]{:S(2)}, u32[]{:S(2)}) %collective-permute-start.6) | collective-permute-done | bytes 307232 | tf_op jit(solution)/shard_map/ppermute | solution.py:580
  70.5 6.6 %collective-permute-start.7 = (bf16[8,48,3200]{2,1,0:T(8,128)(2,1)}, bf16[8,48,3200]{2,1,0:T(8,128)(2,1)}, u32[]{:S(2)}, u32[]{:S(2)}) collective-permute-start(bf16[8,48,3200]{2,1,0:T(8,128)(2,1)} %place_blocks.1), channel_id=1, source_target_pairs={{0,8},{8,0},{16,24},{24,16},{1,9},{9,1},{17,25},{25,17},{2,10},{10... | collective-permute-start | bytes 7372808 | tf_op jit(solution)/shard_map/ppermute | solution.py:564
  91.1 8.0 %convolution_convert_fusion.q_ref.k_ref.v_ref = bf16[1024,2304]{1,0:T(8,128)(2,1)} fusion(bf16[1024,768]{1,0:T(8,128)(2,1)S(1)} %fusion.7.act_ref, bf16[768,3200]{1,0:T(8,128)(2,1)} %bitcast.13.weight_ref), kind=kOutput, calls=%fused_computation.2 | convolution fusion | flops 3626237952 | bytes 9830400 | tf_op jit(solution)/shard_map/dot_general | solution.py:671
  99.2 28.3 %attend_forward.1 = (bf16[1024,768]{1,0:T(8,128)(2,1)S(1)}, f32[6,8,1024]{2,1,0:T(8,128)S(1)}) custom-call(bf16[1024,2304]{1,0:T(8,128)(2,1)} %convolution_convert_fusion.q_ref.k_ref.v_ref, bf16[1024,2304]{1,0:T(8,128)(2,1)} %convolution_convert_fusion.q_ref.k_ref.v_ref, bf16[1024,2304]{1,0:T(8,128)(2,1)} %convolution_convert_fusion.q_ref.k_ref.v_ref, ...), custom_call_target="tpu_custom_call" | custom-call | flops 12582912 | bytes 24576 | tf_op jit(solution)/shard_map/attend_forward/pallas_call | solution.py:181
  127.5 3.4 multiply_reduce_fusion
  135.3 33.3 %collective-permute-done.8.act_one_ref = bf16[1024,768]{1,0:T(8,128)(2,1)} collective-permute-done((bf16[1024,768]{1,0:T(8,128)(2,1)}, bf16[1024,768]{1,0:T(8,128)(2,1)}, u32[]{:S(2)}, u32[]{:S(2)}) %collective-permute-start.8) | collective-permute-done | bytes 1572896 | tf_op jit(solution)/shard_map/ppermute | solution.py:564
  179.6 29.1 %expert_first.2 = (bf16[2560,768]{1,0:T(8,128)(2,1)}, bf16[2560,768]{1,0:T(8,128)(2,1)}, bf16[2560,768]{1,0:T(8,128)(2,1)}, f32[2560,1]{1,0:T(8,128)}, bf16[2560...) custom-call(bf16[1024,768]{1,0:T(8,128)(2,1)} %multiply_convert_fusion.act_one_ref, ...), custom_call_target="tpu_custom_call" | custom-call | flops 47185920 | bytes 56832 | tf_op jit(solution)/shard_map/expert_first/pallas_call | solution.py:516
  208.8 28.9 %expert_first.3 = (bf16[2560,768]{1,0:T(8,128)(2,1)}, bf16[2560,768]{1,0:T(8,128)(2,1)}, bf16[2560,768]{1,0:T(8,128)(2,1)}, f32[2560,1]{1,0:T(8,128)}, bf16[2560...) custom-call(bf16[1024,768]{1,0:T(8,128)(2,1)} %collective-permute-do, ...), custom_call_target="tpu_custom_call", output_to_operand_aliasing={{0}: (9, {}), {1}: (10, {}), {2}: (11, {}), {3}: (12, {}), ... | custom-call | flops 47185920 | bytes 56832 | tf_op jit(solution)/shard_map/expert_first/pallas_call | solution.py:516
  237.7 11.4 %convolution_convert_fusion.4 = bf16[768,1536]{1,0:T(8,128)(2,1)} fusion(bf16[2560,768]{1,0:T(8,128)(2,1)} %get-tuple-element.71.rows_ref, bf16[2560,1536]{1,0:T(8,128)(2,1)} %get-tuple-element.77), kind=kOutput, calls=%fused_computation.17 | convolution fusion | flops 6040977408 | bytes 14155776 | tf_op jit(solution)/shard_map/dot_general | solution.py:693
  249.1 23.8 %expert_second.2 = (bf16[2560,1536]{1,0:T(8,128)(2,1)}, bf16[2560,1536]{1,0:T(8,128)(2,1)}, bf16[1280,768]{1,0:T(8,128)(2,1)}, bf16[1280,768]{1,0:T(8,128)(2,1)}, f32[8,1024]{1,0:T(8,128)}) custom-call(bf16[2560,768]{1,0:T(8,128)(2,1)} %get-tuple-element.71.rows_ref, bf16[2560,768]{1,0:T(8,128)(2,1)} %get-tuple-element.72.graw_ref, ...), custom_call_target="tpu_custom_call" | custom-call | flops 47185920 | bytes 56832 | tf_op jit(solution)/shard_map/expert_second/pallas_call | solution.py:537
  285.9 24.1 %expert_second.3 = (bf16[2560,1536]{1,0:T(8,128)(2,1)}, bf16[2560,1536]{1,0:T(8,128)(2,1)}, bf16[1280,768]{1,0:T(8,128)(2,1)}, bf16[1280,768]{1,0:T(8,128)(2,1)}, f32[8,1024]{1,0:T(8,128)}) custom-call(bf16[2560,768]{1,0:T(8,128)(2,1)} %get-tuple-element.71.rows_ref, ...), custom_call_target="tpu_custom_call", output_to_operand_aliasing={{0}: (9, {}), {1}: (10, {})} | custom-call | flops 47185920 | bytes 56832 | tf_op jit(solution)/shard_map/expert_second/pallas_call | solution.py:537
  310.0 8.9 %convolution_convert_fusion.3 = bf16[1536,768]{1,0:T(8,128)(2,1)S(1)} fusion(bf16[2560,1536]{1,0:T(8,128)(2,1)} %get-tuple-element.89, bf16[2560,768]{1,0:T(8,128)(2,1)S(1)} %copy-done.21), kind=kOutput, calls=%fused_computation.16 | convolution fusion | flops 6040977408 | bytes 14155776 | tf_op jit(solution)/shard_map/dot_general | solution.py:693
  318.9 6.7 %convolution_convert_fusion.2 = bf16[1536,768]{1,0:T(8,128)(2,1)S(1)} fusion(bf16[2560,1536]{1,0:T(8,128)(2,1)S(1)} %copy-done.24, bf16[2560,768]{1,0:T(8,128)(2,1)S(1)} %copy-done.21), kind=kOutput, calls=%fused_computation.15 | convolution fusion | flops 6040977408 | bytes 14155776 | tf_op jit(solution)/shard_map/dot_general | solution.py:693
  335.0 16.6 %collective-permute-done.18 = f32[1024]{0:T(1024)S(1)} collective-permute-done((f32[1024]{0:T(1024)S(1)}, f32[1024]{0:T(1024)S(1)}, u32[]{:S(2)}, u32[]{:S(2)}) %collective-permute-start.18) | collective-permute-done | bytes 4128 | tf_op jit(solution)/shard_map/ppermute | solution.py:564
  355.0 3.3 fusion.18.extra_ref
  358.6 15.1 %token_back.1 = (f32[1024,768]{1,0:T(8,128)S(1)}, bf16[1024,768]{1,0:T(8,128)(2,1)S(1)}, bf16[768,768]{1,0:T(8,128)(2,1)S(1)}, f32[1,768]{1,0:T(1,128)S(1)}) custom-call(f32[1024,4]{1,0:T(8,128)S(1)} %copy.111.key_ref, f32[1024,768]{1,0:T(8,128)} %fusion.18.extra_ref, f32[1024,768]{1,0:T(8,128)} %copy-done.2, bf16[1024,768]{1,0:T(8,128)(2,1)} %cot_ref.1, ...), custom_call_target="tpu_custom_call" | custom-call | flops 25165824 | bytes 70656 | tf_op jit(solution)/shard_map/token_back/pallas_call | solution.py:434
  378.1 11.0 %convolution_convert_fusion.1 = bf16[768,1536]{1,0:T(8,128)(2,1)} fusion(bf16[2560,768]{1,0:T(8,128)(2,1)} %get-tuple-element.71.rows_ref, bf16[2560,1536]{1,0:T(8,128)(2,1)} %get-tuple-element.91), kind=kOutput, calls=%fused_computation.14 | convolution fusion | flops 6040977408 | bytes 14155776 | tf_op jit(solution)/shard_map/dot_general | solution.py:693
  391.6 31.4 %attend_backward.1 = (bf16[3,1024,768]{2,1,0:T(8,128)(2,1)}, f32[6,8,512]{2,1,0:T(8,128)S(1)}) custom-call(bf16[1024,2304]{1,0:T(8,128)(2,1)} %convolution_convert_fusion.q_ref.k_ref.v_ref, bf16[1024,2304]{1,0:T(8,128)(2,1)} %convolution_convert_fusion.q_ref.k_ref.v_ref, bf16[1024,2304]{1,0:T(8,128)(2,1)} %convolution_convert_fusion.q_ref.k_ref.v_ref, ...), custom_call_target="tpu_custom_call" | custom-call | flops 31457280 | bytes 49152 | tf_op jit(solution)/shard_map/attend_backward/pallas_call | solution.py:198
  424.4 30.5 %reduce-scatter.6.cloned.1.call-done = bf16[384,768]{1,0:T(8,128)(2,1)} async-done(((bf16[3072,768]{1,0:T(8,128)(2,1)}), bf16[384,768]{1,0:T(8,128)(2,1)}) %reduce-scatter.6.cloned.1.call-update) | async-done | bytes 589840 | tf_op jit(solution)/shard_map/reduce_scatter | solution.py:706
  456.3 14.7 %qkv_back.1 = (bf16[768,2304]{1,0:T(8,128)(2,1)}, bf16[1024,768]{1,0:T(8,128)(2,1)}, f32[1,768]{1,0:T(1,128)S(1)}) custom-call(bf16[1024,768]{1,0:T(8,128)(2,1)S(1)} %copy-done.10, bf16[3,1024,768]{2,1,0:T(8,128)(2,1)} %get-tuple-element.97.split_ref, bf16[768,3200]{1,0:T(8,128)(2,1)} %bitcast.13.weight_ref, bf16[1024,768]{1,0:T(8,128)(2,1)S(1)} %copy-done.6, ...), custom_call_target="tpu_custom_call" | custom-call | flops 28311552 | bytes 76800 | tf_op jit(solution)/shard_map/qkv_back/pallas_call | solution.py:477
  471.2 4.9 fusion.1
  476.1 3.4 dynamic-slice_bitcast_fusion
  493.0 4.1 collective-permute-done.30
  501.0 8.0 %mix_rows.1 = bf16[1024,768]{1,0:T(8,128)(2,1)} custom-call(f32[1024,4]{1,0:T(8,128)S(1)} %copy-done.14, f32[1024,768]{1,0:T(8,128)S(1)} %copy-done.3, bf16[640,768]{1,0:T(8,128)(2,1)S(1)} %get-tuple-element.168.one_ref, bf16[640,768]{1,0:T(8,128)(2,1)S(1)} %collective-permute-done.27.two_ref, bf16[640,768]{1,0:T(8,128)(2,1)S(1)} %get-tuple-element.166.three_ref, ...), custom_call_target="tpu_custom_call" | custom-call | flops 15728640 | bytes 33792 | tf_op jit(solution)/shard_map/mix_rows/pallas_call | solution.py:384
  509.1 19.8 %collective-permute-done.26 = bf16[4,48,3200]{2,1,0:T(8,128)(2,1)} collective-permute-done((bf16[4,48,3200]{2,1,0:T(8,128)(2,1)}, bf16[4,48,3200]{2,1,0:T(8,128)(2,1)}, u32[]{:S(2)}, u32[]{:S(2)}) %collective-permute-start.26) | collective-permute-done | bytes 1228832 | tf_op jit(solution)/shard_map/ppermute | solution.py:580
  536.8 3.5 collective-permute-done.39
  543.1 22.3 %collective-permute-done.33 = bf16[48,3200]{1,0:T(8,128)(2,1)S(1)} collective-permute-done((bf16[48,3200]{1,0:T(8,128)(2,1)S(1)}, bf16[48,3200]{1,0:T(8,128)(2,1)S(1)}, u32[]{:S(2)}, u32[]{:S(2)}) %collective-permute-start.33) | collective-permute-done | bytes 307232 | tf_op jit(solution)/shard_map/ppermute | solution.py:574
  565.4 4.3 collective-permute-done.34
  572.6 6.6 %collective-permute-done.40 = bf16[96,1536]{1,0:T(8,128)(2,1)S(1)} collective-permute-done((bf16[96,1536]{1,0:T(8,128)(2,1)}, bf16[96,1536]{1,0:T(8,128)(2,1)S(1)}, u32[]{:S(2)}, u32[]{:S(2)}) %collective-permute-start.40) | collective-permute-done | bytes 294944 | tf_op jit(solution)/shard_map/ppermute | solution.py:564
  581.7 4.2 collective-permute-done.35
  (267 shorter events, 119.8 us)
Async XLA Ops:
  7.2 172.4 %all-gather.5.cloned.1.call-start = ((), (), s32[]{:S(2)}) async-start(), calls=%async_computation.3 | async-start | bytes 2654208 | tf_op jit(solution)/shard_map/all_gather | solution.py:638
  9.8 169.9 %all-gather.9.cloned.1.call-start = ((), (), s32[]{:S(2)}) async-start(), calls=%async_computation.8 | async-start | bytes 5308416 | tf_op jit(solution)/shard_map/all_gather | solution.py:639
  13.8 35.2 %collective-permute-start.3 = (bf16[48,3200]{1,0:T(8,128)(2,1)S(1)}, bf16[48,3200]{1,0:T(8,128)(2,1)S(1)}, u32[]{:S(2)}, u32[]{:S(2)}) collective-permute-start(bf16[48,3200]{1,0:T(8,128)(2,1)S(1)} %fusion.15.refs_0_), channel_id=1, source_target_pairs={{0,4},{1,5},{2,6},{3,7},{4,0},{5,1},{6,2},{7,3},{8,12},{9,13},{10,... | collective-permute-start | bytes 921608 | tf_op jit(solution)/shard_map/ppermute | solution.py:574
  14.9 36.9 %collective-permute-start.5 = (bf16[48,3200]{1,0:T(8,128)(2,1)S(1)}, bf16[48,3200]{1,0:T(8,128)(2,1)S(1)}, u32[]{:S(2)}, u32[]{:S(2)}) collective-permute-start(bf16[48,3200]{1,0:T(8,128)(2,1)S(1)} %fusion.15.refs_0_), channel_id=1, source_target_pairs={{0,6},{1,7},{2,0},{3,1},{4,2},{5,3},{6,4},{7,5},{8,14},{9,15},{10,... | collective-permute-start | bytes 921608 | tf_op jit(solution)/shard_map/ppermute | solution.py:574
  16.3 39.0 %collective-permute-start = (bf16[48,3200]{1,0:T(8,128)(2,1)S(1)}, bf16[48,3200]{1,0:T(8,128)(2,1)S(1)}, u32[]{:S(2)}, u32[]{:S(2)}) collective-permute-start(bf16[48,3200]{1,0:T(8,128)(2,1)S(1)} %fusion.15.refs_0_), channel_id=1, source_target_pairs={{0,1},{1,0},{2,3},{3,2},{4,5},{5,4},{6,7},{7,6},{8,9},{9,8},{10,11... | collective-permute-start | bytes 921608 | tf_op jit(solution)/shard_map/ppermute | solution.py:580
  20.6 34.6 %collective-permute-start.2 = (bf16[48,3200]{1,0:T(8,128)(2,1)S(1)}, bf16[48,3200]{1,0:T(8,128)(2,1)S(1)}, u32[]{:S(2)}, u32[]{:S(2)}) collective-permute-start(bf16[48,3200]{1,0:T(8,128)(2,1)S(1)} %collective-permute-done.1.refs_2_), channel_id=1, source_target_pairs={{0,1},{1,0},{2,3},{3,2},{4,5},{5,4},{6,7},{7,6},{8,9},{9,8},{10,11... | collective-permute-start | bytes 921608 | tf_op jit(solution)/shard_map/ppermute | solution.py:580
  51.8 16.0 %collective-permute-start.6 = (bf16[48,3200]{1,0:T(8,128)(2,1)S(1)}, bf16[48,3200]{1,0:T(8,128)(2,1)}, u32[]{:S(2)}, u32[]{:S(2)}) collective-permute-start(bf16[48,3200]{1,0:T(8,128)(2,1)S(1)} %collective-permute-done.5.refs_6_), channel_id=1, source_target_pairs={{0,1},{1,0},{2,3},{3,2},{4,5},{5,4},{6,7},{7,6},{8,9},{9,8},{10,11... | collective-permute-start | bytes 921608 | tf_op jit(solution)/shard_map/ppermute | solution.py:580
  55.0 194.1 %all-gather.7.cloned.1.call-start = ((), (), s32[]{:S(2)}) async-start(), calls=%async_computation.4 | async-start | bytes 2654208 | tf_op jit(solution)/shard_map/all_gather | solution.py:640
  77.1 57.6 %collective-permute-start.10 = (bf16[1024,768]{1,0:T(8,128)(2,1)}, bf16[1024,768]{1,0:T(8,128)(2,1)}, u32[]{:S(2)}, u32[]{:S(2)}) collective-permute-start(bf16[1024,768]{1,0:T(8,128)(2,1)} %cot_ref.1), channel_id=1, source_target_pairs={{0,16},{8,24},{16,0},{24,8},{1,17},{9,25},{17,1},{25,9},{2,18},{10... | collective-permute-start | bytes 4718600 | tf_op jit(solution)/shard_map/ppermute | solution.py:564
  132.6 35.9 %collective-permute-start.8 = (bf16[1024,768]{1,0:T(8,128)(2,1)}, bf16[1024,768]{1,0:T(8,128)(2,1)}, u32[]{:S(2)}, u32[]{:S(2)}) collective-permute-start(bf16[1024,768]{1,0:T(8,128)(2,1)} %multiply_convert_fusion.act_one_ref), channel_id=1, source_target_pairs={{0,16},{8,24},{16,0},{24,8},{1,17},{9,25},{17,1},{25,9},{2,18},{10... | collective-permute-start | bytes 4718600 | tf_op jit(solution)/shard_map/ppermute | solution.py:564
  133.9 244.2 %reduce-scatter.4.cloned.1.call-start = ((), (), s32[]{:S(2)}) async-start(), calls=%async_computation.5 | async-start | bytes 2654208 | tf_op jit(solution)/shard_map/reduce_scatter | solution.py:696
  134.0 45.6 %collective-permute-start.15 = (bf16[1024,768]{1,0:T(8,128)(2,1)}, bf16[1024,768]{1,0:T(8,128)(2,1)}, u32[]{:S(2)}, u32[]{:S(2)}) collective-permute-start(bf16[1024,768]{1,0:T(8,128)(2,1)} %cot_ref.1), channel_id=1, source_target_pairs={{0,8},{8,0},{16,24},{24,16},{1,9},{9,1},{17,25},{25,17},{2,10},{10... | collective-permute-start | bytes 4718600 | tf_op jit(solution)/shard_map/ppermute | solution.py:564
  134.7 74.1 %collective-permute-start.11 = (bf16[1024,768]{1,0:T(8,128)(2,1)}, bf16[1024,768]{1,0:T(8,128)(2,1)}, u32[]{:S(2)}, u32[]{:S(2)}) collective-permute-start(bf16[1024,768]{1,0:T(8,128)(2,1)} %collective-permute-done.10.cot_one_ref), channel_id=1, source_target_pairs={{0,8},{8,0},{16,24},{24,16},{1,9},{9,1},{17,25},{25,17},{2,10},{10... | collective-permute-start | bytes 4718600 | tf_op jit(solution)/shard_map/ppermute | solution.py:564
  134.8 44.8 %collective-permute-start.14 = (bf16[1024,768]{1,0:T(8,128)(2,1)}, bf16[1024,768]{1,0:T(8,128)(2,1)}, u32[]{:S(2)}, u32[]{:S(2)}) collective-permute-start(bf16[1024,768]{1,0:T(8,128)(2,1)} %multiply_convert_fusion.act_one_ref), channel_id=1, source_target_pairs={{0,8},{8,0},{16,24},{24,16},{1,9},{9,1},{17,25},{25,17},{2,10},{10... | collective-permute-start | bytes 4718600 | tf_op jit(solution)/shard_map/ppermute | solution.py:564
  168.6 40.2 %collective-permute-start.9 = (bf16[1024,768]{1,0:T(8,128)(2,1)}, bf16[1024,768]{1,0:T(8,128)(2,1)}, u32[]{:S(2)}, u32[]{:S(2)}) collective-permute-start(bf16[1024,768]{1,0:T(8,128)(2,1)} %collective-permute-done.8.act_one_ref), channel_id=1, source_target_pairs={{0,8},{8,0},{16,24},{24,16},{1,9},{9,1},{17,25},{25,17},{2,10},{10... | collective-permute-start | bytes 4718600 | tf_op jit(solution)/shard_map/ppermute | solution.py:564
  275.5 34.5 %collective-permute-start.21 = (bf16[640,768]{1,0:T(8,128)(2,1)S(1)}, bf16[640,768]{1,0:T(8,128)(2,1)S(1)}, u32[]{:S(2)}, u32[]{:S(2)}) collective-permute-start(bf16[640,768]{1,0:T(8,128)(2,1)S(1)} %get-tuple-element.170), channel_id=1, source_target_pairs={{0,16},{8,24},{16,0},{24,8},{1,17},{9,25},{17,1},{25,9},{2,18},{10... | collective-permute-start | bytes 2949128 | tf_op jit(solution)/shard_map/ppermute | solution.py:564
  285.1 169.8 %reduce-scatter.6.cloned.1.call-start = ((), (), s32[]{:S(2)}) async-start(), calls=%async_computation.6 | async-start | bytes 5308416 | tf_op jit(solution)/shard_map/reduce_scatter | solution.py:706
  328.1 241.8 %reduce-scatter.8.cloned.1.call-start = ((), (), s32[]{:S(2)}) async-start(), calls=%async_computation.7 | async-start | bytes 2654208 | tf_op jit(solution)/shard_map/reduce_scatter | solution.py:708
  328.5 24.4 %collective-permute-start.22 = (bf16[640,768]{1,0:T(8,128)(2,1)}, bf16[640,768]{1,0:T(8,128)(2,1)S(1)}, u32[]{:S(2)}, u32[]{:S(2)}) collective-permute-start(bf16[640,768]{1,0:T(8,128)(2,1)} %get-tuple-element.169), channel_id=1, source_target_pairs={{0,16},{8,24},{16,0},{24,8},{1,17},{9,25},{17,1},{25,9},{2,18},{10... | collective-permute-start | bytes 2949128 | tf_op jit(solution)/shard_map/ppermute | solution.py:564
  331.4 20.2 %collective-permute-start.18 = (f32[1024]{0:T(1024)S(1)}, f32[1024]{0:T(1024)S(1)}, u32[]{:S(2)}, u32[]{:S(2)}) collective-permute-start(f32[1024]{0:T(1024)S(1)} %bitcast.158), channel_id=1, source_target_pairs={{0,16},{8,24},{16,0},{24,8},{1,17},{9,25},{17,1},{25,9},{2,18},{10... | collective-permute-start | bytes 12296 | tf_op jit(solution)/shard_map/ppermute | solution.py:564
  332.6 20.2 %collective-permute-start.19 = (f32[1024]{0:T(1024)S(1)}, f32[1024]{0:T(1024)S(1)}, u32[]{:S(2)}, u32[]{:S(2)}) collective-permute-start(f32[1024]{0:T(1024)S(1)} %bitcast.157), channel_id=1, source_target_pairs={{0,24},{8,16},{16,8},{24,0},{1,25},{9,17},{17,9},{25,1},{2,26},{10... | collective-permute-start | bytes 12296 | tf_op jit(solution)/shard_map/ppermute | solution.py:564
  334.7 23.8 %collective-permute-start.20 = (bf16[640,768]{1,0:T(8,128)(2,1)S(1)}, bf16[640,768]{1,0:T(8,128)(2,1)S(1)}, u32[]{:S(2)}, u32[]{:S(2)}) collective-permute-start(bf16[640,768]{1,0:T(8,128)(2,1)S(1)} %get-tuple-element.171), channel_id=1, source_target_pairs={{0,8},{8,0},{16,24},{24,16},{1,9},{9,1},{17,25},{25,17},{2,10},{10... | collective-permute-start | bytes 2949128 | tf_op jit(solution)/shard_map/ppermute | solution.py:564
  358.3 66.0 %collective-permute-start.24 = (bf16[1280,768]{1,0:T(8,128)(2,1)}, bf16[1280,768]{1,0:T(8,128)(2,1)}, u32[]{:S(2)}, u32[]{:S(2)}) collective-permute-start(bf16[1280,768]{1,0:T(8,128)(2,1)} %get-tuple-element.96), channel_id=1, source_target_pairs={{0,16},{8,24},{16,0},{24,8},{1,17},{9,25},{17,1},{25,9},{2,18},{10... | collective-permute-start | bytes 5898248 | tf_op jit(solution)/shard_map/ppermute | solution.py:564
  481.4 19.5 %collective-permute-start.27 = (bf16[640,768]{1,0:T(8,128)(2,1)}, bf16[640,768]{1,0:T(8,128)(2,1)S(1)}, u32[]{:S(2)}, u32[]{:S(2)}) collective-permute-start(bf16[640,768]{1,0:T(8,128)(2,1)} %get-tuple-element.167), channel_id=1, source_target_pairs={{0,8},{8,0},{16,24},{24,16},{1,9},{9,1},{17,25},{25,17},{2,10},{10... | collective-permute-start | bytes 2949128 | tf_op jit(solution)/shard_map/ppermute | solution.py:564
  481.5 16.9 %collective-permute-start.29 = (bf16[384,768]{1,0:T(8,128)(2,1)S(1)}, bf16[384,768]{1,0:T(8,128)(2,1)}, u32[]{:S(2)}, u32[]{:S(2)}) collective-permute-start(bf16[384,768]{1,0:T(8,128)(2,1)S(1)} %copy-done.28), channel_id=1, source_target_pairs={{0,8},{8,0},{16,24},{24,16},{1,9},{9,1},{17,25},{25,17},{2,10},{10... | collective-permute-start | bytes 1769480 | tf_op jit(solution)/shard_map/ppermute | solution.py:564
  482.1 15.0 %collective-permute-start.30 = (bf16[384,768]{1,0:T(8,128)(2,1)S(1)}, bf16[384,768]{1,0:T(8,128)(2,1)}, u32[]{:S(2)}, u32[]{:S(2)}) collective-permute-start(bf16[384,768]{1,0:T(8,128)(2,1)S(1)} %copy-done.28), channel_id=1, source_target_pairs={{0,16},{8,24},{16,0},{24,8},{1,17},{9,25},{17,1},{25,9},{2,18},{10... | collective-permute-start | bytes 1769480 | tf_op jit(solution)/shard_map/ppermute | solution.py:564
  485.9 15.1 %collective-permute-start.28 = (bf16[640,768]{1,0:T(8,128)(2,1)}, bf16[640,768]{1,0:T(8,128)(2,1)}, u32[]{:S(2)}, u32[]{:S(2)}) collective-permute-start(bf16[640,768]{1,0:T(8,128)(2,1)} %get-tuple-element.165), channel_id=1, source_target_pairs={{0,8},{8,0},{16,24},{24,16},{1,9},{9,1},{17,25},{25,17},{2,10},{10... | collective-permute-start | bytes 2949128 | tf_op jit(solution)/shard_map/ppermute | solution.py:564
  491.8 37.1 %collective-permute-start.26 = (bf16[4,48,3200]{2,1,0:T(8,128)(2,1)}, bf16[4,48,3200]{2,1,0:T(8,128)(2,1)}, u32[]{:S(2)}, u32[]{:S(2)}) collective-permute-start(bf16[4,48,3200]{2,1,0:T(8,128)(2,1)} %dynamic-slice_bitcast_fusion.1), channel_id=1, source_target_pairs={{0,1},{1,0},{2,3},{3,2},{4,5},{5,4},{6,7},{7,6},{8,9},{9,8},{10,11... | collective-permute-start | bytes 3686408 | tf_op jit(solution)/shard_map/ppermute | solution.py:580
  531.5 33.9 %collective-permute-start.33 = (bf16[48,3200]{1,0:T(8,128)(2,1)S(1)}, bf16[48,3200]{1,0:T(8,128)(2,1)S(1)}, u32[]{:S(2)}, u32[]{:S(2)}) collective-permute-start(bf16[48,3200]{1,0:T(8,128)(2,1)S(1)} %get-tuple-element.177), channel_id=1, source_target_pairs={{0,4},{1,5},{2,6},{3,7},{4,0},{5,1},{6,2},{7,3},{8,12},{9,13},{10,... | collective-permute-start | bytes 921608 | tf_op jit(solution)/shard_map/ppermute | solution.py:574
  532.7 37.0 %collective-permute-start.34 = (bf16[48,3200]{1,0:T(8,128)(2,1)S(1)}, bf16[48,3200]{1,0:T(8,128)(2,1)S(1)}, u32[]{:S(2)}, u32[]{:S(2)}) collective-permute-start(bf16[48,3200]{1,0:T(8,128)(2,1)S(1)} %get-tuple-element.176), channel_id=1, source_target_pairs={{0,6},{1,7},{2,0},{3,1},{4,2},{5,3},{6,4},{7,5},{8,14},{9,15},{10,... | collective-permute-start | bytes 921608 | tf_op jit(solution)/shard_map/ppermute | solution.py:574
  534.9 45.7 %collective-permute-start.37 = (bf16[96,1536]{1,0:T(8,128)(2,1)S(1)}, bf16[96,1536]{1,0:T(8,128)(2,1)}, u32[]{:S(2)}, u32[]{:S(2)}) collective-permute-start(bf16[96,1536]{1,0:T(8,128)(2,1)S(1)} %copy-done.29), channel_id=1, source_target_pairs={{0,8},{8,0},{16,24},{24,16},{1,9},{9,1},{17,25},{25,17},{2,10},{10... | collective-permute-start | bytes 884744 | tf_op jit(solution)/shard_map/ppermute | solution.py:564
  540.3 47.6 %collective-permute-start.41 = (bf16[96,1536]{1,0:T(8,128)(2,1)}, bf16[96,1536]{1,0:T(8,128)(2,1)}, u32[]{:S(2)}, u32[]{:S(2)}) collective-permute-start(bf16[96,1536]{1,0:T(8,128)(2,1)} %collective-permute-done.39), channel_id=1, source_target_pairs={{0,8},{8,0},{16,24},{24,16},{1,9},{9,1},{17,25},{25,17},{2,10},{10... | collective-permute-start | bytes 884744 | tf_op jit(solution)/shard_map/ppermute | solution.py:564
  (52 other events, 573.5 us)
Sparse Core Ops, SparseCore 0:
  10.8 76.7 all-gather.4
  90.3 78.1 all-gather.8
  171.3 51.2 all-gather.6
  285.3 69.9 reduce-scatter.3
  358.7 96.1 reduce-scatter.5
  481.6 86.9 reduce-scatter.7

commit v3 on v2

--- a/solution.py
+++ b/solution.py
@@ -243,7 +243,7 @@
 
 
 FF_HALF = FF // 2
-FF_BLOCK = 512
+FF_BLOCK = 1536
 SLOTS = EXPERTS * CAP
 
 
@@ -317,7 +317,7 @@
 
 
 def second_half_kernel(
-    rows_ref, graw_ref, dout_ref, gcol_ref, out_in, drow_in, key_ref, w_in_ref, w_out_ref, *rest
+    rows_ref, graw_ref, dout_ref, gcol_ref, out_in, drow_in, key_ref, mine_ref, w_in_ref, w_out_ref, *rest
 ):
     act_ref, dhid_ref, out_ref, drow_ref, dgate_ref, out_acc, drow_acc = rest[-7:]
     out_acc[...] = out_in[...]
@@ -331,7 +331,8 @@
 
         @pl.when(pl.program_id(0) == index)
         def _():
-            picks = pick_slots(key_ref[index : index + 1, :])
+            keys = key_ref[index * EXPERTS : (index + 1) * EXPERTS, :]
+            picks = pick_slots(jnp.sum(jnp.where(mine_ref[...] > 0.0, keys, 0.0), axis=0, keepdims=True))
             dgate_ref[index : index + 1, :] = jnp.sum(jnp.where(picks, dgates, 0.0), axis=0, keepdims=True)
 
 
@@ -529,16 +530,17 @@
     )(*inputs, *earlier)
 
 
-def expert_second(pair, first, keys, w_in, w_out, earlier):
+def expert_second(pair, first, keys, mine, w_in, w_out, earlier):
     rows, graw, dout, gcol, _, _, outs, drows = first
     wide = jax.ShapeDtypeStruct((SLOTS, FF_HALF), BF16)
     narrow = jax.ShapeDtypeStruct((2 * CAP, D), BF16)
-    inputs = [rows, graw, dout, gcol, outs, drows, keys, w_in, w_out]
+    inputs = [rows, graw, dout, gcol, outs, drows, keys, mine, w_in, w_out]
     return pl.pallas_call(
         second_half_kernel,
         grid=(2,),
         in_specs=[slot_spec(pair, width) for width in (D, D, D, 1, D, D)]
-        + [fixed_spec((2, SEQ)), fixed_spec((D, FF_HALF)), fixed_spec((FF_HALF, D), 1)]
+        + [fixed_spec((2 * EXPERTS, SEQ)), fixed_spec((EXPERTS, 1))]
+        + [fixed_spec((D, FF_HALF)), fixed_spec((FF_HALF, D), 1)]
         + [ANY_SPEC] * len(earlier),
         out_specs=[slot_spec(pair, FF_HALF)] * 2 + [slot_spec(0, D)] * 2 + [fixed_spec((8, SEQ))],
         out_shape=[wide, wide, narrow, narrow, jax.ShapeDtypeStruct((8, SEQ), F32)],
@@ -591,20 +593,32 @@
             blocks.append(block)
         return place_blocks(jnp.stack(order).astype(jnp.int32), blocks)
 
-    def sum_over_x(value):
+    def parts_over_x(value):
         value = value.reshape(DEEP, across_x, -1, value.shape[-1])
-        total = lax.dynamic_index_in_dim(value, my_x, 1, keepdims=False).astype(F32)
+        parts = [lax.dynamic_index_in_dim(value, my_x, 1, keepdims=False)]
         for step in range(1, across_x):
             sent = lax.dynamic_index_in_dim(value, (my_x + step) % across_x, 1, keepdims=False)
-            total = total + step_x(sent, step).astype(F32)
-        return total.astype(BF16)
-
-    def sum_over_z(value):
-        total = lax.dynamic_index_in_dim(value, my_z, 0, keepdims=False).astype(F32)
+            parts.append(step_x(sent, step))
+        return parts
+
+    def parts_over_z(value):
+        parts = [lax.dynamic_index_in_dim(value, my_z, 0, keepdims=False)]
         for step in range(1, DEEP):
             sent = lax.dynamic_index_in_dim(value, (my_z + step) % DEEP, 0, keepdims=False)
-            total = total + step_z(sent, step).astype(F32)
+            parts.append(step_z(sent, step))
+        return parts
+
+    def add_parts(parts):
+        total = parts[0].astype(F32)
+        for part in parts[1:]:
+            total = total + part.astype(F32)
         return total
+
+    def sum_over_x(value):
+        return add_parts(parts_over_x(value)).astype(BF16)
+
+    def sum_over_z(value):
+        return add_parts(parts_over_z(value))
 
     def after(values, earlier):
         return lax.optimization_barrier((values, earlier))[0]
@@ -652,13 +666,12 @@
     relation_ids = me ^ expert_ids
 
     def related(rows):
-        return [lax.dynamic_index_in_dim(rows, relation_ids[x], 0, keepdims=False) for x in range(EXPERTS)]
-
-    my_keys = related(keys)
+        chosen = (relation_ids[:, None] == expert_ids[None, :]).astype(F32)
+        return jnp.sum(chosen[:, :, None] * rows[None], axis=1)
+
     all_keys = spread(keys)
-    their_keys = [lax.dynamic_index_in_dim(rows, me, 0, keepdims=False) for rows in all_keys]
     mine_col = (expert_ids == me).astype(F32)[:, None]
-    key_cols = jnp.stack(my_keys, axis=1)
+    key_cols = related(keys).T
 
     bucket_hits = (jnp.arange(BUCKETS, dtype=jnp.int32)[:, None] == buckets[None, :]).astype(BF16)
     bias_vec = lax.dot_general(bias_full, bucket_hits, (((0,), (0,)), ((), ())), preferred_element_type=F32)
@@ -678,7 +691,6 @@
     logits = lax.dot_general(router_weight, act_two, (((0,), (1,)), ((), ())), preferred_element_type=F32)
     prob_all, chosen_sum, gates = route_gates(logits, hits)
 
-    key_pairs = [jnp.stack(their_keys[:2]), jnp.stack(their_keys[2:])]
     all_pairs = [jnp.concatenate(all_keys[:2], axis=0), jnp.concatenate(all_keys[2:], axis=0)]
     router_rows = jnp.pad(router_weight.T, ((0, EXPERTS), (0, 0)))
     first = []
@@ -693,19 +705,20 @@
         return lax.dot_general(left, right, (((0,), (0,)), ((), ())), preferred_element_type=F32).astype(BF16)
 
     grad_in_first = weight_grad(rows, dhid_first)
-    sum_in_first = lax.psum_scatter(grad_in_first, "shard", scatter_dimension=0, tiled=True)
-    far = expert_second(1, first, after(key_pairs[1], grad_in_first), half_in[1], full_out, [])
-    near = expert_second(0, first, key_pairs[0], half_in[1], full_out, far[:2])
+    sum_in_first = sum_over_x(grad_in_first)
+    far = expert_second(1, first, after(all_pairs[1], grad_in_first), mine_col, half_in[1], full_out, [])
+    near = expert_second(0, first, after(all_pairs[0], sum_in_first), mine_col, half_in[1], full_out, far[:2])
+    sum_in_first = sum_over_z(sum_in_first).astype(BF16)
     act_second, dhid_second = near[:2]
     dgate_parts = [swap(row, x) for x, row in enumerate([near[4][0], near[4][1], far[4][0], far[4][1]])]
     across_one = swap(far[3][:CAP], 2)
     across_two = swap(far[3][CAP:], 2)
 
-    act_first, act_second = after((act_first, act_second), across_one)
+    act_first, act_second = after((act_first, act_second), (across_one, across_two, sum_in_first))
     grad_out = jnp.concatenate([weight_grad(act_first, dout), weight_grad(act_second, dout)], axis=0)
     sum_out = lax.psum_scatter(grad_out, "shard", scatter_dimension=0, tiled=True)
-    grad_in_second = weight_grad(rows, after(dhid_second, (grad_out, across_two, sum_in_first)))
-    sum_in_second = lax.psum_scatter(grad_in_second, "shard", scatter_dimension=0, tiled=True)
+    grad_in_second = weight_grad(rows, after(dhid_second, grad_out))
+    in_second_x = parts_over_x(grad_in_second)
 
     def send_back(near_rows, across_one, across_two):
         return [near_rows[:CAP], swap(near_rows[CAP:], 1), across_one, swap(across_two, 1)]
@@ -726,7 +739,7 @@
             out = lax.dynamic_update_index_in_dim(out, parts[x], relation_ids[x], 0)
         return out
 
-    grad_gates = jnp.stack(related(jnp.stack(dgate_parts, axis=0)), axis=0)
+    grad_gates = related(jnp.stack(dgate_parts, axis=0))
     weighted = jnp.sum(grad_gates * gates, axis=0, keepdims=True)
     grad_prob = hits * (grad_gates - weighted) / chosen_sum
     grad_logits = (prob_all * (grad_prob - jnp.sum(prob_all * grad_prob, axis=0, keepdims=True))).astype(BF16)
@@ -739,12 +752,13 @@
     grad_split, grad_lines = attend_backward(
         qkv_rows, attended, grad_attended, totals, seg_col, seg_row, lines
     )
-    grad_split, out_far, sum_out = lax.optimization_barrier((grad_split, out_far, sum_out))
+    grad_split, out_far, in_second_x = lax.optimization_barrier((grad_split, out_far, in_second_x))
+    in_second_z = parts_over_z(add_parts(in_second_x).astype(BF16))
     grad_qkv_weight, grad_tokens, grad_gain_one = qkv_back(
         act_one, grad_split, packed, tokens, gain_one[None], grad_residual
     )
+    grad_qkv_weight, sum_out = lax.optimization_barrier((grad_qkv_weight, sum_out))
     mixed_out = mix_rows(key_cols, residual, send_back(near[2], out_far[:CAP], out_far[CAP:]))
-    grad_w_out = place([sum_out])
     grad_table = lax.dot_general(
         bucket_hits.astype(F32), bias_line_grads(grad_lines), (((1,), (1,)), ((), ())), precision=HIGHEST
     )
@@ -761,10 +775,12 @@
     kept = lax.dynamic_index_in_dim(packed, core, 1, keepdims=False)
     sent = lax.dynamic_index_in_dim(packed, 1 - core, 1, keepdims=False)
     kept = (kept.astype(F32) + swap(sent, 1).astype(F32)).astype(BF16)
-    kept, mixed_out, grad_tokens, grad_w_out = lax.optimization_barrier(
-        (sum_over_x(kept), mixed_out, grad_tokens, grad_w_out)
-    )
-    kept, sum_in_second = lax.optimization_barrier((sum_over_z(kept), sum_in_second))
+    kept, mixed_out, grad_tokens, in_second_z = lax.optimization_barrier(
+        (sum_over_x(kept), mixed_out, grad_tokens, in_second_z)
+    )
+    sum_in_second = add_parts(in_second_z).astype(BF16)
+    grad_w_out = place([sum_out])
+    kept = sum_over_z(kept)
     grad_w_in = place([sum_in_first, sum_in_second])
     if dp_size > EXPERTS:
         total = lax.all_gather(kept, "dp", axis=0).reshape((-1, 2) + kept.shape)

time: 612 us -> 557 us (0.910)
  waiting for transfers between devices: 195 us -> 147 us
  starting transfers between devices: 45.9 us -> 61.3 us
  Pallas kernels: 206 us -> 194 us
  other arithmetic: 33.5 us -> 26.9 us
    ppermute x32, waiting for transfers between devices: 73.1 us -> 53 us  [swap(): lax.ppermute(value, 'dp', [(i, i ^ relation) for i in range(dp_size)])]
    reduce_scatter x1, waiting for transfers between devices: 30.5 us -> 12.7 us  [body(): lax.psum_scatter(grad_out, 'shard', scatter_dimension=0, tiled=True)]
    ppermute x6 -> x12, starting transfers between devices: 6.81 us -> 15.6 us  [step_z(): return lax.ppermute(value, 'shard', pairs)]
    ppermute x5 -> x7, waiting for transfers between devices: 32.4 us -> 24.4 us  [step_x(): return lax.ppermute(value, 'shard', pairs)]
    pallas_call x2, Pallas kernels: 58 us -> 50.2 us  [expert_first(): pl.pallas_call(first_half_kernel, grid=(2,), in_specs=[fixed_spec((SEQ, D...]
    ppermute x6 -> x12, waiting for transfers between devices: 58.5 us -> 57.3 us  [step_z(): return lax.ppermute(value, 'shard', pairs)]
    unnamed x78 -> x102, local copies, waits for them, and re-layouts: 12.6 us -> 13 us
  transfers between devices with their start and end apart: 49 -> 55, of which waited for: 19 -> 22; matrix products, arithmetic and copies ran while one was open for 17% -> 15% of each run, Pallas kernels for 28% -> 35%
where the time goes in v3:
time: 557 us; the launch traced here: 547 us
  Pallas kernels  194 us (35%)
  waiting for transfers between devices  147 us (26%)
  starting transfers between devices  61.3 us (11%)
  matrix products  55.8 us (10%)
  local copies, waits for them, and re-layouts  38.5 us (7%)
  other arithmetic  26.9 us (5%)
  between operations  23.2 us (4%)
    ppermute x12, waiting for transfers between devices, step_z(): return lax.ppermute(value, 'shard', pairs)  57.3 us
    ppermute x32, waiting for transfers between devices, swap(): lax.ppermute(value, 'dp', [(i, i ^ relation) for i in range(dp_size)])  53 us
    pallas_call x2, Pallas kernels, expert_first(): pl.pallas_call(first_half_kernel, grid=(2,), in_specs=[fixed_spec((SEQ, D...  50.2 us
    pallas_call x2, Pallas kernels, expert_second(): pl.pallas_call(second_half_kernel, grid=(2,), in_specs=[slot_spec(pair, w...  44.7 us
    ppermute x32, starting transfers between devices, swap(): lax.ppermute(value, 'dp', [(i, i ^ relation) for i in range(dp_size)])  36.8 us
    dot_general x4, matrix products, weight_grad(): lax.dot_general(left, right, (((0,), (0,)), ((), ())), preferred_element_...  36.2 us
    pallas_call x1, Pallas kernels, attend_backward(): pl.pallas_call(attention_back_kernel, grid=(PAIRS,), in_specs=[pair_spec(...  31.8 us
    pallas_call x1, Pallas kernels, attend_forward(): pl.pallas_call(attention_kernel, grid=(PAIRS,), in_specs=[pair_spec(0), p...  28.3 us
  transfers between devices with their start and end apart: 55, of which 22 were waited for; matrix products, arithmetic and copies ran while one was open for 15% of the time, Pallas kernels for 35%

profile of v3, /device:TPU:9, one launch (start us, length us, event | category | flops | bytes accessed | tf_op | source)
XLA Modules:
  0.0 547.3 jit_solution(4890581354852578498)
XLA Ops:
  15.2 3.2 collective-permute-done.1.refs_2_
  19.6 27.1 %collective-permute-done.3.refs_4_ = bf16[48,3200]{1,0:T(8,128)(2,1)S(1)} collective-permute-done((bf16[48,3200]{1,0:T(8,128)(2,1)S(1)}, bf16[48,3200]{1,0:T(8,128)(2,1)S(1)}, u32[]{:S(2)}, u32[]{:S(2)}) %collective-permute-start.3) | collective-permute-done | bytes 307232 | tf_op jit(solution)/shard_map/ppermute | solution.py:576
  50.8 3.2 collective-permute-done.4.refs_5_
  54.0 11.1 %collective-permute-done.6.refs_7_ = bf16[48,3200]{1,0:T(8,128)(2,1)} collective-permute-done((bf16[48,3200]{1,0:T(8,128)(2,1)S(1)}, bf16[48,3200]{1,0:T(8,128)(2,1)}, u32[]{:S(2)}, u32[]{:S(2)}) %collective-permute-start.6) | collective-permute-done | bytes 307232 | tf_op jit(solution)/shard_map/ppermute | solution.py:582
  67.7 6.6 %collective-permute-start.7 = (bf16[8,48,3200]{2,1,0:T(8,128)(2,1)}, bf16[8,48,3200]{2,1,0:T(8,128)(2,1)}, u32[]{:S(2)}, u32[]{:S(2)}) collective-permute-start(bf16[8,48,3200]{2,1,0:T(8,128)(2,1)} %place_blocks.1), channel_id=1, source_target_pairs={{0,8},{8,0},{16,24},{24,16},{1,9},{9,1},{17,25},{25,17},{2,10},{10... | collective-permute-start | bytes 7372808 | tf_op jit(solution)/shard_map/ppermute | solution.py:566
  79.0 2.9 select_bitcast_fusion.1
  88.4 8.0 %convolution_convert_fusion.q_ref.k_ref.v_ref = bf16[1024,2304]{1,0:T(8,128)(2,1)} fusion(bf16[1024,768]{1,0:T(8,128)(2,1)S(1)} %fusion.7.act_ref, bf16[768,3200]{1,0:T(8,128)(2,1)} %bitcast.13.weight_ref), kind=kOutput, calls=%fused_computation.2 | convolution fusion | flops 3626237952 | bytes 9830400 | tf_op jit(solution)/shard_map/dot_general | solution.py:684
  96.4 28.3 %attend_forward.1 = (bf16[1024,768]{1,0:T(8,128)(2,1)S(1)}, f32[6,8,1024]{2,1,0:T(8,128)S(1)}) custom-call(bf16[1024,2304]{1,0:T(8,128)(2,1)} %convolution_convert_fusion.q_ref.k_ref.v_ref, bf16[1024,2304]{1,0:T(8,128)(2,1)} %convolution_convert_fusion.q_ref.k_ref.v_ref, bf16[1024,2304]{1,0:T(8,128)(2,1)} %convolution_convert_fusion.q_ref.k_ref.v_ref, ...), custom_call_target="tpu_custom_call" | custom-call | flops 12582912 | bytes 24576 | tf_op jit(solution)/shard_map/attend_forward/pallas_call | solution.py:181
  124.8 3.5 multiply_reduce_fusion
  133.1 32.9 %collective-permute-done.8.act_one_ref = bf16[1024,768]{1,0:T(8,128)(2,1)} collective-permute-done((bf16[1024,768]{1,0:T(8,128)(2,1)}, bf16[1024,768]{1,0:T(8,128)(2,1)}, u32[]{:S(2)}, u32[]{:S(2)}) %collective-permute-start.8) | collective-permute-done | bytes 1572896 | tf_op jit(solution)/shard_map/ppermute | solution.py:566
  177.6 24.7 %expert_first.2 = (bf16[2560,768]{1,0:T(8,128)(2,1)}, bf16[2560,768]{1,0:T(8,128)(2,1)}, bf16[2560,768]{1,0:T(8,128)(2,1)}, f32[2560,1]{1,0:T(8,128)}, bf16[2560...) custom-call(bf16[1024,768]{1,0:T(8,128)(2,1)} %multiply_convert_fusion.act_one_ref, ...), custom_call_target="tpu_custom_call" | custom-call | flops 47185920 | bytes 56832 | tf_op jit(solution)/shard_map/expert_first/pallas_call | solution.py:517
  203.5 25.4 %expert_first.3 = (bf16[2560,768]{1,0:T(8,128)(2,1)}, bf16[2560,768]{1,0:T(8,128)(2,1)}, bf16[2560,768]{1,0:T(8,128)(2,1)}, f32[2560,1]{1,0:T(8,128)}, bf16[2560...) custom-call(bf16[1024,768]{1,0:T(8,128)(2,1)} %collective-permute-do, ...), custom_call_target="tpu_custom_call", output_to_operand_aliasing={{0}: (9, {}), {1}: (10, {}), {2}: (11, {}), {3}: (12, {}), ... | custom-call | flops 47185920 | bytes 56832 | tf_op jit(solution)/shard_map/expert_first/pallas_call | solution.py:517
  228.9 10.1 %convolution_convert_fusion.4 = bf16[768,1536]{1,0:T(8,128)(2,1)S(1)} fusion(bf16[2560,768]{1,0:T(8,128)(2,1)} %get-tuple-element.76.rows_ref, bf16[2560,1536]{1,0:T(8,128)(2,1)} %get-tuple-element.82), kind=kOutput, calls=%fused_computation.17 | convolution fusion | flops 6040977408 | bytes 14155776 | tf_op jit(solution)/shard_map/dot_general | solution.py:705
  242.6 22.1 %expert_second.2 = (bf16[2560,1536]{1,0:T(8,128)(2,1)}, bf16[2560,1536]{1,0:T(8,128)(2,1)}, bf16[1280,768]{1,0:T(8,128)(2,1)}, bf16[1280,768]{1,0:T(8,128)(2,1)}, f32[8,1024]{1,0:T(8,128)}) custom-call(bf16[2560,768]{1,0:T(8,128)(2,1)} %get-tuple-element.76.rows_ref, bf16[2560,768]{1,0:T(8,128)(2,1)} %get-tuple-element.77.graw_ref, ...), custom_call_target="tpu_custom_call" | custom-call | flops 47185920 | bytes 56832 | tf_op jit(solution)/shard_map/expert_second/pallas_call | solution.py:538
  271.4 4.0 collective-permute-start.26
  276.9 22.6 %expert_second.3 = (bf16[2560,1536]{1,0:T(8,128)(2,1)}, bf16[2560,1536]{1,0:T(8,128)(2,1)}, bf16[1280,768]{1,0:T(8,128)(2,1)}, bf16[1280,768]{1,0:T(8,128)(2,1)}, f32[8,1024]{1,0:T(8,128)}) custom-call(bf16[2560,768]{1,0:T(8,128)(2,1)} %get-tuple-element.76.rows_ref, ...), custom_call_target="tpu_custom_call", output_to_operand_aliasing={{0}: (10, {}), {1}: (11, {})} | custom-call | flops 47185920 | bytes 56832 | tf_op jit(solution)/shard_map/expert_second/pallas_call | solution.py:538
  304.4 7.0 %collective-permute-done.22.three_ref = bf16[640,768]{1,0:T(8,128)(2,1)S(1)} collective-permute-done((bf16[640,768]{1,0:T(8,128)(2,1)S(1)}, bf16[640,768]{1,0:T(8,128)(2,1)S(1)}, u32[]{:S(2)}, u32[]{:S(2)}) %collective-permute-start.22) | collective-permute-done | bytes 983072 | tf_op jit(solution)/shard_map/ppermute | solution.py:566
  311.4 8.9 %convolution_convert_fusion.3 = bf16[1536,768]{1,0:T(8,128)(2,1)S(1)} fusion(bf16[2560,1536]{1,0:T(8,128)(2,1)} %get-tuple-element.95, bf16[2560,768]{1,0:T(8,128)(2,1)S(1)} %copy-done.22), kind=kOutput, calls=%fused_computation.16 | convolution fusion | flops 6040977408 | bytes 14155776 | tf_op jit(solution)/shard_map/dot_general | solution.py:705
  320.3 6.9 %convolution_convert_fusion.2 = bf16[1536,768]{1,0:T(8,128)(2,1)S(1)} fusion(bf16[2560,1536]{1,0:T(8,128)(2,1)S(1)} %bitcast.170, bf16[2560,768]{1,0:T(8,128)(2,1)S(1)} %copy-done.22), kind=kOutput, calls=%fused_computation.15 | convolution fusion | flops 6040977408 | bytes 14155776 | tf_op jit(solution)/shard_map/dot_general | solution.py:705
  339.6 10.4 %convolution_convert_fusion.1 = bf16[768,1536]{1,0:T(8,128)(2,1)S(1)} fusion(bf16[2560,768]{1,0:T(8,128)(2,1)} %get-tuple-element.76.rows_ref, bf16[2560,1536]{1,0:T(8,128)(2,1)} %get-tuple-element.97), kind=kOutput, calls=%fused_computation.14 | convolution fusion | flops 6040977408 | bytes 14155776 | tf_op jit(solution)/shard_map/dot_general | solution.py:705
  353.6 3.3 fusion.23.extra_ref
  357.0 15.4 %token_back.1 = (f32[1024,768]{1,0:T(8,128)S(1)}, bf16[1024,768]{1,0:T(8,128)(2,1)S(1)}, bf16[768,768]{1,0:T(8,128)(2,1)S(1)}, f32[1,768]{1,0:T(1,128)S(1)}) custom-call(f32[1024,4]{1,0:T(8,128)S(1)} %bitcast.155, f32[1024,768]{1,0:T(8,128)} %fusion.23.extra_ref, f32[1024,768]{1,0:T(8,128)} %copy-done.2, bf16[1024,768]{1,0:T(8,128)(2,1)} %cot_ref.1, ...), custom_call_target="tpu_custom_call" | custom-call | flops 25165824 | bytes 70656 | tf_op jit(solution)/shard_map/token_back/pallas_call | solution.py:435
  375.1 31.8 %attend_backward.1 = (bf16[3,1024,768]{2,1,0:T(8,128)(2,1)}, f32[6,8,512]{2,1,0:T(8,128)S(1)}) custom-call(bf16[1024,2304]{1,0:T(8,128)(2,1)} %convolution_convert_fusion.q_ref.k_ref.v_ref, bf16[1024,2304]{1,0:T(8,128)(2,1)} %convolution_convert_fusion.q_ref.k_ref.v_ref, bf16[1024,2304]{1,0:T(8,128)(2,1)} %convolution_convert_fusion.q_ref.k_ref.v_ref, ...), custom_call_target="tpu_custom_call" | custom-call | flops 31457280 | bytes 49152 | tf_op jit(solution)/shard_map/attend_backward/pallas_call | solution.py:198
  407.6 14.3 %qkv_back.1 = (bf16[768,2304]{1,0:T(8,128)(2,1)}, bf16[1024,768]{1,0:T(8,128)(2,1)}, f32[1,768]{1,0:T(1,128)S(1)}) custom-call(bf16[1024,768]{1,0:T(8,128)(2,1)S(1)} %copy-done.10, bf16[3,1024,768]{2,1,0:T(8,128)(2,1)} %get-tuple-element.103.split_ref, bf16[768,3200]{1,0:T(8,128)(2,1)} %bitcast.13.weight_ref, bf16[1024,768]{1,0:T(8,128)(2,1)S(1)} %copy-done.6, ...), custom_call_target="tpu_custom_call" | custom-call | flops 28311552 | bytes 76800 | tf_op jit(solution)/shard_map/qkv_back/pallas_call | solution.py:478
  422.1 12.7 %reduce-scatter.2.cloned.1.call-done = bf16[384,768]{1,0:T(8,128)(2,1)} async-done(((bf16[3072,768]{1,0:T(8,128)(2,1)}), bf16[384,768]{1,0:T(8,128)(2,1)}) %reduce-scatter.2.cloned.1.call-update) | async-done | bytes 589840 | tf_op jit(solution)/shard_map/reduce_scatter | solution.py:719
  434.8 3.1 fusion.1
  461.6 6.8 %mix_rows.1 = bf16[1024,768]{1,0:T(8,128)(2,1)} custom-call(f32[1024,4]{1,0:T(8,128)S(1)} %bitcast.156, f32[1024,768]{1,0:T(8,128)S(1)} %copy-done.3, bf16[640,768]{1,0:T(8,128)(2,1)S(1)} %get-tuple-element.190.one_ref, bf16[640,768]{1,0:T(8,128)(2,1)S(1)} %collective-permute-done.32.two_ref, bf16[640,768]{1,0:T(8,128)(2,1)S(1)} %get-tuple-element.188.three_ref, ...), custom_call_target="tpu_custom_call" | custom-call | flops 15728640 | bytes 33792 | tf_op jit(solution)/shard_map/mix_rows/pallas_call | solution.py:385
  477.0 10.1 %collective-permute-done.31 = bf16[4,48,3200]{2,1,0:T(8,128)(2,1)S(1)} collective-permute-done((bf16[4,48,3200]{2,1,0:T(8,128)(2,1)S(1)}, bf16[4,48,3200]{2,1,0:T(8,128)(2,1)S(1)}, u32[]{:S(2)}, u32[]{:S(2)}) %collective-permute-start.31) | collective-permute-done | bytes 1228832 | tf_op jit(solution)/shard_map/ppermute | solution.py:582
  487.4 4.9 collective-permute-done.35
  503.2 3.1 collective-permute-start.43
  506.4 14.3 %collective-permute-done.38 = bf16[48,3200]{1,0:T(8,128)(2,1)S(1)} collective-permute-done((bf16[48,3200]{1,0:T(8,128)(2,1)S(1)}, bf16[48,3200]{1,0:T(8,128)(2,1)S(1)}, u32[]{:S(2)}, u32[]{:S(2)}) %collective-permute-start.38) | collective-permute-done | bytes 307232 | tf_op jit(solution)/shard_map/ppermute | solution.py:576
  525.1 7.9 %collective-permute-done.40 = bf16[48,3200]{1,0:T(8,128)(2,1)S(1)} collective-permute-done((bf16[48,3200]{1,0:T(8,128)(2,1)S(1)}, bf16[48,3200]{1,0:T(8,128)(2,1)S(1)}, u32[]{:S(2)}, u32[]{:S(2)}) %collective-permute-start.40) | collective-permute-done | bytes 307232 | tf_op jit(solution)/shard_map/ppermute | solution.py:566
  (304 shorter events, 127.4 us)
Async XLA Ops:
  7.3 169.2 %all-gather.5.cloned.1.call-start = ((), (), s32[]{:S(2)}) async-start(), calls=%async_computation.1 | async-start | bytes 2654208 | tf_op jit(solution)/shard_map/all_gather | solution.py:652
  9.8 166.7 %all-gather.9.cloned.1.call-start = ((), (), s32[]{:S(2)}) async-start(), calls=%async_computation.4 | async-start | bytes 5308416 | tf_op jit(solution)/shard_map/all_gather | solution.py:653
  11.5 35.2 %collective-permute-start.3 = (bf16[48,3200]{1,0:T(8,128)(2,1)S(1)}, bf16[48,3200]{1,0:T(8,128)(2,1)S(1)}, u32[]{:S(2)}, u32[]{:S(2)}) collective-permute-start(bf16[48,3200]{1,0:T(8,128)(2,1)S(1)} %fusion.20.refs_0_), channel_id=1, source_target_pairs={{0,4},{1,5},{2,6},{3,7},{4,0},{5,1},{6,2},{7,3},{8,12},{9,13},{10,... | collective-permute-start | bytes 921608 | tf_op jit(solution)/shard_map/ppermute | solution.py:576
  12.6 36.9 %collective-permute-start.5 = (bf16[48,3200]{1,0:T(8,128)(2,1)S(1)}, bf16[48,3200]{1,0:T(8,128)(2,1)S(1)}, u32[]{:S(2)}, u32[]{:S(2)}) collective-permute-start(bf16[48,3200]{1,0:T(8,128)(2,1)S(1)} %fusion.20.refs_0_), channel_id=1, source_target_pairs={{0,6},{1,7},{2,0},{3,1},{4,2},{5,3},{6,4},{7,5},{8,14},{9,15},{10,... | collective-permute-start | bytes 921608 | tf_op jit(solution)/shard_map/ppermute | solution.py:576
  14.0 36.8 %collective-permute-start = (bf16[48,3200]{1,0:T(8,128)(2,1)S(1)}, bf16[48,3200]{1,0:T(8,128)(2,1)S(1)}, u32[]{:S(2)}, u32[]{:S(2)}) collective-permute-start(bf16[48,3200]{1,0:T(8,128)(2,1)S(1)} %fusion.20.refs_0_), channel_id=1, source_target_pairs={{0,1},{1,0},{2,3},{3,2},{4,5},{5,4},{6,7},{7,6},{8,9},{9,8},{10,11... | collective-permute-start | bytes 921608 | tf_op jit(solution)/shard_map/ppermute | solution.py:582
  18.3 32.5 %collective-permute-start.2 = (bf16[48,3200]{1,0:T(8,128)(2,1)S(1)}, bf16[48,3200]{1,0:T(8,128)(2,1)S(1)}, u32[]{:S(2)}, u32[]{:S(2)}) collective-permute-start(bf16[48,3200]{1,0:T(8,128)(2,1)S(1)} %collective-permute-done.1.refs_2_), channel_id=1, source_target_pairs={{0,1},{1,0},{2,3},{3,2},{4,5},{5,4},{6,7},{7,6},{8,9},{9,8},{10,11... | collective-permute-start | bytes 921608 | tf_op jit(solution)/shard_map/ppermute | solution.py:582
  76.3 166.3 %all-gather.7.cloned.1.call-start = ((), (), s32[]{:S(2)}) async-start(), calls=%async_computation.2 | async-start | bytes 2654208 | tf_op jit(solution)/shard_map/all_gather | solution.py:654
  76.3 56.1 %collective-permute-start.10 = (bf16[1024,768]{1,0:T(8,128)(2,1)}, bf16[1024,768]{1,0:T(8,128)(2,1)}, u32[]{:S(2)}, u32[]{:S(2)}) collective-permute-start(bf16[1024,768]{1,0:T(8,128)(2,1)} %cot_ref.1), channel_id=1, source_target_pairs={{0,16},{8,24},{16,0},{24,8},{1,17},{9,25},{17,1},{25,9},{2,18},{10... | collective-permute-start | bytes 4718600 | tf_op jit(solution)/shard_map/ppermute | solution.py:566
  130.0 35.9 %collective-permute-start.8 = (bf16[1024,768]{1,0:T(8,128)(2,1)}, bf16[1024,768]{1,0:T(8,128)(2,1)}, u32[]{:S(2)}, u32[]{:S(2)}) collective-permute-start(bf16[1024,768]{1,0:T(8,128)(2,1)} %multiply_convert_fusion.act_one_ref), channel_id=1, source_target_pairs={{0,16},{8,24},{16,0},{24,8},{1,17},{9,25},{17,1},{25,9},{2,18},{10... | collective-permute-start | bytes 4718600 | tf_op jit(solution)/shard_map/ppermute | solution.py:566
  131.3 45.1 %collective-permute-start.15 = (bf16[1024,768]{1,0:T(8,128)(2,1)}, bf16[1024,768]{1,0:T(8,128)(2,1)}, u32[]{:S(2)}, u32[]{:S(2)}) collective-permute-start(bf16[1024,768]{1,0:T(8,128)(2,1)} %cot_ref.1), channel_id=1, source_target_pairs={{0,8},{8,0},{16,24},{24,16},{1,9},{9,1},{17,25},{25,17},{2,10},{10... | collective-permute-start | bytes 4718600 | tf_op jit(solution)/shard_map/ppermute | solution.py:566
  132.0 302.8 %reduce-scatter.2.cloned.1.call-start = ((), (), s32[]{:S(2)}) async-start(), calls=%async_computation.3 | async-start | bytes 5308416 | tf_op jit(solution)/shard_map/reduce_scatter | solution.py:719
  132.5 69.8 %collective-permute-start.11 = (bf16[1024,768]{1,0:T(8,128)(2,1)}, bf16[1024,768]{1,0:T(8,128)(2,1)S(1)}, u32[]{:S(2)}, u32[]{:S(2)}) collective-permute-start(bf16[1024,768]{1,0:T(8,128)(2,1)} %collective-permute-done.10.cot_one_ref), channel_id=1, source_target_pairs={{0,8},{8,0},{16,24},{24,16},{1,9},{9,1},{17,25},{25,17},{2,10},{10... | collective-permute-start | bytes 4718600 | tf_op jit(solution)/shard_map/ppermute | solution.py:566
  132.6 43.8 %collective-permute-start.14 = (bf16[1024,768]{1,0:T(8,128)(2,1)}, bf16[1024,768]{1,0:T(8,128)(2,1)S(1)}, u32[]{:S(2)}, u32[]{:S(2)}) collective-permute-start(bf16[1024,768]{1,0:T(8,128)(2,1)} %multiply_convert_fusion.act_one_ref), channel_id=1, source_target_pairs={{0,8},{8,0},{16,24},{24,16},{1,9},{9,1},{17,25},{25,17},{2,10},{10... | collective-permute-start | bytes 4718600 | tf_op jit(solution)/shard_map/ppermute | solution.py:566
  166.0 36.4 %collective-permute-start.9 = (bf16[1024,768]{1,0:T(8,128)(2,1)}, bf16[1024,768]{1,0:T(8,128)(2,1)}, u32[]{:S(2)}, u32[]{:S(2)}) collective-permute-start(bf16[1024,768]{1,0:T(8,128)(2,1)} %collective-permute-done.8.act_one_ref), channel_id=1, source_target_pairs={{0,8},{8,0},{16,24},{24,16},{1,9},{9,1},{17,25},{25,17},{2,10},{10... | collective-permute-start | bytes 4718600 | tf_op jit(solution)/shard_map/ppermute | solution.py:566
  240.5 28.4 %collective-permute-start.17 = (bf16[4,96,1536]{2,1,0:T(8,128)(2,1)S(1)}, bf16[4,96,1536]{2,1,0:T(8,128)(2,1)}, u32[]{:S(2)}, u32[]{:S(2)}) collective-permute-start(bf16[4,96,1536]{2,1,0:T(8,128)(2,1)S(1)} %dynamic-slice_bitcast_fusion.4), channel_id=1, source_target_pairs={{0,1},{1,0},{2,3},{3,2},{4,5},{5,4},{6,7},{7,6},{8,9},{9,8},{10,11... | collective-permute-start | bytes 3538952 | tf_op jit(solution)/shard_map/ppermute | solution.py:582
  267.4 36.9 %collective-permute-start.23 = (bf16[640,768]{1,0:T(8,128)(2,1)}, bf16[640,768]{1,0:T(8,128)(2,1)}, u32[]{:S(2)}, u32[]{:S(2)}) collective-permute-start(bf16[640,768]{1,0:T(8,128)(2,1)} %get-tuple-element.191), channel_id=1, source_target_pairs={{0,16},{8,24},{16,0},{24,8},{1,17},{9,25},{17,1},{25,9},{2,18},{10... | collective-permute-start | bytes 2949128 | tf_op jit(solution)/shard_map/ppermute | solution.py:566
  268.8 42.6 %collective-permute-start.22 = (bf16[640,768]{1,0:T(8,128)(2,1)S(1)}, bf16[640,768]{1,0:T(8,128)(2,1)S(1)}, u32[]{:S(2)}, u32[]{:S(2)}) collective-permute-start(bf16[640,768]{1,0:T(8,128)(2,1)S(1)} %get-tuple-element.192), channel_id=1, source_target_pairs={{0,16},{8,24},{16,0},{24,8},{1,17},{9,25},{17,1},{25,9},{2,18},{10... | collective-permute-start | bytes 2949128 | tf_op jit(solution)/shard_map/ppermute | solution.py:566
  271.4 28.1 %collective-permute-start.25 = (bf16[96,1536]{1,0:T(8,128)(2,1)}, bf16[96,1536]{1,0:T(8,128)(2,1)}, u32[]{:S(2)}, u32[]{:S(2)}) collective-permute-start(bf16[96,1536]{1,0:T(8,128)(2,1)} %get-tuple-element.204), channel_id=1, source_target_pairs={{0,2},{1,3},{2,4},{3,5},{4,6},{5,7},{6,0},{7,1},{8,10},{9,11},{10,... | collective-permute-start | bytes 884744 | tf_op jit(solution)/shard_map/ppermute | solution.py:576
  271.4 28.1 %collective-permute-start.26 = (bf16[96,1536]{1,0:T(8,128)(2,1)}, bf16[96,1536]{1,0:T(8,128)(2,1)}, u32[]{:S(2)}, u32[]{:S(2)}) collective-permute-start(bf16[96,1536]{1,0:T(8,128)(2,1)} %get-tuple-element.206), channel_id=1, source_target_pairs={{0,4},{1,5},{2,6},{3,7},{4,0},{5,1},{6,2},{7,3},{8,12},{9,13},{10,... | collective-permute-start | bytes 884744 | tf_op jit(solution)/shard_map/ppermute | solution.py:576
  275.4 26.8 %collective-permute-start.27 = (bf16[96,1536]{1,0:T(8,128)(2,1)S(1)}, bf16[96,1536]{1,0:T(8,128)(2,1)}, u32[]{:S(2)}, u32[]{:S(2)}) collective-permute-start(bf16[96,1536]{1,0:T(8,128)(2,1)S(1)} %get-tuple-element.205), channel_id=1, source_target_pairs={{0,6},{1,7},{2,0},{3,1},{4,2},{5,3},{6,4},{7,5},{8,14},{9,15},{10,... | collective-permute-start | bytes 884744 | tf_op jit(solution)/shard_map/ppermute | solution.py:576
  333.8 73.7 %collective-permute-start.28 = (bf16[1280,768]{1,0:T(8,128)(2,1)}, bf16[1280,768]{1,0:T(8,128)(2,1)}, u32[]{:S(2)}, u32[]{:S(2)}) collective-permute-start(bf16[1280,768]{1,0:T(8,128)(2,1)} %get-tuple-element.102), channel_id=1, source_target_pairs={{0,16},{8,24},{16,0},{24,8},{1,17},{9,25},{17,1},{25,9},{2,18},{10... | collective-permute-start | bytes 5898248 | tf_op jit(solution)/shard_map/ppermute | solution.py:566
  335.1 21.8 %collective-permute-start.24 = (bf16[640,768]{1,0:T(8,128)(2,1)}, bf16[640,768]{1,0:T(8,128)(2,1)S(1)}, u32[]{:S(2)}, u32[]{:S(2)}) collective-permute-start(bf16[640,768]{1,0:T(8,128)(2,1)} %collective-permute-done.23), channel_id=1, source_target_pairs={{0,8},{8,0},{16,24},{24,16},{1,9},{9,1},{17,25},{25,17},{2,10},{10... | collective-permute-start | bytes 2949128 | tf_op jit(solution)/shard_map/ppermute | solution.py:566
  351.6 55.9 %collective-permute-start.29 = (bf16[4,96,1536]{2,1,0:T(8,128)(2,1)}, bf16[4,96,1536]{2,1,0:T(8,128)(2,1)}, u32[]{:S(2)}, u32[]{:S(2)}) collective-permute-start(bf16[4,96,1536]{2,1,0:T(8,128)(2,1)} %get-tuple-element.185), channel_id=1, source_target_pairs={{0,1},{1,0},{2,3},{3,2},{4,5},{5,4},{6,7},{7,6},{8,9},{9,8},{10,11... | collective-permute-start | bytes 3538952 | tf_op jit(solution)/shard_map/ppermute | solution.py:582
  459.0 28.0 %collective-permute-start.31 = (bf16[4,48,3200]{2,1,0:T(8,128)(2,1)S(1)}, bf16[4,48,3200]{2,1,0:T(8,128)(2,1)S(1)}, u32[]{:S(2)}, u32[]{:S(2)}) collective-permute-start(bf16[4,48,3200]{2,1,0:T(8,128)(2,1)S(1)} %dynamic-slice_bitcast_fusion.1), channel_id=1, source_target_pairs={{0,1},{1,0},{2,3},{3,2},{4,5},{5,4},{6,7},{7,6},{8,9},{9,8},{10,11... | collective-permute-start | bytes 3686408 | tf_op jit(solution)/shard_map/ppermute | solution.py:582
  460.4 38.7 %collective-permute-start.44 = (bf16[96,1536]{1,0:T(8,128)(2,1)S(1)}, bf16[96,1536]{1,0:T(8,128)(2,1)S(1)}, u32[]{:S(2)}, u32[]{:S(2)}) collective-permute-start(bf16[96,1536]{1,0:T(8,128)(2,1)S(1)} %copy-done.32), channel_id=1, source_target_pairs={{0,16},{8,24},{16,0},{24,8},{1,17},{9,25},{17,1},{25,9},{2,18},{10... | collective-permute-start | bytes 884744 | tf_op jit(solution)/shard_map/ppermute | solution.py:566
  460.7 26.6 %collective-permute-start.34 = (bf16[96,1536]{1,0:T(8,128)(2,1)S(1)}, bf16[96,1536]{1,0:T(8,128)(2,1)S(1)}, u32[]{:S(2)}, u32[]{:S(2)}) collective-permute-start(bf16[96,1536]{1,0:T(8,128)(2,1)S(1)} %get-tuple-element.202), channel_id=1, source_target_pairs={{0,2},{1,3},{2,4},{3,5},{4,6},{5,7},{6,0},{7,1},{8,10},{9,11},{10,... | collective-permute-start | bytes 884744 | tf_op jit(solution)/shard_map/ppermute | solution.py:576
  473.5 20.1 %collective-permute-start.36 = (bf16[96,1536]{1,0:T(8,128)(2,1)S(1)}, bf16[96,1536]{1,0:T(8,128)(2,1)S(1)}, u32[]{:S(2)}, u32[]{:S(2)}) collective-permute-start(bf16[96,1536]{1,0:T(8,128)(2,1)S(1)} %get-tuple-element.200), channel_id=1, source_target_pairs={{0,6},{1,7},{2,0},{3,1},{4,2},{5,3},{6,4},{7,5},{8,14},{9,15},{10,... | collective-permute-start | bytes 884744 | tf_op jit(solution)/shard_map/ppermute | solution.py:576
  495.1 25.6 %collective-permute-start.38 = (bf16[48,3200]{1,0:T(8,128)(2,1)S(1)}, bf16[48,3200]{1,0:T(8,128)(2,1)S(1)}, u32[]{:S(2)}, u32[]{:S(2)}) collective-permute-start(bf16[48,3200]{1,0:T(8,128)(2,1)S(1)} %get-tuple-element.199), channel_id=1, source_target_pairs={{0,4},{1,5},{2,6},{3,7},{4,0},{5,1},{6,2},{7,3},{8,12},{9,13},{10,... | collective-permute-start | bytes 921608 | tf_op jit(solution)/shard_map/ppermute | solution.py:576
  497.0 27.4 %collective-permute-start.39 = (bf16[48,3200]{1,0:T(8,128)(2,1)S(1)}, bf16[48,3200]{1,0:T(8,128)(2,1)S(1)}, u32[]{:S(2)}, u32[]{:S(2)}) collective-permute-start(bf16[48,3200]{1,0:T(8,128)(2,1)S(1)} %get-tuple-element.198), channel_id=1, source_target_pairs={{0,6},{1,7},{2,0},{3,1},{4,2},{5,3},{6,4},{7,5},{8,14},{9,15},{10,... | collective-permute-start | bytes 921608 | tf_op jit(solution)/shard_map/ppermute | solution.py:576
  499.1 25.9 %collective-permute-start.42 = (bf16[96,1536]{1,0:T(8,128)(2,1)S(1)}, bf16[96,1536]{1,0:T(8,128)(2,1)S(1)}, u32[]{:S(2)}, u32[]{:S(2)}) collective-permute-start(bf16[96,1536]{1,0:T(8,128)(2,1)S(1)} %copy-done.32), channel_id=1, source_target_pairs={{0,8},{8,0},{16,24},{24,16},{1,9},{9,1},{17,25},{25,17},{2,10},{10... | collective-permute-start | bytes 884744 | tf_op jit(solution)/shard_map/ppermute | solution.py:566
  501.6 33.1 %collective-permute-start.46 = (bf16[96,1536]{1,0:T(8,128)(2,1)S(1)}, bf16[96,1536]{1,0:T(8,128)(2,1)S(1)}, u32[]{:S(2)}, u32[]{:S(2)}) collective-permute-start(bf16[96,1536]{1,0:T(8,128)(2,1)S(1)} %collective-permute-done.44), channel_id=1, source_target_pairs={{0,8},{8,0},{16,24},{24,16},{1,9},{9,1},{17,25},{25,17},{2,10},{10... | collective-permute-start | bytes 884744 | tf_op jit(solution)/shard_map/ppermute | solution.py:566
  503.2 21.8 %collective-permute-start.43 = (bf16[96,1536]{1,0:T(8,128)(2,1)S(1)}, bf16[96,1536]{1,0:T(8,128)(2,1)S(1)}, u32[]{:S(2)}, u32[]{:S(2)}) collective-permute-start(bf16[96,1536]{1,0:T(8,128)(2,1)S(1)} %add_convert_fusion.1), channel_id=1, source_target_pairs={{0,8},{8,0},{16,24},{24,16},{1,9},{9,1},{17,25},{25,17},{2,10},{10... | collective-permute-start | bytes 884744 | tf_op jit(solution)/shard_map/ppermute | solution.py:566
  (70 other events, 693.3 us)
Sparse Core Ops, SparseCore 0:
  10.8 74.3 all-gather.4
  88.0 78.2 all-gather.8
  169.0 51.2 all-gather.6
  329.8 104.9 reduce-scatter.1

commit v4 on v3

--- a/solution.py
+++ b/solution.py
@@ -708,13 +708,16 @@
     sum_in_first = sum_over_x(grad_in_first)
     far = expert_second(1, first, after(all_pairs[1], grad_in_first), mine_col, half_in[1], full_out, [])
     near = expert_second(0, first, after(all_pairs[0], sum_in_first), mine_col, half_in[1], full_out, far[:2])
-    sum_in_first = sum_over_z(sum_in_first).astype(BF16)
+    in_first_z = parts_over_z(sum_in_first)
     act_second, dhid_second = near[:2]
     dgate_parts = [swap(row, x) for x, row in enumerate([near[4][0], near[4][1], far[4][0], far[4][1]])]
     across_one = swap(far[3][:CAP], 2)
     across_two = swap(far[3][CAP:], 2)
 
-    act_first, act_second = after((act_first, act_second), (across_one, across_two, sum_in_first))
+    act_first, act_second, across_one, across_two, in_first_z = lax.optimization_barrier(
+        (act_first, act_second, across_one, across_two, in_first_z)
+    )
+    sum_in_first = add_parts(in_first_z).astype(BF16)
     grad_out = jnp.concatenate([weight_grad(act_first, dout), weight_grad(act_second, dout)], axis=0)
     sum_out = lax.psum_scatter(grad_out, "shard", scatter_dimension=0, tiled=True)
     grad_in_second = weight_grad(rows, after(dhid_second, grad_out))
@@ -757,7 +760,6 @@
     grad_qkv_weight, grad_tokens, grad_gain_one = qkv_back(
         act_one, grad_split, packed, tokens, gain_one[None], grad_residual
     )
-    grad_qkv_weight, sum_out = lax.optimization_barrier((grad_qkv_weight, sum_out))
     mixed_out = mix_rows(key_cols, residual, send_back(near[2], out_far[:CAP], out_far[CAP:]))
     grad_table = lax.dot_general(
         bucket_hits.astype(F32), bias_line_grads(grad_lines), (((1,), (1,)), ((), ())), precision=HIGHEST
@@ -771,6 +773,7 @@
         [grad_qkv_weight, grad_attn_weight, jnp.pad(small, ((0, 0), (0, 121))).astype(BF16)],
         axis=1,
     )
+    packed, sum_out = lax.optimization_barrier((packed, sum_out))
     packed = packed.reshape(shards, 2, core_rows, packed.shape[1])
     kept = lax.dynamic_index_in_dim(packed, core, 1, keepdims=False)
     sent = lax.dynamic_index_in_dim(packed, 1 - core, 1, keepdims=False)

time: 557 us -> 554 us (level)
    unnamed x102 -> x112, local copies, waits for them, and re-layouts: 13 us -> 11 us
  transfers between devices with their start and end apart: 55 -> 55, of which waited for: 22 -> 21; matrix products, arithmetic and copies ran while one was open for 15% -> 16% of each run, Pallas kernels for 35% -> 36%
where the time goes in v4:
time: 554 us; the launch traced here: 545 us
  Pallas kernels  194 us (35%)
  waiting for transfers between devices  145 us (26%)
  starting transfers between devices  61.9 us (11%)
  matrix products  55.9 us (10%)
  local copies, waits for them, and re-layouts  38.3 us (7%)
  other arithmetic  27.3 us (5%)
  between operations  23.3 us (4%)
    ppermute x32, waiting for transfers between devices, swap(): lax.ppermute(value, 'dp', [(i, i ^ relation) for i in range(dp_size)])  57.9 us
    ppermute x12, waiting for transfers between devices, step_z(): return lax.ppermute(value, 'shard', pairs)  54.7 us
    pallas_call x2, Pallas kernels, expert_first(): pl.pallas_call(first_half_kernel, grid=(2,), in_specs=[fixed_spec((SEQ, D...  50.3 us
    pallas_call x2, Pallas kernels, expert_second(): pl.pallas_call(second_half_kernel, grid=(2,), in_specs=[slot_spec(pair, w...  44.7 us
    ppermute x32, starting transfers between devices, swap(): lax.ppermute(value, 'dp', [(i, i ^ relation) for i in range(dp_size)])  37.3 us
    dot_general x4, matrix products, weight_grad(): lax.dot_general(left, right, (((0,), (0,)), ((), ())), preferred_element_...  36.3 us
    pallas_call x1, Pallas kernels, attend_backward(): pl.pallas_call(attention_back_kernel, grid=(PAIRS,), in_specs=[pair_spec(...  31.8 us
    pallas_call x1, Pallas kernels, attend_forward(): pl.pallas_call(attention_kernel, grid=(PAIRS,), in_specs=[pair_spec(0), p...  28.3 us
  transfers between devices with their start and end apart: 55, of which 21 were waited for; matrix products, arithmetic and copies ran while one was open for 16% of the time, Pallas kernels for 36%

profile of v4, /device:TPU:9, one launch (start us, length us, event | category | flops | bytes accessed | tf_op | source)
XLA Modules:
  0.0 545.3 jit_solution(923170473410303848)
XLA Ops:
  15.2 3.2 collective-permute-done.1.refs_2_
  19.6 27.1 %collective-permute-done.3.refs_4_ = bf16[48,3200]{1,0:T(8,128)(2,1)S(1)} collective-permute-done((bf16[48,3200]{1,0:T(8,128)(2,1)S(1)}, bf16[48,3200]{1,0:T(8,128)(2,1)S(1)}, u32[]{:S(2)}, u32[]{:S(2)}) %collective-permute-start.3) | collective-permute-done | bytes 307232 | tf_op jit(solution)/shard_map/ppermute | solution.py:576
  50.8 3.2 collective-permute-done.4.refs_5_
  54.0 11.1 %collective-permute-done.6.refs_7_ = bf16[48,3200]{1,0:T(8,128)(2,1)} collective-permute-done((bf16[48,3200]{1,0:T(8,128)(2,1)S(1)}, bf16[48,3200]{1,0:T(8,128)(2,1)}, u32[]{:S(2)}, u32[]{:S(2)}) %collective-permute-start.6) | collective-permute-done | bytes 307232 | tf_op jit(solution)/shard_map/ppermute | solution.py:582
  67.7 6.6 %collective-permute-start.7 = (bf16[8,48,3200]{2,1,0:T(8,128)(2,1)}, bf16[8,48,3200]{2,1,0:T(8,128)(2,1)}, u32[]{:S(2)}, u32[]{:S(2)}) collective-permute-start(bf16[8,48,3200]{2,1,0:T(8,128)(2,1)} %place_blocks.1), channel_id=1, source_target_pairs={{0,8},{8,0},{16,24},{24,16},{1,9},{9,1},{17,25},{25,17},{2,10},{10... | collective-permute-start | bytes 7372808 | tf_op jit(solution)/shard_map/ppermute | solution.py:566
  79.0 2.9 select_bitcast_fusion.1
  88.4 8.0 %convolution_convert_fusion.q_ref.k_ref.v_ref = bf16[1024,2304]{1,0:T(8,128)(2,1)} fusion(bf16[1024,768]{1,0:T(8,128)(2,1)S(1)} %fusion.7.act_ref, bf16[768,3200]{1,0:T(8,128)(2,1)} %bitcast.13.weight_ref), kind=kOutput, calls=%fused_computation.2 | convolution fusion | flops 3626237952 | bytes 9830400 | tf_op jit(solution)/shard_map/dot_general | solution.py:684
  96.5 28.3 %attend_forward.1 = (bf16[1024,768]{1,0:T(8,128)(2,1)S(1)}, f32[6,8,1024]{2,1,0:T(8,128)S(1)}) custom-call(bf16[1024,2304]{1,0:T(8,128)(2,1)} %convolution_convert_fusion.q_ref.k_ref.v_ref, bf16[1024,2304]{1,0:T(8,128)(2,1)} %convolution_convert_fusion.q_ref.k_ref.v_ref, bf16[1024,2304]{1,0:T(8,128)(2,1)} %convolution_convert_fusion.q_ref.k_ref.v_ref, ...), custom_call_target="tpu_custom_call" | custom-call | flops 12582912 | bytes 24576 | tf_op jit(solution)/shard_map/attend_forward/pallas_call | solution.py:181
  124.8 3.5 multiply_reduce_fusion
  133.1 32.9 %collective-permute-done.8.act_one_ref = bf16[1024,768]{1,0:T(8,128)(2,1)} collective-permute-done((bf16[1024,768]{1,0:T(8,128)(2,1)}, bf16[1024,768]{1,0:T(8,128)(2,1)}, u32[]{:S(2)}, u32[]{:S(2)}) %collective-permute-start.8) | collective-permute-done | bytes 1572896 | tf_op jit(solution)/shard_map/ppermute | solution.py:566
  177.6 24.8 %expert_first.2 = (bf16[2560,768]{1,0:T(8,128)(2,1)}, bf16[2560,768]{1,0:T(8,128)(2,1)}, bf16[2560,768]{1,0:T(8,128)(2,1)}, f32[2560,1]{1,0:T(8,128)}, bf16[2560...) custom-call(bf16[1024,768]{1,0:T(8,128)(2,1)} %multiply_convert_fusion.act_one_ref, ...), custom_call_target="tpu_custom_call" | custom-call | flops 47185920 | bytes 56832 | tf_op jit(solution)/shard_map/expert_first/pallas_call | solution.py:517
  203.6 25.4 %expert_first.3 = (bf16[2560,768]{1,0:T(8,128)(2,1)}, bf16[2560,768]{1,0:T(8,128)(2,1)}, bf16[2560,768]{1,0:T(8,128)(2,1)}, f32[2560,1]{1,0:T(8,128)}, bf16[2560...) custom-call(bf16[1024,768]{1,0:T(8,128)(2,1)} %collective-permute-do, ...), custom_call_target="tpu_custom_call", output_to_operand_aliasing={{0}: (9, {}), {1}: (10, {}), {2}: (11, {}), {3}: (12, {}), ... | custom-call | flops 47185920 | bytes 56832 | tf_op jit(solution)/shard_map/expert_first/pallas_call | solution.py:517
  229.0 10.1 %convolution_convert_fusion.4 = bf16[768,1536]{1,0:T(8,128)(2,1)S(1)} fusion(bf16[2560,768]{1,0:T(8,128)(2,1)} %get-tuple-element.82.rows_ref, bf16[2560,1536]{1,0:T(8,128)(2,1)} %get-tuple-element.88), kind=kOutput, calls=%fused_computation.17 | convolution fusion | flops 6040977408 | bytes 14155776 | tf_op jit(solution)/shard_map/dot_general | solution.py:705
  242.9 22.0 %expert_second.2 = (bf16[2560,1536]{1,0:T(8,128)(2,1)}, bf16[2560,1536]{1,0:T(8,128)(2,1)}, bf16[1280,768]{1,0:T(8,128)(2,1)}, bf16[1280,768]{1,0:T(8,128)(2,1)}, f32[8,1024]{1,0:T(8,128)}) custom-call(bf16[2560,768]{1,0:T(8,128)(2,1)} %get-tuple-element.82.rows_ref, bf16[2560,768]{1,0:T(8,128)(2,1)} %get-tuple-element.83.graw_ref, ...), custom_call_target="tpu_custom_call" | custom-call | flops 47185920 | bytes 56832 | tf_op jit(solution)/shard_map/expert_second/pallas_call | solution.py:538
  271.5 4.0 collective-permute-start.25
  276.9 22.7 %expert_second.3 = (bf16[2560,1536]{1,0:T(8,128)(2,1)}, bf16[2560,1536]{1,0:T(8,128)(2,1)}, bf16[1280,768]{1,0:T(8,128)(2,1)}, bf16[1280,768]{1,0:T(8,128)(2,1)}, f32[8,1024]{1,0:T(8,128)}) custom-call(bf16[2560,768]{1,0:T(8,128)(2,1)} %get-tuple-element.82.rows_ref, ...), custom_call_target="tpu_custom_call", output_to_operand_aliasing={{0}: (10, {}), {1}: (11, {})} | custom-call | flops 47185920 | bytes 56832 | tf_op jit(solution)/shard_map/expert_second/pallas_call | solution.py:538
  299.6 12.1 %collective-permute-done.23 = bf16[640,768]{1,0:T(8,128)(2,1)} collective-permute-done((bf16[640,768]{1,0:T(8,128)(2,1)S(1)}, bf16[640,768]{1,0:T(8,128)(2,1)}, u32[]{:S(2)}, u32[]{:S(2)}) %collective-permute-start.23) | collective-permute-done | bytes 983072 | tf_op jit(solution)/shard_map/ppermute | solution.py:566
  311.7 9.0 %convolution_convert_fusion.3 = bf16[1536,768]{1,0:T(8,128)(2,1)S(1)} fusion(bf16[2560,1536]{1,0:T(8,128)(2,1)} %get-tuple-element.103, bf16[2560,768]{1,0:T(8,128)(2,1)S(1)} %copy-done.22), kind=kOutput, calls=%fused_computation.16 | convolution fusion | flops 6040977408 | bytes 14155776 | tf_op jit(solution)/shard_map/dot_general | solution.py:705
  320.8 6.9 %convolution_convert_fusion.2 = bf16[1536,768]{1,0:T(8,128)(2,1)S(1)} fusion(bf16[2560,1536]{1,0:T(8,128)(2,1)S(1)} %copy-done.23, bf16[2560,768]{1,0:T(8,128)(2,1)S(1)} %copy-done.22), kind=kOutput, calls=%fused_computation.15 | convolution fusion | flops 6040977408 | bytes 14155776 | tf_op jit(solution)/shard_map/dot_general | solution.py:705
  340.3 10.2 %convolution_convert_fusion.1 = bf16[768,1536]{1,0:T(8,128)(2,1)S(1)} fusion(bf16[2560,768]{1,0:T(8,128)(2,1)} %get-tuple-element.82.rows_ref, bf16[2560,1536]{1,0:T(8,128)(2,1)} %get-tuple-element.105), kind=kOutput, calls=%fused_computation.14 | convolution fusion | flops 6040977408 | bytes 14155776 | tf_op jit(solution)/shard_map/dot_general | solution.py:705
  354.3 3.3 fusion.20.extra_ref
  357.7 15.1 %token_back.1 = (f32[1024,768]{1,0:T(8,128)S(1)}, bf16[1024,768]{1,0:T(8,128)(2,1)S(1)}, bf16[768,768]{1,0:T(8,128)(2,1)S(1)}, f32[1,768]{1,0:T(1,128)S(1)}) custom-call(f32[1024,4]{1,0:T(8,128)S(1)} %bitcast.152, f32[1024,768]{1,0:T(8,128)} %fusion.20.extra_ref, f32[1024,768]{1,0:T(8,128)} %copy-done.2, bf16[1024,768]{1,0:T(8,128)(2,1)} %cot_ref.1, ...), custom_call_target="tpu_custom_call" | custom-call | flops 25165824 | bytes 70656 | tf_op jit(solution)/shard_map/token_back/pallas_call | solution.py:435
  375.5 31.8 %attend_backward.1 = (bf16[3,1024,768]{2,1,0:T(8,128)(2,1)}, f32[6,8,512]{2,1,0:T(8,128)S(1)}) custom-call(bf16[1024,2304]{1,0:T(8,128)(2,1)} %convolution_convert_fusion.q_ref.k_ref.v_ref, bf16[1024,2304]{1,0:T(8,128)(2,1)} %convolution_convert_fusion.q_ref.k_ref.v_ref, bf16[1024,2304]{1,0:T(8,128)(2,1)} %convolution_convert_fusion.q_ref.k_ref.v_ref, ...), custom_call_target="tpu_custom_call" | custom-call | flops 31457280 | bytes 49152 | tf_op jit(solution)/shard_map/attend_backward/pallas_call | solution.py:198
  407.9 14.3 %qkv_back.1 = (bf16[768,2304]{1,0:T(8,128)(2,1)}, bf16[1024,768]{1,0:T(8,128)(2,1)}, f32[1,768]{1,0:T(1,128)S(1)}) custom-call(bf16[1024,768]{1,0:T(8,128)(2,1)S(1)} %copy-done.10, bf16[3,1024,768]{2,1,0:T(8,128)(2,1)} %get-tuple-element.111.split_ref, bf16[768,3200]{1,0:T(8,128)(2,1)} %bitcast.13.weight_ref, bf16[1024,768]{1,0:T(8,128)(2,1)S(1)} %copy-done.6, ...), custom_call_target="tpu_custom_call" | custom-call | flops 28311552 | bytes 76800 | tf_op jit(solution)/shard_map/qkv_back/pallas_call | solution.py:478
  422.5 5.5 %fusion.1 = bf16[768,3200]{1,0:T(8,128)(2,1)} fusion(bf16[768,7]{1,0:T(8,128)(2,1)S(1)} %copy.128, bf16[768,768]{1,0:T(8,128)(2,1)} %copy-done.16, bf16[768,2304]{1,0:T(8,128)(2,1)} %get-tuple-element.113), kind=kLoop, calls=%fused_computation.3 | loop fusion | flops 19660800 | bytes 9644544 | tf_op jit(solution)/shard_map/concatenate | solution.py:772
  428.0 7.9 %reduce-scatter.2.cloned.1.call-done = bf16[384,768]{1,0:T(8,128)(2,1)} async-done(((bf16[3072,768]{1,0:T(8,128)(2,1)}), bf16[384,768]{1,0:T(8,128)(2,1)}) %reduce-scatter.2.cloned.1.call-update) | async-done | bytes 589840 | tf_op jit(solution)/shard_map/reduce_scatter | solution.py:722
  459.5 6.8 %mix_rows.1 = bf16[1024,768]{1,0:T(8,128)(2,1)} custom-call(f32[1024,4]{1,0:T(8,128)S(1)} %bitcast.153, f32[1024,768]{1,0:T(8,128)S(1)} %copy-done.3, bf16[640,768]{1,0:T(8,128)(2,1)S(1)} %get-tuple-element.202.one_ref, bf16[640,768]{1,0:T(8,128)(2,1)S(1)} %collective-permute-done.32.two_ref, bf16[640,768]{1,0:T(8,128)(2,1)S(1)} %get-tuple-element.200.three_ref, ...), custom_call_target="tpu_custom_call" | custom-call | flops 15728640 | bytes 33792 | tf_op jit(solution)/shard_map/mix_rows/pallas_call | solution.py:385
  475.0 9.9 %collective-permute-done.31 = bf16[4,48,3200]{2,1,0:T(8,128)(2,1)S(1)} collective-permute-done((bf16[4,48,3200]{2,1,0:T(8,128)(2,1)S(1)}, bf16[4,48,3200]{2,1,0:T(8,128)(2,1)S(1)}, u32[]{:S(2)}, u32[]{:S(2)}) %collective-permute-start.31) | collective-permute-done | bytes 1228832 | tf_op jit(solution)/shard_map/ppermute | solution.py:582
  485.2 5.1 collective-permute-done.35
  501.2 3.2 collective-permute-start.43
  504.4 14.3 %collective-permute-done.38 = bf16[48,3200]{1,0:T(8,128)(2,1)S(1)} collective-permute-done((bf16[48,3200]{1,0:T(8,128)(2,1)S(1)}, bf16[48,3200]{1,0:T(8,128)(2,1)S(1)}, u32[]{:S(2)}, u32[]{:S(2)}) %collective-permute-start.38) | collective-permute-done | bytes 307232 | tf_op jit(solution)/shard_map/ppermute | solution.py:576
  523.1 7.9 %collective-permute-done.40 = bf16[48,3200]{1,0:T(8,128)(2,1)S(1)} collective-permute-done((bf16[48,3200]{1,0:T(8,128)(2,1)S(1)}, bf16[48,3200]{1,0:T(8,128)(2,1)S(1)}, u32[]{:S(2)}, u32[]{:S(2)}) %collective-permute-start.40) | collective-permute-done | bytes 307232 | tf_op jit(solution)/shard_map/ppermute | solution.py:566
  (314 shorter events, 122.9 us)
Async XLA Ops:
  7.3 169.2 %all-gather.5.cloned.1.call-start = ((), (), s32[]{:S(2)}) async-start(), calls=%async_computation.1 | async-start | bytes 2654208 | tf_op jit(solution)/shard_map/all_gather | solution.py:652
  9.8 166.7 %all-gather.9.cloned.1.call-start = ((), (), s32[]{:S(2)}) async-start(), calls=%async_computation.4 | async-start | bytes 5308416 | tf_op jit(solution)/shard_map/all_gather | solution.py:653
  11.5 35.2 %collective-permute-start.3 = (bf16[48,3200]{1,0:T(8,128)(2,1)S(1)}, bf16[48,3200]{1,0:T(8,128)(2,1)S(1)}, u32[]{:S(2)}, u32[]{:S(2)}) collective-permute-start(bf16[48,3200]{1,0:T(8,128)(2,1)S(1)} %fusion.17.refs_0_), channel_id=1, source_target_pairs={{0,4},{1,5},{2,6},{3,7},{4,0},{5,1},{6,2},{7,3},{8,12},{9,13},{10,... | collective-permute-start | bytes 921608 | tf_op jit(solution)/shard_map/ppermute | solution.py:576
  12.6 36.9 %collective-permute-start.5 = (bf16[48,3200]{1,0:T(8,128)(2,1)S(1)}, bf16[48,3200]{1,0:T(8,128)(2,1)S(1)}, u32[]{:S(2)}, u32[]{:S(2)}) collective-permute-start(bf16[48,3200]{1,0:T(8,128)(2,1)S(1)} %fusion.17.refs_0_), channel_id=1, source_target_pairs={{0,6},{1,7},{2,0},{3,1},{4,2},{5,3},{6,4},{7,5},{8,14},{9,15},{10,... | collective-permute-start | bytes 921608 | tf_op jit(solution)/shard_map/ppermute | solution.py:576
  14.0 36.8 %collective-permute-start = (bf16[48,3200]{1,0:T(8,128)(2,1)S(1)}, bf16[48,3200]{1,0:T(8,128)(2,1)S(1)}, u32[]{:S(2)}, u32[]{:S(2)}) collective-permute-start(bf16[48,3200]{1,0:T(8,128)(2,1)S(1)} %fusion.17.refs_0_), channel_id=1, source_target_pairs={{0,1},{1,0},{2,3},{3,2},{4,5},{5,4},{6,7},{7,6},{8,9},{9,8},{10,11... | collective-permute-start | bytes 921608 | tf_op jit(solution)/shard_map/ppermute | solution.py:582
  18.3 32.5 %collective-permute-start.2 = (bf16[48,3200]{1,0:T(8,128)(2,1)S(1)}, bf16[48,3200]{1,0:T(8,128)(2,1)S(1)}, u32[]{:S(2)}, u32[]{:S(2)}) collective-permute-start(bf16[48,3200]{1,0:T(8,128)(2,1)S(1)} %collective-permute-done.1.refs_2_), channel_id=1, source_target_pairs={{0,1},{1,0},{2,3},{3,2},{4,5},{5,4},{6,7},{7,6},{8,9},{9,8},{10,11... | collective-permute-start | bytes 921608 | tf_op jit(solution)/shard_map/ppermute | solution.py:582
  76.3 166.6 %all-gather.7.cloned.1.call-start = ((), (), s32[]{:S(2)}) async-start(), calls=%async_computation.2 | async-start | bytes 2654208 | tf_op jit(solution)/shard_map/all_gather | solution.py:654
  76.3 56.2 %collective-permute-start.10 = (bf16[1024,768]{1,0:T(8,128)(2,1)}, bf16[1024,768]{1,0:T(8,128)(2,1)}, u32[]{:S(2)}, u32[]{:S(2)}) collective-permute-start(bf16[1024,768]{1,0:T(8,128)(2,1)} %cot_ref.1), channel_id=1, source_target_pairs={{0,16},{8,24},{16,0},{24,8},{1,17},{9,25},{17,1},{25,9},{2,18},{10... | collective-permute-start | bytes 4718600 | tf_op jit(solution)/shard_map/ppermute | solution.py:566
  130.1 35.9 %collective-permute-start.8 = (bf16[1024,768]{1,0:T(8,128)(2,1)}, bf16[1024,768]{1,0:T(8,128)(2,1)}, u32[]{:S(2)}, u32[]{:S(2)}) collective-permute-start(bf16[1024,768]{1,0:T(8,128)(2,1)} %multiply_convert_fusion.act_one_ref), channel_id=1, source_target_pairs={{0,16},{8,24},{16,0},{24,8},{1,17},{9,25},{17,1},{25,9},{2,18},{10... | collective-permute-start | bytes 4718600 | tf_op jit(solution)/shard_map/ppermute | solution.py:566
  131.3 45.1 %collective-permute-start.15 = (bf16[1024,768]{1,0:T(8,128)(2,1)}, bf16[1024,768]{1,0:T(8,128)(2,1)}, u32[]{:S(2)}, u32[]{:S(2)}) collective-permute-start(bf16[1024,768]{1,0:T(8,128)(2,1)} %cot_ref.1), channel_id=1, source_target_pairs={{0,8},{8,0},{16,24},{24,16},{1,9},{9,1},{17,25},{25,17},{2,10},{10... | collective-permute-start | bytes 4718600 | tf_op jit(solution)/shard_map/ppermute | solution.py:566
  132.0 303.9 %reduce-scatter.2.cloned.1.call-start = ((), (), s32[]{:S(2)}) async-start(), calls=%async_computation.3 | async-start | bytes 5308416 | tf_op jit(solution)/shard_map/reduce_scatter | solution.py:722
  132.5 69.9 %collective-permute-start.11 = (bf16[1024,768]{1,0:T(8,128)(2,1)}, bf16[1024,768]{1,0:T(8,128)(2,1)S(1)}, u32[]{:S(2)}, u32[]{:S(2)}) collective-permute-start(bf16[1024,768]{1,0:T(8,128)(2,1)} %collective-permute-done.10.cot_one_ref), channel_id=1, source_target_pairs={{0,8},{8,0},{16,24},{24,16},{1,9},{9,1},{17,25},{25,17},{2,10},{10... | collective-permute-start | bytes 4718600 | tf_op jit(solution)/shard_map/ppermute | solution.py:566
  132.6 43.8 %collective-permute-start.14 = (bf16[1024,768]{1,0:T(8,128)(2,1)}, bf16[1024,768]{1,0:T(8,128)(2,1)S(1)}, u32[]{:S(2)}, u32[]{:S(2)}) collective-permute-start(bf16[1024,768]{1,0:T(8,128)(2,1)} %multiply_convert_fusion.act_one_ref), channel_id=1, source_target_pairs={{0,8},{8,0},{16,24},{24,16},{1,9},{9,1},{17,25},{25,17},{2,10},{10... | collective-permute-start | bytes 4718600 | tf_op jit(solution)/shard_map/ppermute | solution.py:566
  166.0 36.4 %collective-permute-start.9 = (bf16[1024,768]{1,0:T(8,128)(2,1)}, bf16[1024,768]{1,0:T(8,128)(2,1)}, u32[]{:S(2)}, u32[]{:S(2)}) collective-permute-start(bf16[1024,768]{1,0:T(8,128)(2,1)} %collective-permute-done.8.act_one_ref), channel_id=1, source_target_pairs={{0,8},{8,0},{16,24},{24,16},{1,9},{9,1},{17,25},{25,17},{2,10},{10... | collective-permute-start | bytes 4718600 | tf_op jit(solution)/shard_map/ppermute | solution.py:566
  240.6 28.4 %collective-permute-start.17 = (bf16[4,96,1536]{2,1,0:T(8,128)(2,1)S(1)}, bf16[4,96,1536]{2,1,0:T(8,128)(2,1)}, u32[]{:S(2)}, u32[]{:S(2)}) collective-permute-start(bf16[4,96,1536]{2,1,0:T(8,128)(2,1)S(1)} %dynamic-slice_bitcast_fusion.4), channel_id=1, source_target_pairs={{0,1},{1,0},{2,3},{3,2},{4,5},{5,4},{6,7},{7,6},{8,9},{9,8},{10,11... | collective-permute-start | bytes 3538952 | tf_op jit(solution)/shard_map/ppermute | solution.py:582
  267.6 32.0 %collective-permute-start.22 = (bf16[640,768]{1,0:T(8,128)(2,1)}, bf16[640,768]{1,0:T(8,128)(2,1)S(1)}, u32[]{:S(2)}, u32[]{:S(2)}) collective-permute-start(bf16[640,768]{1,0:T(8,128)(2,1)} %get-tuple-element.204), channel_id=1, source_target_pairs={{0,16},{8,24},{16,0},{24,8},{1,17},{9,25},{17,1},{25,9},{2,18},{10... | collective-permute-start | bytes 2949128 | tf_op jit(solution)/shard_map/ppermute | solution.py:566
  268.9 42.8 %collective-permute-start.23 = (bf16[640,768]{1,0:T(8,128)(2,1)S(1)}, bf16[640,768]{1,0:T(8,128)(2,1)}, u32[]{:S(2)}, u32[]{:S(2)}) collective-permute-start(bf16[640,768]{1,0:T(8,128)(2,1)S(1)} %get-tuple-element.203), channel_id=1, source_target_pairs={{0,16},{8,24},{16,0},{24,8},{1,17},{9,25},{17,1},{25,9},{2,18},{10... | collective-permute-start | bytes 2949128 | tf_op jit(solution)/shard_map/ppermute | solution.py:566
  271.5 40.2 %collective-permute-start.24 = (bf16[96,1536]{1,0:T(8,128)(2,1)S(1)}, bf16[96,1536]{1,0:T(8,128)(2,1)S(1)}, u32[]{:S(2)}, u32[]{:S(2)}) collective-permute-start(bf16[96,1536]{1,0:T(8,128)(2,1)S(1)} %get-tuple-element.218), channel_id=1, source_target_pairs={{0,2},{1,3},{2,4},{3,5},{4,6},{5,7},{6,0},{7,1},{8,10},{9,11},{10,... | collective-permute-start | bytes 884744 | tf_op jit(solution)/shard_map/ppermute | solution.py:576
  271.5 40.2 %collective-permute-start.25 = (bf16[96,1536]{1,0:T(8,128)(2,1)S(1)}, bf16[96,1536]{1,0:T(8,128)(2,1)S(1)}, u32[]{:S(2)}, u32[]{:S(2)}) collective-permute-start(bf16[96,1536]{1,0:T(8,128)(2,1)S(1)} %get-tuple-element.217), channel_id=1, source_target_pairs={{0,4},{1,5},{2,6},{3,7},{4,0},{5,1},{6,2},{7,3},{8,12},{9,13},{10,... | collective-permute-start | bytes 884744 | tf_op jit(solution)/shard_map/ppermute | solution.py:576
  275.4 36.3 %collective-permute-start.26 = (bf16[96,1536]{1,0:T(8,128)(2,1)S(1)}, bf16[96,1536]{1,0:T(8,128)(2,1)S(1)}, u32[]{:S(2)}, u32[]{:S(2)}) collective-permute-start(bf16[96,1536]{1,0:T(8,128)(2,1)S(1)} %get-tuple-element.216), channel_id=1, source_target_pairs={{0,6},{1,7},{2,0},{3,1},{4,2},{5,3},{6,4},{7,5},{8,14},{9,15},{10,... | collective-permute-start | bytes 884744 | tf_op jit(solution)/shard_map/ppermute | solution.py:576
  338.9 69.0 %collective-permute-start.28 = (bf16[1280,768]{1,0:T(8,128)(2,1)}, bf16[1280,768]{1,0:T(8,128)(2,1)}, u32[]{:S(2)}, u32[]{:S(2)}) collective-permute-start(bf16[1280,768]{1,0:T(8,128)(2,1)} %get-tuple-element.110), channel_id=1, source_target_pairs={{0,16},{8,24},{16,0},{24,8},{1,17},{9,25},{17,1},{25,9},{2,18},{10... | collective-permute-start | bytes 5898248 | tf_op jit(solution)/shard_map/ppermute | solution.py:566
  352.2 55.7 %collective-permute-start.29 = (bf16[4,96,1536]{2,1,0:T(8,128)(2,1)}, bf16[4,96,1536]{2,1,0:T(8,128)(2,1)}, u32[]{:S(2)}, u32[]{:S(2)}) collective-permute-start(bf16[4,96,1536]{2,1,0:T(8,128)(2,1)} %get-tuple-element.197), channel_id=1, source_target_pairs={{0,1},{1,0},{2,3},{3,2},{4,5},{5,4},{6,7},{7,6},{8,9},{9,8},{10,11... | collective-permute-start | bytes 3538952 | tf_op jit(solution)/shard_map/ppermute | solution.py:582
  457.0 28.0 %collective-permute-start.31 = (bf16[4,48,3200]{2,1,0:T(8,128)(2,1)S(1)}, bf16[4,48,3200]{2,1,0:T(8,128)(2,1)S(1)}, u32[]{:S(2)}, u32[]{:S(2)}) collective-permute-start(bf16[4,48,3200]{2,1,0:T(8,128)(2,1)S(1)} %dynamic-slice_bitcast_fusion.1), channel_id=1, source_target_pairs={{0,1},{1,0},{2,3},{3,2},{4,5},{5,4},{6,7},{7,6},{8,9},{9,8},{10,11... | collective-permute-start | bytes 3686408 | tf_op jit(solution)/shard_map/ppermute | solution.py:582
  458.3 38.8 %collective-permute-start.44 = (bf16[96,1536]{1,0:T(8,128)(2,1)S(1)}, bf16[96,1536]{1,0:T(8,128)(2,1)S(1)}, u32[]{:S(2)}, u32[]{:S(2)}) collective-permute-start(bf16[96,1536]{1,0:T(8,128)(2,1)S(1)} %add_convert_fusion.2), channel_id=1, source_target_pairs={{0,16},{8,24},{16,0},{24,8},{1,17},{9,25},{17,1},{25,9},{2,18},{10... | collective-permute-start | bytes 884744 | tf_op jit(solution)/shard_map/ppermute | solution.py:566
  458.6 26.6 %collective-permute-start.34 = (bf16[96,1536]{1,0:T(8,128)(2,1)S(1)}, bf16[96,1536]{1,0:T(8,128)(2,1)S(1)}, u32[]{:S(2)}, u32[]{:S(2)}) collective-permute-start(bf16[96,1536]{1,0:T(8,128)(2,1)S(1)} %get-tuple-element.214), channel_id=1, source_target_pairs={{0,2},{1,3},{2,4},{3,5},{4,6},{5,7},{6,0},{7,1},{8,10},{9,11},{10,... | collective-permute-start | bytes 884744 | tf_op jit(solution)/shard_map/ppermute | solution.py:576
  470.4 20.0 %collective-permute-start.35 = (bf16[96,1536]{1,0:T(8,128)(2,1)S(1)}, bf16[96,1536]{1,0:T(8,128)(2,1)S(1)}, u32[]{:S(2)}, u32[]{:S(2)}) collective-permute-start(bf16[96,1536]{1,0:T(8,128)(2,1)S(1)} %get-tuple-element.213), channel_id=1, source_target_pairs={{0,4},{1,5},{2,6},{3,7},{4,0},{5,1},{6,2},{7,3},{8,12},{9,13},{10,... | collective-permute-start | bytes 884744 | tf_op jit(solution)/shard_map/ppermute | solution.py:576
  471.6 20.0 %collective-permute-start.36 = (bf16[96,1536]{1,0:T(8,128)(2,1)S(1)}, bf16[96,1536]{1,0:T(8,128)(2,1)S(1)}, u32[]{:S(2)}, u32[]{:S(2)}) collective-permute-start(bf16[96,1536]{1,0:T(8,128)(2,1)S(1)} %get-tuple-element.212), channel_id=1, source_target_pairs={{0,6},{1,7},{2,0},{3,1},{4,2},{5,3},{6,4},{7,5},{8,14},{9,15},{10,... | collective-permute-start | bytes 884744 | tf_op jit(solution)/shard_map/ppermute | solution.py:576
  493.2 25.6 %collective-permute-start.38 = (bf16[48,3200]{1,0:T(8,128)(2,1)S(1)}, bf16[48,3200]{1,0:T(8,128)(2,1)S(1)}, u32[]{:S(2)}, u32[]{:S(2)}) collective-permute-start(bf16[48,3200]{1,0:T(8,128)(2,1)S(1)} %get-tuple-element.211), channel_id=1, source_target_pairs={{0,4},{1,5},{2,6},{3,7},{4,0},{5,1},{6,2},{7,3},{8,12},{9,13},{10,... | collective-permute-start | bytes 921608 | tf_op jit(solution)/shard_map/ppermute | solution.py:576
  495.0 27.4 %collective-permute-start.39 = (bf16[48,3200]{1,0:T(8,128)(2,1)S(1)}, bf16[48,3200]{1,0:T(8,128)(2,1)S(1)}, u32[]{:S(2)}, u32[]{:S(2)}) collective-permute-start(bf16[48,3200]{1,0:T(8,128)(2,1)S(1)} %get-tuple-element.210), channel_id=1, source_target_pairs={{0,6},{1,7},{2,0},{3,1},{4,2},{5,3},{6,4},{7,5},{8,14},{9,15},{10,... | collective-permute-start | bytes 921608 | tf_op jit(solution)/shard_map/ppermute | solution.py:576
  497.1 25.9 %collective-permute-start.42 = (bf16[96,1536]{1,0:T(8,128)(2,1)S(1)}, bf16[96,1536]{1,0:T(8,128)(2,1)S(1)}, u32[]{:S(2)}, u32[]{:S(2)}) collective-permute-start(bf16[96,1536]{1,0:T(8,128)(2,1)S(1)} %add_convert_fusion.2), channel_id=1, source_target_pairs={{0,8},{8,0},{16,24},{24,16},{1,9},{9,1},{17,25},{25,17},{2,10},{10... | collective-permute-start | bytes 884744 | tf_op jit(solution)/shard_map/ppermute | solution.py:566
  499.6 33.1 %collective-permute-start.46 = (bf16[96,1536]{1,0:T(8,128)(2,1)S(1)}, bf16[96,1536]{1,0:T(8,128)(2,1)S(1)}, u32[]{:S(2)}, u32[]{:S(2)}) collective-permute-start(bf16[96,1536]{1,0:T(8,128)(2,1)S(1)} %collective-permute-done.44), channel_id=1, source_target_pairs={{0,8},{8,0},{16,24},{24,16},{1,9},{9,1},{17,25},{25,17},{2,10},{10... | collective-permute-start | bytes 884744 | tf_op jit(solution)/shard_map/ppermute | solution.py:566
  501.2 21.8 %collective-permute-start.43 = (bf16[96,1536]{1,0:T(8,128)(2,1)S(1)}, bf16[96,1536]{1,0:T(8,128)(2,1)S(1)}, u32[]{:S(2)}, u32[]{:S(2)}) collective-permute-start(bf16[96,1536]{1,0:T(8,128)(2,1)S(1)} %add_convert_fusion.1), channel_id=1, source_target_pairs={{0,8},{8,0},{16,24},{24,16},{1,9},{9,1},{17,25},{25,17},{2,10},{10... | collective-permute-start | bytes 884744 | tf_op jit(solution)/shard_map/ppermute | solution.py:566
  (75 other events, 732.4 us)
Sparse Core Ops, SparseCore 0:
  10.8 74.3 all-gather.4
  88.0 78.2 all-gather.8
  169.0 51.0 all-gather.6
  330.4 105.5 reduce-scatter.1
